TPU v7x, 32 devices: a whole 2x2x4 slice. The times are simulated.
32 devices in a mesh: dp: 8 (over y, x, core), tensor: 4 (over z).
Axes of the slice: x: 2, y: 2, z: 4, core: 2. Of those that a mesh axis runs over, the one named last changes fastest.
Arguments:
- block_input: bfloat16 [48, 200, 512], P('dp', 'tensor'), may hold values from -6 to 6
- gains: bfloat16 [512, 2], P('dp'), may hold values from 0.5 to 1.5
- w_qkv: bfloat16 [512, 3, 512], P('dp', None, 'tensor'), may hold values from -0.25 to 0.25
- w_o: bfloat16 [512, 512], P('tensor', 'dp'), may hold values from -1.5 to 1.5
- w_router: bfloat16 [512, 16], P('dp'), may hold values from -0.1875 to 0.1875
- w_in: bfloat16 [512, 16, 2048], P('dp', None, 'tensor'), may hold values from -0.25 to 0.25
- w_out: bfloat16 [2048, 16, 512], P('tensor', None, 'dp'), may hold values from -1 to 1
- pictures_alive_per_shard: int32 [8], P('dp'), may hold values from 5 to 6, as said below
- expert_ids: int32 [48, 200, 2], P('dp'), may hold values from 0 to 15, as said below
- slot_index: int32 [48, 200, 2], P('dp'), may hold values from -1 to 191, as said below
- cotangent: bfloat16 [48, 200, 512], P('dp', 'tensor'), may hold values from -6 to 6
Outputs:
- output: bfloat16 [48, 200, 512], P('dp', 'tensor')
- grad_x: float32 [48, 200, 512], P('dp', 'tensor')
- grad_gains: float32 [512, 2], P('dp')
- grad_qkv: float32 [512, 3, 512], P('dp', None, 'tensor')
- grad_o: float32 [512, 512], P('tensor', 'dp')
- grad_router: float32 [512, 16], P('dp')
- grad_in: float32 [512, 16, 2048], P('dp', None, 'tensor')
- grad_out: float32 [2048, 16, 512], P('tensor', None, 'dp')
Inputs may be any that keep to these rules, and one draw needn't show every extreme that they name: `pictures_alive_per_shard`: each index of dp has 5 or 6 live images; both counts occur in every draw. `expert_ids`: the two experts of a token differ. `slot_index`: within one group, slots are given to live tokens' choices in order, all first choices of the group in token order and then all second choices; a choice gets -1 when its token isn't live or its expert already has 192 entries. Distinct choices of a group never share an (expert, slot) pair.
All inputs are finite; a program needn't handle non-finite values.
Results may differ from a plain program's by a relative error of at most 0.014.
Values may be sent and summed in bfloat16 or wider, within the bound.
A program may use at most 192 MiB of HBM per device.

v0:
```python
import math

import jax
import jax.numpy as jnp
from jax import lax
from jax.sharding import PartitionSpec as P

HEAD_DIM = 64
TOK_IMG = 197
CAP = 192


epsilon = 1e-06
negative_fill = -1e30


def as_sent(shard):
    return jax.tree.map(lambda a: a.astype(jnp.bfloat16) if a.dtype == jnp.float32 else a, shard)


def layer_norm(values, gain):
    centre = values - jnp.mean(values, -1, keepdims=True)
    spread = jnp.mean(centre * centre, -1, keepdims=True)
    return centre * lax.rsqrt(spread + epsilon) * gain


def gelu_exact(values):
    return jax.nn.gelu(values, approximate=False)


def gate_values(logits, chosen):
    router_probs = jax.nn.softmax(logits, axis=-1)
    return jnp.einsum("re,rke->rk", router_probs, chosen)


def rows_in(values):
    return lax.all_gather(values, "tensor", axis=1, tiled=True)


def rows_out(values):
    return lax.psum_scatter(values, "tensor", scatter_dimension=1, tiled=True)


def grads_in(values):
    return jax.tree.map(
        lambda part, own: part.astype(own.dtype),
        lax.all_gather(as_sent(values), "tensor", axis=1, tiled=True),
        values,
    )


def grads_out(values):
    return lax.psum_scatter(values, "tensor", scatter_dimension=1, tiled=True)


def attention_scores(queries, keys_all, key_live, scale_factor):
    gating_logits_matrix = (
        jnp.einsum("ilhe,imhe->ihlm", queries, keys_all, preferred_element_type=jnp.float32)
        * scale_factor
    )
    return jnp.where(key_live[None, None, None, :], gating_logits_matrix, negative_fill)


def body(
    block_input,
    gains,
    w_qkv,
    w_o,
    w_router,
    w_in,
    w_out,
    pictures_alive_per_shard,
    expert_ids,
    slot_index,
    cotangent,
):
    tensor_size = lax.axis_size("tensor")
    tensor_pos = lax.axis_index("tensor")
    images, quarter, model_width = block_input.shape
    length = quarter * tensor_size
    all_rows = images * length
    own_rows = images * quarter
    start_row = tensor_pos * quarter
    experts = w_in.shape[1]
    slot_count = experts * CAP
    key_live = jnp.arange(length) < TOK_IMG
    live_all = (
        (jnp.arange(images) < pictures_alive_per_shard[0])[:, None] & key_live[None, :]
    ).astype(jnp.float32)
    live_own = lax.dynamic_slice_in_dim(live_all, start_row, quarter, 1)
    gathered = (
        lax.all_gather(gains, "dp", axis=0, tiled=True),
        lax.all_gather(w_qkv, "dp", axis=0, tiled=True),
        lax.all_gather(w_o, "dp", axis=1, tiled=True),
        lax.all_gather(w_router, "dp", axis=0, tiled=True),
        lax.all_gather(w_in, "dp", axis=0, tiled=True),
        lax.all_gather(w_out, "dp", axis=2, tiled=True),
    )
    gain_all, qkv_all, outproj_all, router_all, expin_all, expout_all = gathered
    head_cols = qkv_all.shape[2]
    local_heads = head_cols // HEAD_DIM
    scale_factor = 1.0 / math.sqrt(HEAD_DIM)
    gain_one = gain_all[:, 0].astype(jnp.float32)
    gain_two = gain_all[:, 1].astype(jnp.float32)
    x_float = block_input.astype(jnp.float32)
    normed = layer_norm(x_float, gain_one).astype(jnp.bfloat16)
    normed_all = rows_in(normed).reshape(all_rows, model_width)
    project = jnp.einsum(
        "rd,djc->rjc", normed_all, qkv_all, preferred_element_type=jnp.float32
    ).astype(jnp.bfloat16)
    queries = project[:, 0].reshape(images, length, local_heads, HEAD_DIM)
    keys_all = project[:, 1].reshape(images, length, local_heads, HEAD_DIM)
    values_all = project[:, 2].reshape(images, length, local_heads, HEAD_DIM)
    masked = attention_scores(queries, keys_all, key_live, scale_factor)
    top_score = jnp.max(masked, -1, keepdims=True)
    expd = jnp.exp(masked - top_score)
    total = jnp.sum(expd, -1, keepdims=True)
    att_probs = expd / total
    log_total = top_score + jnp.log(total)
    attended = jnp.einsum(
        "ihlm,imhe->ilhe",
        att_probs.astype(jnp.bfloat16),
        values_all,
        preferred_element_type=jnp.float32,
    )
    attended = attended.astype(jnp.bfloat16).reshape(all_rows, head_cols)
    branch_part = jnp.dot(attended, outproj_all, preferred_element_type=jnp.float32).reshape(
        images, length, model_width
    )
    middle = x_float + live_own[:, :, None] * rows_out(branch_part)
    normed_two = layer_norm(middle, gain_two).astype(jnp.bfloat16)
    normed_two_all = rows_in(normed_two).reshape(all_rows, model_width)
    own_flat = normed_two.reshape(own_rows, model_width)
    expert_range = jnp.arange(experts)
    own_ids = lax.dynamic_slice_in_dim(expert_ids, start_row, quarter, 1).reshape(own_rows, 2)
    chosen = (own_ids[:, :, None] == expert_range[None, None, :]).astype(jnp.float32)
    targets = jnp.where(slot_index >= 0, expert_ids * CAP + slot_index, -1).reshape(all_rows, 2)
    slot_ids = jnp.arange(slot_count)
    first_hot = (targets[:, 0:1] == slot_ids[None, :]).astype(jnp.bfloat16)
    second_hot = (targets[:, 1:2] == slot_ids[None, :]).astype(jnp.bfloat16)
    dispatched = jnp.einsum(
        "rs,rd->sd", first_hot, normed_two_all, preferred_element_type=jnp.float32
    )
    dispatched = dispatched + jnp.einsum(
        "rs,rd->sd", second_hot, normed_two_all, preferred_element_type=jnp.float32
    )
    dispatched = dispatched.astype(jnp.bfloat16).reshape(experts, CAP, model_width)
    hidden = jnp.einsum("ecd,def->ecf", dispatched, expin_all, preferred_element_type=jnp.float32)
    active = gelu_exact(hidden).astype(jnp.bfloat16)
    expert_part = jnp.einsum("ecf,fed->ecd", active, expout_all, preferred_element_type=jnp.float32)
    expert_part = expert_part.astype(jnp.bfloat16).reshape(slot_count, model_width)
    first_rows = jnp.dot(first_hot, expert_part, preferred_element_type=jnp.float32)
    second_rows = jnp.dot(second_hot, expert_part, preferred_element_type=jnp.float32)
    logits = jnp.dot(own_flat, router_all, preferred_element_type=jnp.float32)
    gates = gate_values(logits, chosen)
    first_own, second_own = rows_out(
        (
            first_rows.reshape(images, length, model_width),
            second_rows.reshape(images, length, model_width),
        )
    )
    gate_grid = gates.reshape(images, quarter, 2)
    output = middle + gate_grid[:, :, 0:1] * first_own + gate_grid[:, :, 1:2] * second_own
    regathered = (
        lax.all_gather(gains, "dp", axis=0, tiled=True),
        lax.all_gather(w_qkv, "dp", axis=0, tiled=True),
        lax.all_gather(w_o, "dp", axis=1, tiled=True),
        lax.all_gather(w_router, "dp", axis=0, tiled=True),
        lax.all_gather(w_in, "dp", axis=0, tiled=True),
        lax.all_gather(w_out, "dp", axis=2, tiled=True),
    )
    qkv_all = regathered[1]
    outproj_all = regathered[2]
    router_all = regathered[3]
    expin_all = regathered[4]
    expout_all = regathered[5]
    grad_output = cotangent.astype(jnp.float32)
    grad_first = (gate_grid[:, :, 0:1] * grad_output).astype(jnp.bfloat16)
    grad_second = (gate_grid[:, :, 1:2] * grad_output).astype(jnp.bfloat16)
    grad_gates = jnp.stack(
        [jnp.sum(grad_output * first_own, -1), jnp.sum(grad_output * second_own, -1)], -1
    ).reshape(own_rows, 2)
    leading_cotangent, second_back = grads_in((grad_first, grad_second))
    leading_cotangent = leading_cotangent.reshape(all_rows, model_width)
    second_back = second_back.reshape(all_rows, model_width)
    unused_gates, gate_pull = jax.vjp(lambda values: gate_values(values, chosen), logits)
    grad_logits = gate_pull(grad_gates)[0].astype(jnp.bfloat16)
    grad_router = jnp.einsum("rd,re->de", own_flat, grad_logits, preferred_element_type=jnp.float32)
    router_back = jnp.einsum(
        "re,de->rd", grad_logits, router_all, preferred_element_type=jnp.float32
    )
    grad_expert = jnp.einsum(
        "rs,rd->sd", first_hot, leading_cotangent, preferred_element_type=jnp.float32
    )
    grad_expert = grad_expert + jnp.einsum(
        "rs,rd->sd", second_hot, second_back, preferred_element_type=jnp.float32
    )
    grad_expert = grad_expert.astype(jnp.bfloat16).reshape(experts, CAP, model_width)
    grad_active = jnp.einsum(
        "ecd,fed->ecf", grad_expert, expout_all, preferred_element_type=jnp.float32
    )
    grad_expout = jnp.einsum(
        "ecf,ecd->fed", active, grad_expert, preferred_element_type=jnp.float32
    )
    unused_gelu, gelu_pull = jax.vjp(gelu_exact, hidden)
    grad_hidden = gelu_pull(grad_active)[0].astype(jnp.bfloat16)
    grad_expin = jnp.einsum(
        "ecd,ecf->def", dispatched, grad_hidden, preferred_element_type=jnp.float32
    )
    grad_dispatch = jnp.einsum(
        "ecf,def->ecd", grad_hidden, expin_all, preferred_element_type=jnp.float32
    )
    grad_dispatch = grad_dispatch.astype(jnp.bfloat16).reshape(slot_count, model_width)
    back_rows = jnp.dot(first_hot, grad_dispatch, preferred_element_type=jnp.float32)
    back_rows = back_rows + jnp.dot(second_hot, grad_dispatch, preferred_element_type=jnp.float32)
    grad_normed_two = grads_out(
        back_rows.reshape(images, length, model_width)
    ) + router_back.reshape(images, quarter, model_width)
    unused_two, norm_two_pull = jax.vjp(layer_norm, middle, gain_two)
    grad_middle_norm, grad_gain_two = norm_two_pull(grad_normed_two)
    grad_middle = grad_output + grad_middle_norm
    grad_branch = (live_own[:, :, None] * grad_middle).astype(jnp.bfloat16)
    grad_branch_all = grads_in(grad_branch).reshape(all_rows, model_width)
    grad_outproj = jnp.einsum(
        "rc,rd->cd", attended, grad_branch_all, preferred_element_type=jnp.float32
    )
    grad_attended = jnp.einsum(
        "rd,cd->rc", grad_branch_all, outproj_all, preferred_element_type=jnp.float32
    )
    grad_attended = grad_attended.astype(jnp.bfloat16).reshape(
        images, length, local_heads, HEAD_DIM
    )
    masked_again = attention_scores(queries, keys_all, key_live, scale_factor)
    probs_again = jnp.exp(masked_again - log_total)
    grad_values = jnp.einsum(
        "ihlm,ilhe->imhe",
        probs_again.astype(jnp.bfloat16),
        grad_attended,
        preferred_element_type=jnp.float32,
    )
    grad_values = grad_values.astype(jnp.bfloat16)
    grad_probs = jnp.einsum(
        "ilhe,imhe->ihlm", grad_attended, values_all, preferred_element_type=jnp.float32
    )
    grad_scores = probs_again * (grad_probs - jnp.sum(probs_again * grad_probs, -1, keepdims=True))
    grad_scores = grad_scores.astype(jnp.bfloat16)
    grad_queries = (
        jnp.einsum("ihlm,imhe->ilhe", grad_scores, keys_all, preferred_element_type=jnp.float32)
        * scale_factor
    ).astype(jnp.bfloat16)
    grad_keys = (
        jnp.einsum("ihlm,ilhe->imhe", grad_scores, queries, preferred_element_type=jnp.float32)
        * scale_factor
    ).astype(jnp.bfloat16)
    grad_project = jnp.stack([grad_queries, grad_keys, grad_values], 2).reshape(
        all_rows, 3, head_cols
    )
    grad_qkv = jnp.einsum(
        "rd,rjc->djc", normed_all, grad_project, preferred_element_type=jnp.float32
    )
    normed_back = jnp.einsum(
        "rjc,djc->rd", grad_project, qkv_all, preferred_element_type=jnp.float32
    )
    grad_normed = grads_out(normed_back.reshape(images, length, model_width))
    unused_one, norm_one_pull = jax.vjp(layer_norm, x_float, gain_one)
    grad_x_norm, grad_gain_one = norm_one_pull(grad_normed)
    grad_input = grad_middle + grad_x_norm
    router_sum, gain_sum = lax.psum(
        (grad_router, jnp.stack([grad_gain_one, grad_gain_two], 1)), "tensor"
    )
    expert_fractions = (
        lax.psum_scatter(gain_sum, "dp", scatter_dimension=0, tiled=True),
        lax.psum_scatter(grad_qkv, "dp", scatter_dimension=0, tiled=True),
        lax.psum_scatter(grad_outproj, "dp", scatter_dimension=1, tiled=True),
        lax.psum_scatter(router_sum, "dp", scatter_dimension=0, tiled=True),
        lax.psum_scatter(grad_expin, "dp", scatter_dimension=0, tiled=True),
        lax.psum_scatter(grad_expout, "dp", scatter_dimension=2, tiled=True),
    )
    return (
        output.astype(jnp.bfloat16),
        grad_input,
        expert_fractions[0],
        expert_fractions[1],
        expert_fractions[2],
        expert_fractions[3],
        expert_fractions[4],
        expert_fractions[5],
    )


def solution(mesh):
    placed = (
        P("dp", "tensor", None),
        P("dp", None),
        P("dp", None, "tensor"),
        P("tensor", "dp"),
        P("dp", None),
        P("dp", None, "tensor"),
        P("tensor", None, "dp"),
        P("dp"),
        P("dp", None, None),
        P("dp", None, None),
        P("dp", "tensor", None),
    )
    return jax.shard_map(
        body,
        mesh=mesh,
        in_specs=placed,
        out_specs=(
            P("dp", "tensor", None),
            P("dp", "tensor", None),
            P("dp", None),
            P("dp", None, "tensor"),
            P("tensor", "dp"),
            P("dp", None),
            P("dp", None, "tensor"),
            P("tensor", None, "dp"),
        ),
        check_vma=False,
    )
```

profile of v0, /device:TPU:0, one launch (start us, length us, event | category | flops | bytes accessed | tf_op | source)
XLA Modules:
  0.0 1283.6 jit_solution(13077234141175463603)
XLA Ops:
  7.2 10.3 all-gather
  22.2 9.1 all_gather.41
  40.1 20.5 %all-gather.10.cloned.1.call-done = bf16[6,200,512]{2,0,1:T(8,128)(2,1)} async-done(((bf16[6,50,512]{2,0,1:T(8,128)(2,1)}), bf16[6,200,512]{2,0,1:T(8,128)(2,1)}) %all-gather.10.cloned.1.call-update) | async-done | bytes 1228816 | tf_op jit(solution)/shard_map/all_gather | solution.py:37
  72.1 95.6 %all-reduce.11.cloned.1.call-done = f32[6,200,512]{2,1,0:T(8,128)} async-done(((f32[6,200,512]{2,1,0:T(8,128)}), f32[6,200,512]{2,1,0:T(8,128)}) %all-reduce.11.cloned.1.call-update) | async-done | bytes 2457616
  190.4 18.4 %all-gather.12.cloned.1.call-done = bf16[6,200,512]{2,0,1:T(8,128)(2,1)} async-done(((bf16[6,50,512]{2,0,1:T(8,128)(2,1)}), bf16[6,200,512]{2,0,1:T(8,128)(2,1)}) %all-gather.12.cloned.1.call-update) | async-done | bytes 1228816 | tf_op jit(solution)/shard_map/all_gather | solution.py:37
  210.6 37.2 %all-gather.18.cloned.1.call-done = bf16[6,200,512]{2,0,1:T(8,128)(2,1)} async-done(((bf16[6,50,512]{2,0,1:T(8,128)(2,1)}), bf16[6,200,512]{2,0,1:T(8,128)(2,1)}) %all-gather.18.cloned.1.call-update) | async-done | bytes 1228816 | tf_op jit(solution)/shard_map/all_gather | solution.py:47
  250.7 35.6 %all-gather.20.cloned.1.call-done = bf16[6,200,512]{2,0,1:T(8,128)(2,1)} async-done(((bf16[6,50,512]{2,0,1:T(8,128)(2,1)}), bf16[6,200,512]{2,0,1:T(8,128)(2,1)}) %all-gather.20.cloned.1.call-update) | async-done | bytes 1228816 | tf_op jit(solution)/shard_map/all_gather | solution.py:47
  311.2 30.2 %all-gather.14.cloned.1.call-done = bf16[512,16,512]{2,0,1:T(8,128)(2,1)} async-done(((bf16[64,16,512]{2,0,1:T(8,128)(2,1)}), bf16[512,16,512]{2,0,1:T(8,128)(2,1)}) %all-gather.14.cloned.1.call-update) | async-done | bytes 8388624 | tf_op jit(solution)/shard_map/all_gather | solution.py:96
  341.4 10.2 fusion.28
  351.6 46.1 %all-gather.16.cloned.1.call-done = bf16[512,16,512]{0,2,1:T(8,128)(2,1)} async-done(((bf16[512,16,64]{0,2,1:T(8,128)(2,1)}), bf16[512,16,512]{0,2,1:T(8,128)(2,1)}) %all-gather.16.cloned.1.call-update) | async-done | bytes 8388624 | tf_op jit(solution)/shard_map/all_gather | solution.py:97
  397.7 21.4 %add_convert_fusion = (bf16[16,192,512]{2,1,0:T(8,128)(2,1)S(1)}, f32[16,192,512]{2,1,0:T(8,128)}) fusion(f32[16,192,512]{2,1,0:T(8,128)} %get-tuple-element.97, u16[192,512]{1,0:T(8,128)(2,1)} %get-tuple-element.65, u16[192,512]{1,0:T(8,128)(2,1)S(1)} %get-tuple-element.64, bf16[16,192,512]{2,1,0:T(8,128)(2,1)} %bitcast.149, ...), kind=kOutput, calls=%fused_computation.31 | convolution fusion | flops 1731723264 | bytes 27656192 | tf_op jit(solution)/shard_map/ecd,fed->ecf/dot_general | solution.py:199
  424.8 9.1 convolution_convert_fusion.2
  464.1 258.1 %all-reduce.15.cloned.1.call-done = (f32[6,200,512]{2,1,0:T(8,128)}, f32[6,200,512]{2,1,0:T(8,128)}, f32[6,200,512]{2,1,0:T(8,128)}) async-done(((f32[6,200,512]{2,1,0:T(8,128)}, f32[6,200,512]{2,1,0:T(8,128)}, f32[6,200,512]{2,1,0:T(8,128)}), (f32[6,200,512]{2,1,0:T(8,128)}, f32[6,200,512]{2,1,0:T(8,128)}, f32[6,200,512]{2,1,0:T(8,128)})) %all-reduce.15.cloned.1.call-update) | async-done | bytes 7372816
  736.1 37.1 %all-gather.22.cloned.1.call-done = bf16[6,200,512]{2,0,1:T(8,128)(2,1)} async-done(((bf16[6,50,512]{2,0,1:T(8,128)(2,1)}), bf16[6,200,512]{2,0,1:T(8,128)(2,1)}) %all-gather.22.cloned.1.call-update) | async-done | bytes 1228816 | tf_op jit(solution)/shard_map/all_gather | solution.py:47
  792.1 95.3 %all-reduce.13.cloned.1.call-done = f32[6,200,512]{2,1,0:T(8,128)} async-done(((f32[6,200,512]{2,1,0:T(8,128)}), f32[6,200,512]{2,1,0:T(8,128)}) %all-reduce.13.cloned.1.call-update) | async-done | bytes 2457616
  898.4 10.2 convolution_bitcast_fusion
  910.5 10.1 convolution_bitcast_fusion.1
  920.6 20.3 %copy.323 = f32[512,16,512]{2,1,0:T(8,128)} copy(f32[512,16,512]{0,2,1:T(8,128)} %convolution_bitcast_fusion.1) | data formatting | bytes 33554432 | tf_op jit(solution)/shard_map/ecd,ecf->def/transpose | solution.py:207
  945.5 14.4 %reduce-scatter.24.cloned.1.call-done = f32[64,2]{1,0:T(8,128)} async-done(((f32[512,2]{1,0:T(8,128)}), f32[64,2]{1,0:T(8,128)}) %reduce-scatter.24.cloned.1.call-update) | async-done | bytes 528
  960.7 12.6 all-reduce.5
  973.3 23.8 %reduce-scatter.18.cloned.1.call-done = f32[128,64]{0,1:T(8,128)} async-done(((f32[128,512]{0,1:T(8,128)}), f32[128,64]{0,1:T(8,128)}) %reduce-scatter.18.cloned.1.call-update) | async-done | bytes 32784 | tf_op jit(solution)/shard_map/reduce_scatter | solution.py:274
  997.2 38.9 %reduce-scatter.16.cloned.1.call-done = f32[64,3,128]{2,0,1:T(8,128)} async-done(((f32[512,3,128]{2,0,1:T(8,128)}), f32[64,3,128]{2,0,1:T(8,128)}) %reduce-scatter.16.cloned.1.call-update) | async-done | bytes 98320 | tf_op jit(solution)/shard_map/reduce_scatter | solution.py:273
  1036.1 120.4 %reduce-scatter.22.cloned.1.call-done = f32[512,16,64]{0,2,1:T(8,128)} async-done(((f32[512,16,512]{0,2,1:T(8,128)}), f32[512,16,64]{0,2,1:T(8,128)}) %reduce-scatter.22.cloned.1.call-update) | async-done | bytes 2097168 | tf_op jit(solution)/shard_map/reduce_scatter | solution.py:277
  1156.5 120.4 %reduce-scatter.20.cloned.1.call-done = f32[64,16,512]{2,1,0:T(8,128)} async-done(((f32[512,16,512]{2,1,0:T(8,128)}), f32[64,16,512]{2,1,0:T(8,128)}) %reduce-scatter.20.cloned.1.call-update) | async-done | bytes 2097168 | tf_op jit(solution)/shard_map/reduce_scatter | solution.py:276
  (351 shorter events, 161.2 us)
Async XLA Ops:
  7.2 53.5 %all-gather.10.cloned.1.call-start = ((), (), s32[]{:S(2)}) async-start(), calls=%async_computation.6 | async-start | bytes 2048000 | tf_op jit(solution)/shard_map/all_gather | solution.py:37
  17.6 152.6 %copy-start.83 = (f32[512,1]{0,1:T(1,128)}, f32[512,1]{0,1:T(1,128)S(1)}, u32[]{:S(2)}) copy-start(f32[512,1]{0,1:T(1,128)S(1)} %get-tuple-element.92) | copy-start | bytes 6148
  22.1 145.5 %all-reduce.11.cloned.1.call-start = ((), (), s32[]{:S(2)}) async-start(), calls=%async_computation.19 | async-start | bytes 4915200
  69.8 139.0 %all-gather.12.cloned.1.call-start = ((), (), s32[]{:S(2)}) async-start(), calls=%async_computation.7 | async-start | bytes 2048000 | tf_op jit(solution)/shard_map/all_gather | solution.py:37
  70.8 111.4 %copy-start.28 = (f32[6,50]{0,1:T(8,128)}, f32[6,50]{0,1:T(8,128)S(1)}, u32[]{:S(2)}) copy-start(f32[6,50]{0,1:T(8,128)S(1)} %copy.272) | copy-start | bytes 3604
  171.5 76.4 %all-gather.18.cloned.1.call-start = ((), (), s32[]{:S(2)}) async-start(), calls=%async_computation.10 | async-start | bytes 2048000 | tf_op jit(solution)/shard_map/all_gather | solution.py:47
  186.2 100.2 %all-gather.20.cloned.1.call-start = ((), (), s32[]{:S(2)}) async-start(), calls=%async_computation.11 | async-start | bytes 2048000 | tf_op jit(solution)/shard_map/all_gather | solution.py:47
  186.8 154.6 %all-gather.14.cloned.1.call-start = ((), (), s32[]{:S(2)}) async-start(), calls=%async_computation.8 | async-start | bytes 9437184 | tf_op jit(solution)/shard_map/all_gather | solution.py:96
  188.5 209.3 %all-gather.16.cloned.1.call-start = ((), (), s32[]{:S(2)}) async-start(), calls=%async_computation.9 | async-start | bytes 9437184 | tf_op jit(solution)/shard_map/all_gather | solution.py:97
  189.2 532.9 %all-reduce.15.cloned.1.call-start = ((), (), s32[]{:S(2)}) async-start(), calls=%async_computation.21 | async-start | bytes 14745600
  463.4 261.6 %copy-start.3 = (bf16[6,50,512]{2,1,0:T(8,128)(2,1)S(1)}, bf16[6,50,512]{2,1,0:T(8,128)(2,1)}, u32[]{:S(2)}) copy-start(bf16[6,50,512]{2,1,0:T(8,128)(2,1)} %param.11) | copy-start | bytes 921604
  463.5 261.6 %copy-start.5 = (f32[6,50,512]{2,1,0:T(8,128)S(1)}, f32[6,50,512]{2,1,0:T(8,128)}, u32[]{:S(2)}) copy-start(f32[6,50,512]{2,1,0:T(8,128)} %copy-done.4) | copy-start | bytes 1843204
  463.5 261.6 %copy-start.17 = (bf16[6,50,512]{2,1,0:T(8,128)(2,1)S(1)}, bf16[6,50,512]{2,1,0:T(8,128)(2,1)}, u32[]{:S(2)}) copy-start(bf16[6,50,512]{2,1,0:T(8,128)(2,1)} %param.21) | copy-start | bytes 921604
  463.5 261.6 %copy-start.29 = (f32[6,50]{0,1:T(8,128)S(1)}, f32[6,50]{0,1:T(8,128)}, u32[]{:S(2)}) copy-start(f32[6,50]{0,1:T(8,128)} %copy-done.28) | copy-start | bytes 3604
  463.5 261.6 %copy-start.59 = (f32[6,50]{0,1:T(8,128)S(1)}, f32[6,50]{0,1:T(8,128)}, u32[]{:S(2)}) copy-start(f32[6,50]{0,1:T(8,128)} %copy-done.58) | copy-start | bytes 3604
  463.5 261.6 %copy-start.61 = (f32[6,50]{0,1:T(8,128)S(1)}, f32[6,50]{0,1:T(8,128)}, u32[]{:S(2)}) copy-start(f32[6,50]{0,1:T(8,128)} %copy-done.60) | copy-start | bytes 3604
  463.5 309.7 %all-gather.22.cloned.1.call-start = ((), (), s32[]{:S(2)}) async-start(), calls=%async_computation.12 | async-start | bytes 2048000 | tf_op jit(solution)/shard_map/all_gather | solution.py:47
  736.0 151.4 %all-reduce.13.cloned.1.call-start = ((), (), s32[]{:S(2)}) async-start(), calls=%async_computation.20 | async-start | bytes 4915200
  789.6 153.1 %reduce-scatter.26.cloned.1.call-start = ((), (), s32[]{:S(2)}) async-start(), calls=%async_computation.18 | async-start | bytes 294912
  792.1 167.9 %reduce-scatter.24.cloned.1.call-start = ((), (), s32[]{:S(2)}) async-start(), calls=%async_computation.17 | async-start | bytes 294912
  891.8 105.4 %reduce-scatter.18.cloned.1.call-start = ((), (), s32[]{:S(2)}) async-start(), calls=%async_computation.14 | async-start | bytes 294912 | tf_op jit(solution)/shard_map/reduce_scatter | solution.py:274
  894.9 141.2 %reduce-scatter.16.cloned.1.call-start = ((), (), s32[]{:S(2)}) async-start(), calls=%async_computation.13 | async-start | bytes 884736 | tf_op jit(solution)/shard_map/reduce_scatter | solution.py:273
  898.3 258.1 %reduce-scatter.22.cloned.1.call-start = ((), (), s32[]{:S(2)}) async-start(), calls=%async_computation.16 | async-start | bytes 18874368 | tf_op jit(solution)/shard_map/reduce_scatter | solution.py:277
  908.6 368.3 %reduce-scatter.20.cloned.1.call-start = ((), (), s32[]{:S(2)}) async-start(), calls=%async_computation.15 | async-start | bytes 18874368 | tf_op jit(solution)/shard_map/reduce_scatter | solution.py:276
  (84 other events, 1672.4 us)
Sparse Core Ops, SparseCore 0:
  22.2 38.3 all-gather.9
  70.0 97.6 all-reduce.10
  171.6 37.1 all-gather.11
  210.8 37.0 all-gather.17
  249.3 37.0 all-gather.19
  288.1 53.2 all-gather.13
  343.3 54.3 all-gather.15
  463.6 258.5 all-reduce.14
  736.1 37.0 all-gather.21
  789.7 97.6 all-reduce.12
  890.5 32.6 reduce-scatter.25
  926.3 33.5 reduce-scatter.23
  963.5 33.6 reduce-scatter.17
  1001.1 34.9 reduce-scatter.15
  1040.5 115.9 reduce-scatter.21
  1160.9 115.9 reduce-scatter.19
where the time goes:
time: 1290 us; the launch traced here: 1280 us
  waiting for transfers between devices  994 us (77%)
  matrix products  132 us (10%)
  local copies, waits for them, and re-layouts  62.8 us (5%)
  blocking collectives  49.8 us (4%)
  other arithmetic  27.5 us (2%)
  between operations  16.9 us (1%)
    unnamed x21, waiting for transfers between devices  465 us
    reduce_scatter x1, waiting for transfers between devices, body(): lax.psum_scatter(grad_expin, 'dp', scatter_dimension=0, tiled=True)  120 us
    reduce_scatter x1, waiting for transfers between devices, body(): lax.psum_scatter(grad_expout, 'dp', scatter_dimension=2, tiled=True)  120 us
    all_gather x3, waiting for transfers between devices, grads_in(): lax.all_gather(as_sent(values), 'tensor', axis=1, tiled=True)  110 us
    all_gather x1, waiting for transfers between devices, body(): lax.all_gather(w_out, 'dp', axis=2, tiled=True)  46.1 us
    all_gather x2, waiting for transfers between devices, rows_in(): return lax.all_gather(values, 'tensor', axis=1, tiled=True)  38.9 us
    reduce_scatter x1, waiting for transfers between devices, body(): lax.psum_scatter(grad_qkv, 'dp', scatter_dimension=0, tiled=True)  38.9 us
    all_gather x1, waiting for transfers between devices, body(): lax.all_gather(w_in, 'dp', axis=0, tiled=True)  30.2 us
  transfers between devices with their start and end apart: 16, of which 15 were waited for; matrix products, arithmetic and copies ran while one was open for 8% of the time, Pallas kernels for 0%

commit v1 on v0

--- a/solution.py
+++ b/solution.py
@@ -1,8 +1,11 @@
 import math
+from typing import NamedTuple
 
 import jax
 import jax.numpy as jnp
 from jax import lax
+from jax.experimental import pallas as pl
+from jax.experimental.pallas import tpu as pltpu
 from jax.sharding import PartitionSpec as P
 
 HEAD_DIM = 64
@@ -161,19 +164,6 @@
     )
     gate_grid = gates.reshape(images, quarter, 2)
     output = middle + gate_grid[:, :, 0:1] * first_own + gate_grid[:, :, 1:2] * second_own
-    regathered = (
-        lax.all_gather(gains, "dp", axis=0, tiled=True),
-        lax.all_gather(w_qkv, "dp", axis=0, tiled=True),
-        lax.all_gather(w_o, "dp", axis=1, tiled=True),
-        lax.all_gather(w_router, "dp", axis=0, tiled=True),
-        lax.all_gather(w_in, "dp", axis=0, tiled=True),
-        lax.all_gather(w_out, "dp", axis=2, tiled=True),
-    )
-    qkv_all = regathered[1]
-    outproj_all = regathered[2]
-    router_all = regathered[3]
-    expin_all = regathered[4]
-    expout_all = regathered[5]
     grad_output = cotangent.astype(jnp.float32)
     grad_first = (gate_grid[:, :, 0:1] * grad_output).astype(jnp.bfloat16)
     grad_second = (gate_grid[:, :, 1:2] * grad_output).astype(jnp.bfloat16)
@@ -288,6 +278,823 @@
     )
 
 
+MESH = pl.DeviceIdType.MESH
+BF = jnp.bfloat16
+F32 = jnp.float32
+VMEM_BYTES = 60 << 20
+
+
+class Sizes(NamedTuple):
+    n_dp: int
+    n_t: int
+    images: int
+    quarter: int
+    rows: int
+    irows: int
+    width: int
+    shard: int
+    heads: int
+    experts: int
+    ff: int
+    lanes: int
+
+    @property
+    def half(self):
+        return self.experts // 2
+
+    @property
+    def slots(self):
+        return self.half * CAP
+
+
+def up(value, step):
+    return -(-value // step) * step
+
+
+def norm_parts(values):
+    centre = values - jnp.mean(values, -1, keepdims=True)
+    scale = lax.rsqrt(jnp.mean(centre * centre, -1, keepdims=True) + epsilon)
+    return centre * scale, scale
+
+
+def norm_back(values, gain, grad):
+    unit, scale = norm_parts(values)
+    inner = grad * gain
+    mean_a = jnp.mean(inner, -1, keepdims=True)
+    mean_b = jnp.mean(inner * unit, -1, keepdims=True)
+    return scale * (inner - mean_a - unit * mean_b), unit
+
+
+def dot(a, b):
+    return jnp.dot(a, b, preferred_element_type=F32)
+
+
+def dot_nt(a, b):
+    return lax.dot_general(a, b, (((1,), (1,)), ((), ())), preferred_element_type=F32)
+
+
+def dot_tn(a, b):
+    return lax.dot_general(a, b, (((0,), (0,)), ((), ())), preferred_element_type=F32)
+
+
+class Place:
+    def __init__(self, s):
+        self.s = s
+        self.dp = lax.axis_index("dp")
+        self.t = lax.axis_index("tensor")
+        self.c = lax.rem(self.dp, 2)
+        self.x = lax.rem(self.dp // 2, 2)
+        self.y = self.dp // 4
+        self.chip = self.dp // 2
+        self.chip_x = self.y * 2 + (1 - self.x)
+        self.chip_y = (1 - self.y) * 2 + self.x
+        self.sib = (self.chip * 2 + (1 - self.c), self.t)
+        self.nx = (self.chip_x * 2 + self.c, self.t)
+        self.ny = (self.chip_y * 2 + self.c, self.t)
+
+    def ring_dp(self, k):
+        return lax.rem(self.dp + k, self.s.n_dp)
+
+    def ring_t(self, k):
+        return lax.rem(self.t + k, self.s.n_t)
+
+    def from_t(self, k):
+        return lax.rem(self.t + self.s.n_t - k, self.s.n_t)
+
+    def greet(self):
+        barrier = pltpu.get_barrier_semaphore()
+        for k in range(1, self.s.n_dp):
+            pl.semaphore_signal(barrier, inc=1, device_id=(self.ring_dp(k), self.t), device_id_type=MESH)
+        for k in range(1, self.s.n_t):
+            pl.semaphore_signal(barrier, inc=1, device_id=(self.dp, self.ring_t(k)), device_id_type=MESH)
+        pl.semaphore_wait(barrier, self.s.n_dp + self.s.n_t - 2)
+
+
+class Copies:
+    def __init__(self, send, recv, local):
+        self.send, self.recv, self.local = send, recv, local
+        self.n = 0
+        self.m = 0
+        self.sent = []
+
+    def to(self, src, dst, device):
+        copy = pltpu.make_async_remote_copy(
+            src_ref=src,
+            dst_ref=dst,
+            send_sem=self.send.at[self.n],
+            recv_sem=self.recv.at[self.n],
+            device_id=device,
+            device_id_type=MESH,
+        )
+        self.n += 1
+        copy.start()
+        self.sent.append(copy)
+        return copy
+
+    def here(self, src, dst):
+        copy = pltpu.make_async_copy(src, dst, self.local.at[self.m])
+        self.m += 1
+        copy.start()
+        return copy
+
+    def finish(self):
+        for copy in self.sent:
+            copy.wait_send()
+
+
+def head_masks(s):
+    lane = lax.broadcasted_iota(jnp.int32, (s.irows, s.heads), 1)
+    return [(lane // HEAD_DIM) == h for h in range(s.heads // HEAD_DIM)]
+
+
+def stack_heads(values, masks):
+    zero = jnp.zeros_like(values)
+    return jnp.concatenate([jnp.where(mask, values, zero) for mask in masks], 0)
+
+
+def pick_heads(stacked, masks, irows):
+    out = stacked[:irows]
+    for h in range(1, len(masks)):
+        out = jnp.where(masks[h], stacked[h * irows : (h + 1) * irows], out)
+    return out
+
+
+def front_kernel(
+    s,
+    x_ref, dz_ref, wq_ref, wo_ref, sm_ref, win_ref, wout_ref, live_ref, tgt_ref,
+    win_all, wout_all, n2_all, dz_all, prob_all, tgt_all,
+    y_ref, n2_ref, prob_ref, qkv_ref, p_ref, n1_ref, o_ref, wq_all, wo_all, small_ref,
+    x_all, sm_all, wo_z, blk, img, oimg, oblk, o_send, send, recv, local,
+):
+    here = Place(s)
+    dp, t, c = here.dp, here.t, here.c
+    here.greet()
+    go = Copies(send, recv, local)
+    nt = s.n_t
+
+    keep_in = go.here(win_ref.at[c], win_all.at[:, dp])
+    keep_out = go.here(wout_ref.at[c], wout_all.at[:, dp])
+    give_in = go.to(win_ref.at[1 - c], win_all.at[:, dp], here.sib)
+    give_out = go.to(wout_ref.at[1 - c], wout_all.at[:, dp], here.sib)
+    keep_sm = go.here(sm_ref, sm_all.at[dp])
+    keep_wq = go.here(wq_ref, wq_all.at[dp])
+    keep_wo = go.here(wo_ref, wo_z.at[t])
+    wo_copies = [go.to(wo_ref, wo_z.at[t], (dp, here.ring_t(k))) for k in range(1, nt)]
+    sm_copies = [go.to(sm_ref, sm_all.at[dp], (here.ring_dp(k), t)) for k in range(1, s.n_dp)]
+    wq_copies = [go.to(wq_ref, wq_all.at[dp], (here.ring_dp(k), t)) for k in range(1, s.n_dp)]
+    x_copies = [go.to(x_ref, x_all.at[t], (dp, here.ring_t(k))) for k in range(1, nt)]
+    tgt_copy = go.to(tgt_ref, tgt_all.at[c], here.sib)
+    keep_tgt = go.here(tgt_ref, tgt_all.at[c])
+    dz_sib = go.to(dz_ref, dz_all.at[c, t], here.sib)
+    keep_dz = go.here(dz_ref, dz_all.at[c, t])
+
+    mine = pl.ds(2 * here.chip, 2)
+    keep_in.wait()
+    give_in.wait_recv()
+    in_x = go.to(win_all.at[:, mine], win_all.at[:, mine], here.nx)
+    in_y = go.to(win_all.at[:, mine], win_all.at[:, mine], here.ny)
+
+    keep_sm.wait()
+    for copy in sm_copies:
+        copy.wait_recv()
+    small = jnp.sum(sm_all[...].astype(F32), 0)
+    small_ref[...] = small
+    gain_one = small[s.experts : s.experts + 1]
+    gain_two = small[s.experts + 1 : s.experts + 2]
+    keep_wq.wait()
+    for copy in wq_copies:
+        copy.wait_recv()
+
+    keep_out.wait()
+    give_out.wait_recv()
+    out_x = go.to(wout_all.at[:, mine], wout_all.at[:, mine], here.nx)
+    out_y = go.to(wout_all.at[:, mine], wout_all.at[:, mine], here.ny)
+
+    keep_wo.wait()
+    for copy in wo_copies:
+        copy.wait_recv()
+    keep_wo_all = go.here(wo_z, wo_all.at[dp])
+    wo_out = [go.to(wo_z, wo_all.at[dp], (here.ring_dp(k), t)) for k in range(1, s.n_dp)]
+
+    def project(slot, values):
+        unit, _ = norm_parts(values.astype(F32))
+        normed = (unit * gain_one).astype(BF)
+        n1_ref[slot] = normed
+        weights = wq_all[...].reshape(s.width, 3 * s.heads)
+        blk[slot] = dot(normed, weights)
+
+    project(t, x_ref[...])
+    for k, copy in enumerate(x_copies, 1):
+        copy.wait_recv()
+        project(here.from_t(k), x_all[here.from_t(k)])
+
+    dz_copies = [go.to(dz_ref, dz_all.at[c, t], (dp, here.ring_t(k))) for k in range(1, nt)]
+
+    from_x = pl.ds(2 * here.chip_x, 2)
+    from_y = pl.ds(2 * here.chip_y, 2)
+    low_half, high_half = pl.ds(0, s.half // 2), pl.ds(s.half // 2, s.half // 2)
+    in_x.wait_recv()
+    in_on_y = go.to(win_all.at[low_half, from_x], win_all.at[low_half, from_x], here.ny)
+    in_y.wait_recv()
+    in_on_x = go.to(win_all.at[high_half, from_y], win_all.at[high_half, from_y], here.nx)
+
+    length = s.quarter * nt
+    img[:, pl.ds(length, s.irows - length), :] = jnp.zeros((s.images, s.irows - length, 3 * s.heads), F32)
+    for i in range(s.images):
+        for q in range(nt):
+            img[i, pl.ds(q * s.quarter, s.quarter), :] = blk[q, pl.ds(i * s.quarter, s.quarter), :]
+
+    masks = head_masks(s)
+
+    def attend(i, carry):
+        block = img[i].astype(BF)
+        qkv_ref[i] = block
+        queries = stack_heads(block[:, : s.heads], masks)
+        scores = dot_nt(queries, block[:, s.heads : 2 * s.heads]) * (1.0 / math.sqrt(HEAD_DIM))
+        key = lax.broadcasted_iota(jnp.int32, scores.shape, 1)
+        scores = jnp.where(key < TOK_IMG, scores, negative_fill)
+        expd = jnp.exp(scores - jnp.max(scores, -1, keepdims=True))
+        probs = (expd / jnp.sum(expd, -1, keepdims=True)).astype(BF)
+        p_ref[i] = probs
+        oimg[i] = pick_heads(dot(probs, block[:, 2 * s.heads :]), masks, s.irows)
+        return carry
+
+    lax.fori_loop(0, s.images, attend, 0)
+    used = s.images * s.quarter
+    for q in range(nt):
+        oblk[q, pl.ds(used, s.rows - used), :] = jnp.zeros((s.rows - used, s.heads), F32)
+        for i in range(s.images):
+            oblk[q, pl.ds(i * s.quarter, s.quarter), :] = oimg[i, pl.ds(q * s.quarter, s.quarter), :]
+        o_send[q] = oblk[q].astype(BF)
+    o_copies = [go.to(o_send.at[here.ring_t(k)], o_ref.at[t], (dp, here.ring_t(k))) for k in range(1, nt)]
+    o_ref[t] = o_send[t]
+
+    keep_wo_all.wait()
+    for copy in wo_out:
+        copy.wait_recv()
+    for copy in o_copies:
+        copy.wait_recv()
+    branch = jnp.zeros((s.rows, s.width), F32)
+    for q in range(nt):
+        branch = branch + dot_nt(o_ref[q], wo_all[:, q].reshape(s.width, s.heads))
+    middle = x_ref[...].astype(F32) + live_ref[...] * branch
+    y_ref[...] = middle
+    unit, _ = norm_parts(middle)
+    normed_two = (unit * gain_two).astype(BF)
+    n2_ref[...] = normed_two
+    n2_sib = go.to(n2_ref, n2_all.at[c, t], here.sib)
+    n2_copies = [go.to(n2_ref, n2_all.at[c, t], (dp, here.ring_t(k))) for k in range(1, nt)]
+    keep_n2 = go.here(n2_ref, n2_all.at[c, t])
+    logits = dot_nt(small[: s.experts].astype(BF), normed_two)
+    expd = jnp.exp(logits - jnp.max(logits, 0, keepdims=True))
+    prob_ref[...] = jnp.zeros((s.experts, s.lanes), F32)
+    prob_ref[:, : s.rows] = expd / jnp.sum(expd, 0, keepdims=True)
+    pr_sib = go.to(prob_ref, prob_all.at[c, t], here.sib)
+    pr_copies = [go.to(prob_ref, prob_all.at[c, t], (dp, here.ring_t(k))) for k in range(1, nt)]
+    keep_pr = go.here(prob_ref, prob_all.at[c, t])
+
+    out_x.wait_recv()
+    out_on_y = go.to(wout_all.at[low_half, from_x], wout_all.at[low_half, from_x], here.ny)
+    out_y.wait_recv()
+    out_on_x = go.to(wout_all.at[high_half, from_y], wout_all.at[high_half, from_y], here.nx)
+
+    on = []
+    for k in range(1, nt):
+        slot = here.from_t(k)
+        for array, copies in ((dz_all, dz_copies), (n2_all, n2_copies), (prob_all, pr_copies)):
+            copies[k - 1].wait_recv()
+            on.append(go.to(array.at[c, slot], array.at[c, slot], here.sib))
+
+    for copy in (keep_tgt, keep_dz, keep_n2, keep_pr):
+        copy.wait()
+    for copy in [tgt_copy, dz_sib, n2_sib, pr_sib, in_on_y, in_on_x, out_on_y, out_on_x] + on:
+        copy.wait_recv()
+    go.finish()
+
+
+def expert_kernel(
+    s,
+    n2_ref, dz_ref, tgt_ref, prob_ref, win_ref, wout_ref,
+    dx_ref, ge_ref, gi_ref, go_ref, dpr_ref,
+    pr, dpr,
+):
+    e = pl.program_id(0)
+    core = lax.rem(lax.axis_index("dp"), 2)
+    expert = core * s.half + e
+
+    @pl.when(e == 0)
+    def _():
+        for q in range(2):
+            pr[q] = jnp.concatenate([prob_ref[q, k][:, : s.rows] for k in range(s.n_t)], 1)
+
+    ids = expert * CAP + lax.broadcasted_iota(jnp.int32, (CAP, s.n_t * s.rows), 0)
+    hits, xs, zs, gates = [], [], [], []
+    for q in range(2):
+        hit = (tgt_ref[q, 0:1, :] == ids) | (tgt_ref[q, 1:2, :] == ids)
+        hot = jnp.where(hit, 1.0, 0.0).astype(BF)
+        hits.append(hit)
+        xs.append(dot(hot, n2_ref[q]).astype(BF))
+        zs.append(dot(hot, dz_ref[q]))
+        row = pr[q, pl.ds(expert, 1), :]
+        gates.append(jnp.sum(jnp.where(hit, row, 0.0), 1, keepdims=True))
+    x_in = jnp.concatenate(xs, 0)
+    z_in = jnp.concatenate(zs, 0)
+    gate = jnp.concatenate(gates, 0)
+    w_in, w_out = win_ref[0], wout_ref[0]
+    hidden = dot(x_in, w_in)
+    size = jnp.abs(hidden)
+    bell = jnp.exp(-0.5 * hidden * hidden)
+    u = 1.0 / (1.0 + (0.3275911 / math.sqrt(2.0)) * size)
+    poly = u * (0.254829592 + u * (-0.284496736 + u * (1.421413741 + u * (-1.453152027 + u * 1.061405429))))
+    tail = 0.5 * poly * bell
+    phi = jnp.where(hidden >= 0, 1.0 - tail, tail)
+    active = (hidden * phi).astype(BF)
+    slope = phi + hidden * bell * (1.0 / math.sqrt(2.0 * math.pi))
+    out = dot_nt(active, w_out).astype(BF).astype(F32)
+    dgate = jnp.sum(z_in * out, 1, keepdims=True)
+    grad = (gate * z_in).astype(BF)
+    go_ref[...] = dot_tn(grad, active).astype(BF).reshape(go_ref.shape)
+    dhidden = (dot(grad, w_out) * slope).astype(BF)
+    gi_ref[...] = dot_tn(x_in, dhidden).astype(BF).reshape(gi_ref.shape)
+    dx_ref[...] = dot_nt(dhidden, w_in).astype(BF).reshape(dx_ref.shape)
+    ge_ref[...] = (gate * out).astype(BF).reshape(ge_ref.shape)
+    for q in range(2):
+        row = jnp.sum(jnp.where(hits[q], dgate[q * CAP : (q + 1) * CAP], 0.0), 0, keepdims=True)
+        dpr[q, pl.ds(e, 1), :] = row
+
+    @pl.when(e == s.half - 1)
+    def _():
+        dpr_ref[...] = jnp.zeros(dpr_ref.shape, F32)
+        for q in range(2):
+            for k in range(s.n_t):
+                dpr_ref[q, k, :, : s.rows] = dpr[q][:, k * s.rows : (k + 1) * s.rows]
+
+
+def back_kernel(
+    s,
+    x_ref, dz_ref, y_ref, n2_ref, prob_ref, live_ref, tcol_ref, qkv_ref, p_ref, n1_ref, o_ref,
+    wq_ref, wo_ref, small_ref, dpr_ref, dx_ref, ge_ref, gi_ref, go_ref,
+    out_ref, gx_ref, gw_ref, gqo_ref, gsm_ref,
+    dxv, gev, dprf, dprz, comb, rs_send, rs_recv, m_send, m_recv, n_send, n_recv,
+    da_s, do_send, do_recv, doblk, doimg, dimg, dblk, dqkv, go_send, go_recv, gq_send, gq_recv,
+    sm_send, sm_z, sm_dp, own, ra, rb, sa, sb, fa, fb, fin, fin_recv, send, recv, local,
+):
+    here = Place(s)
+    dp, t, c = here.dp, here.t, here.c
+    x, y = here.x, here.y
+    here.greet()
+    go = Copies(send, recv, local)
+    nt = s.n_t
+    per = s.half // 2
+
+    ra_copies, rb_copies = [], []
+    for j in range(2):
+        piece = pl.ds(j * per, per)
+        ra_copies.append(go.to(gi_ref.at[:, 1 - x, piece], ra.at[j], here.nx))
+        rb_copies.append(go.to(go_ref.at[1 - y, :, piece], rb.at[j], here.ny))
+    dx_sib = go.to(dx_ref.at[1 - c], dxv.at[c], here.sib)
+    dpr_sib = go.to(dpr_ref.at[1 - c], dprf.at[:, c], here.sib)
+    ge_sib = go.to(ge_ref.at[1 - c], gev.at[c], here.sib)
+    keep_dx = go.here(dx_ref.at[c], dxv.at[c])
+    keep_dpr = go.here(dpr_ref.at[c], dprf.at[:, c])
+    keep_ge = go.here(ge_ref.at[c], gev.at[c])
+    own_a = go.here(gi_ref.at[:, x], own.at[0])
+    own_b = go.here(go_ref.at[y], own.at[1])
+
+    chunk = s.slots // 2
+
+    def combine(values, half, q, total):
+        first = tcol_ref[q, :, 0:1]
+        second = tcol_ref[q, :, 1:2]
+        for j in range(2):
+            ids = half * s.slots + j * chunk + lax.broadcasted_iota(jnp.int32, (s.rows, chunk), 1)
+            hot = jnp.where((first == ids) | (second == ids), 1.0, 0.0).astype(BF)
+            total = total + dot(hot, values[half, pl.ds(j * chunk, chunk), :])
+        return total
+
+    zero_rows = jnp.zeros((s.rows, s.width), F32)
+    keep_dx.wait()
+    for k in range(nt):
+        comb[k] = combine(dxv, c, here.ring_t(k), zero_rows)
+    dx_sib.wait_recv()
+    rs_copies = []
+    for k in range(1, nt):
+        q = here.ring_t(k)
+        rs_send[k - 1] = combine(dxv, 1 - c, q, comb[k]).astype(BF)
+        rs_copies.append(go.to(rs_send.at[k - 1], rs_recv.at[k - 1], (dp, q)))
+    keep_dpr.wait()
+    dpr_sib.wait_recv()
+    dpr_copies = [go.to(dprf.at[here.ring_t(k)], dprz.at[k - 1], (dp, here.ring_t(k))) for k in range(1, nt)]
+    comb[0] = combine(dxv, 1 - c, t, comb[0])
+
+    keep_ge.wait()
+    ge_sib.wait_recv()
+    for k in range(1, nt):
+        q = here.ring_t(k)
+        m_send[k - 1] = combine(gev, 1 - c, q, combine(gev, c, q, zero_rows)).astype(BF)
+    out_own = combine(gev, 1 - c, t, combine(gev, c, t, zero_rows))
+    gx_ref[...] = out_own
+
+    dprobs = dprf[t]
+    for k, copy in enumerate(dpr_copies):
+        copy.wait_recv()
+        dprobs = dprobs + dprz[k]
+    dprobs = dprobs.reshape(s.experts, s.lanes)
+    probs = prob_ref[...]
+    dlogits = (probs * (dprobs - jnp.sum(probs * dprobs, 0, keepdims=True))).astype(BF)[:, : s.rows]
+    small = small_ref[...]
+    gain_one = small[s.experts : s.experts + 1]
+    gain_two = small[s.experts + 1 : s.experts + 2]
+    grad_router = dot_tn(n2_ref[...], dlogits.T).T
+    dn2 = comb[0] + dot_tn(dlogits, small[: s.experts].astype(BF))
+    for k, copy in enumerate(rs_copies):
+        copy.wait_recv()
+        dn2 = dn2 + rs_recv[k].astype(F32)
+    middle = y_ref[...]
+    dy_ln, unit = norm_back(middle, gain_two, dn2)
+    dgain_two = jnp.sum(dn2 * unit, 0, keepdims=True)
+    dy = dz_ref[...].astype(F32) + dy_ln
+    comb[0] = dy
+    da = (live_ref[...] * dy).astype(BF)
+    da_s[...] = da
+    for q in range(nt):
+        do_send[q] = dot(da, wo_ref[:, q].reshape(s.width, s.heads)).astype(BF)
+    do_copies = [go.to(do_send.at[here.ring_t(k)], do_recv.at[t], (dp, here.ring_t(k))) for k in range(1, nt)]
+    do_recv[t] = do_send[t]
+    for q in range(nt):
+        go_send[q] = dot_tn(da, o_ref[q]).astype(BF)
+
+    own_a.wait()
+    own_b.wait()
+
+    def add_up(a, b, out):
+        def step(i, carry):
+            out[i] = (a[i].astype(F32) + b[i].astype(F32)).astype(out.dtype)
+            return carry
+
+        lax.fori_loop(0, out.shape[0], step, 0)
+
+    fa_copies, fb_copies = [], []
+
+    def pump(j):
+        piece = pl.ds(j * per, per)
+        ra_copies[j].wait_recv()
+        add_up(own.at[0, 1 - y, piece], ra.at[j, 1 - y], sa.at[j])
+        fa_copies.append(go.to(sa.at[j], fa.at[j], here.ny))
+        rb_copies[j].wait_recv()
+        add_up(own.at[1, 1 - x, piece], rb.at[j, 1 - x], sb.at[j])
+        fb_copies.append(go.to(sb.at[j], fb.at[j], here.nx))
+
+    pump(0)
+
+    for copy in do_copies:
+        copy.wait_recv()
+    go_copies = [go.to(go_send.at[here.ring_t(k)], go_recv.at[k - 1], (dp, here.ring_t(k))) for k in range(1, nt)]
+    m_copies = [go.to(m_send.at[k - 1], m_recv.at[k - 1], (dp, here.ring_t(k))) for k in range(1, nt)]
+    length = s.quarter * nt
+    doblk[...] = do_recv[...].astype(F32)
+    doimg[:, pl.ds(length, s.irows - length), :] = jnp.zeros((s.images, s.irows - length, s.heads), F32)
+    for i in range(s.images):
+        for q in range(nt):
+            doimg[i, pl.ds(q * s.quarter, s.quarter), :] = doblk[q, pl.ds(i * s.quarter, s.quarter), :]
+    masks = head_masks(s)
+    scale_factor = 1.0 / math.sqrt(HEAD_DIM)
+
+    def attend_back(i, carry):
+        block = qkv_ref[i]
+        queries = stack_heads(block[:, : s.heads], masks)
+        grads = stack_heads(doimg[i].astype(BF), masks)
+        probs = p_ref[i]
+        dvalues = dot_tn(probs, grads)
+        dprob = dot_nt(grads, block[:, 2 * s.heads :])
+        wide = probs.astype(F32)
+        both = wide * dprob
+        dscore = (both - wide * jnp.sum(both, -1, keepdims=True)).astype(BF)
+        dqueries = pick_heads(dot(dscore, block[:, s.heads : 2 * s.heads]), masks, s.irows)
+        dkeys = dot_tn(dscore, queries)
+        dimg[i, :, : s.heads] = dqueries * scale_factor
+        dimg[i, :, s.heads : 2 * s.heads] = dkeys * scale_factor
+        dimg[i, :, 2 * s.heads :] = dvalues
+        return carry
+
+    lax.fori_loop(0, s.images, attend_back, 0)
+    used = s.images * s.quarter
+    for q in range(nt):
+        dblk[q, pl.ds(used, s.rows - used), :] = jnp.zeros((s.rows - used, 3 * s.heads), F32)
+        for i in range(s.images):
+            dblk[q, pl.ds(i * s.quarter, s.quarter), :] = dimg[i, pl.ds(q * s.quarter, s.quarter), :]
+    dqkv[...] = dblk[...].astype(BF)
+    w_qkv = wq_ref[...].reshape(s.width, 3 * s.heads)
+    n_copies = []
+    dgain_one = jnp.zeros((1, s.width), F32)
+    for k in list(range(1, nt)) + [0]:
+        q = here.ring_t(k)
+        part = dot_nt(dqkv[q], w_qkv)
+        dgain_one = dgain_one + jnp.sum(part * n1_ref[q].astype(F32), 0, keepdims=True)
+        if k:
+            n_send[k - 1] = part.astype(BF)
+            n_copies.append(go.to(n_send.at[k - 1], n_recv.at[k - 1], (dp, q)))
+        else:
+            comb[1] = part
+    dgain_one = dgain_one / gain_one
+
+    sm_send[0] = jnp.concatenate(
+        [grad_router, dgain_one, dgain_two, jnp.zeros((sm_send.shape[1] - s.experts - 2, s.width), F32)], 0
+    )
+    sm_copies = [go.to(sm_send.at[0], sm_z.at[k - 1], (dp, here.ring_t(k))) for k in range(1, nt)]
+
+    grad_qkv = jnp.zeros((s.width, 3 * s.heads), F32)
+    for q in range(nt):
+        grad_qkv = grad_qkv + dot_tn(n1_ref[q], dqkv[q])
+    gq_send[:, :, : 3 * s.heads] = grad_qkv.astype(BF).reshape(s.n_dp, s.shard, 3 * s.heads)
+    total = go_send[t].astype(F32)
+    for k, copy in enumerate(go_copies):
+        copy.wait_recv()
+        total = total + go_recv[k].astype(F32)
+    gq_send[:, :, 3 * s.heads :] = total.astype(BF).reshape(s.n_dp, s.shard, s.heads)
+    gq_copies = [go.to(gq_send.at[here.ring_dp(k)], gq_recv.at[k - 1], (here.ring_dp(k), t)) for k in range(1, s.n_dp)]
+    pump(1)
+    total = sm_send[0]
+    for k, copy in enumerate(sm_copies):
+        copy.wait_recv()
+        total = total + sm_z[k]
+    sm_send[1] = total
+    smd_copies = [go.to(sm_send.at[1], sm_dp.at[k - 1], (here.ring_dp(k), t)) for k in range(1, s.n_dp)]
+
+    dn1 = comb[1]
+    for k, copy in enumerate(n_copies):
+        copy.wait_recv()
+        dn1 = dn1 + n_recv[k].astype(F32)
+    result = gx_ref[...] + middle
+    for k, copy in enumerate(m_copies):
+        copy.wait_recv()
+        result = result + m_recv[k].astype(F32)
+    out_ref[...] = result.astype(BF)
+    dx_ln, _ = norm_back(x_ref[...].astype(F32), gain_one, dn1)
+    gx_ref[...] = comb[0] + dx_ln
+
+    grad = gq_send[dp].astype(F32)
+    for k, copy in enumerate(gq_copies):
+        copy.wait_recv()
+        grad = grad + gq_recv[k].astype(F32)
+    gqo_ref[...] = grad
+
+    mine = pl.ds(pl.multiple_of(c * s.shard, s.shard), s.shard)
+    other = pl.ds(pl.multiple_of((1 - c) * s.shard, s.shard), s.shard)
+    fin_copies = []
+    for w, (first, mine_first, second, copies) in enumerate(((ra, y, fa, fa_copies), (rb, x, fb, fb_copies))):
+        for j in range(2):
+            copies[j].wait_recv()
+
+            def last(i, carry, w=w, first=first, mine_first=mine_first, second=second, j=j):
+                def total(rows):
+                    return (
+                        own[w, mine_first, j * per + i, rows, :].astype(F32)
+                        + first[j, mine_first, i, rows, :].astype(F32)
+                        + second[j, i, rows, :].astype(F32)
+                    )
+
+                fin[w, j, i] = total(other).astype(BF)
+                gw_ref[w, c, j * per + i] = total(mine)
+                return carry
+
+            lax.fori_loop(0, per, last, 0)
+            fin_copies.append(go.to(fin.at[w, j], fin_recv.at[w, j], here.sib))
+    total = sm_send[1]
+    for k, copy in enumerate(smd_copies):
+        copy.wait_recv()
+        total = total + sm_dp[k]
+    gsm_ref[...] = total
+    for w in range(2):
+        for j in range(2):
+            fin_copies[2 * w + j].wait_recv()
+
+            def widen(i, carry, w=w, j=j):
+                gw_ref[w, 1 - c, j * per + i] = fin_recv[w, j, i].astype(F32)
+                return carry
+
+            lax.fori_loop(0, per, widen, 0)
+    go.finish()
+
+
+VSPEC = pl.BlockSpec(memory_space=pltpu.VMEM)
+ASPEC = pl.BlockSpec(memory_space=pl.ANY)
+
+
+def shape(dims, kind):
+    return jax.ShapeDtypeStruct(dims, kind)
+
+
+def linked_body(
+    block_input,
+    gains,
+    w_qkv,
+    w_o,
+    w_router,
+    w_in,
+    w_out,
+    pictures_alive_per_shard,
+    expert_ids,
+    slot_index,
+    cotangent,
+):
+    images, quarter, width = block_input.shape
+    n_dp, n_t = lax.axis_size("dp"), lax.axis_size("tensor")
+    shard, experts, ff = w_in.shape
+    heads = w_qkv.shape[2]
+    length = quarter * n_t
+    used = images * quarter
+    rows = up(used, 16)
+    s = Sizes(n_dp, n_t, images, quarter, rows, up(length, 16), width, shard, heads, experts, ff, up(rows, 128))
+    dp, t = lax.axis_index("dp"), lax.axis_index("tensor")
+
+    def by_rows(values):
+        return jnp.pad(values.reshape(used, width), ((0, rows - used), (0, 0)))
+
+    x_own, dz_own = by_rows(block_input), by_rows(cotangent)
+    wq = w_qkv.reshape(shard, 3 * heads)
+    wo = w_o.T
+    sm_rows = up(experts + 2, 16)
+    small = jnp.zeros((sm_rows, width), BF)
+    piece = jnp.concatenate([w_router.T, gains.T], 0)
+    small = lax.dynamic_update_slice(small, piece, (0, dp * shard))
+    win_t = w_in.transpose(1, 0, 2).reshape(2, s.half, shard, ff)
+    wout_t = w_out.transpose(1, 2, 0).reshape(2, s.half, shard, ff)
+    place = t * quarter + jnp.arange(quarter)
+    live = (jnp.arange(images) < pictures_alive_per_shard[0])[:, None] & (place < TOK_IMG)[None, :]
+    live = jnp.pad(live.astype(F32).reshape(used, 1), ((0, rows - used), (0, 0)))
+    targets = jnp.where(slot_index >= 0, expert_ids * CAP + slot_index, -1)
+    targets = targets.reshape(images, n_t, quarter, 2).transpose(1, 0, 2, 3).reshape(n_t, used, 2)
+    targets = jnp.pad(targets, ((0, 0), (0, rows - used), (0, 0)), constant_values=-1)
+    tgt_rows = jnp.pad(targets.reshape(n_t * rows, 2).T, ((0, 6), (0, 0)), constant_values=-1)
+
+    params = dict(has_side_effects=True, vmem_limit_bytes=VMEM_BYTES)
+    front_links = 2 + (n_t - 1) * 6 + (n_dp - 1) * 3 + 8 + 4 + (n_t - 1) * 3
+    front = pl.pallas_call(
+        lambda *refs: front_kernel(s, *refs),
+        out_shape=(
+            shape((s.half, n_dp, shard, ff), BF),
+            shape((s.half, n_dp, shard, ff), BF),
+            shape((2, n_t, rows, width), BF),
+            shape((2, n_t, rows, width), BF),
+            shape((2, n_t, experts, s.lanes), F32),
+            shape((2, 8, n_t * rows), jnp.int32),
+            shape((rows, width), F32),
+            shape((rows, width), BF),
+            shape((experts, s.lanes), F32),
+            shape((images, s.irows, 3 * heads), BF),
+            shape((images, heads // HEAD_DIM * s.irows, s.irows), BF),
+            shape((n_t, rows, width), BF),
+            shape((n_t, rows, heads), BF),
+            shape((n_dp, shard, 3 * heads), BF),
+            shape((n_dp, n_t, shard, heads), BF),
+            shape((sm_rows, width), F32),
+        ),
+        in_specs=[VSPEC] * 5 + [ASPEC] * 2 + [VSPEC] * 2,
+        out_specs=[ASPEC] * 6 + [VSPEC] * 10,
+        scratch_shapes=[
+            pltpu.VMEM((n_t, rows, width), BF),
+            pltpu.VMEM((n_dp, sm_rows, width), BF),
+            pltpu.VMEM((n_t, shard, heads), BF),
+            pltpu.VMEM((n_t, rows, 3 * heads), F32),
+            pltpu.VMEM((images, s.irows, 3 * heads), F32),
+            pltpu.VMEM((images, s.irows, heads), F32),
+            pltpu.VMEM((n_t, rows, heads), F32),
+            pltpu.VMEM((n_t, rows, heads), BF),
+            pltpu.SemaphoreType.DMA((front_links,)),
+            pltpu.SemaphoreType.DMA((front_links,)),
+            pltpu.SemaphoreType.DMA((10,)),
+        ],
+        compiler_params=pltpu.CompilerParams(collective_id=1, **params),
+        name="front",
+    )
+    (
+        win_all, wout_all, n2_all, dz_all, prob_all, tgt_all,
+        y, n2, prob, qkv, p, n1, o, wq_all, wo_all, small_sum,
+    ) = front(x_own, dz_own, wq, wo, small, win_t, wout_t, live, tgt_rows)
+
+    tokens = n_t * rows
+    two_y, two_x = n_dp // 4, 2
+    whole = lambda *dims: pl.BlockSpec(dims, lambda e: (0,) * len(dims))
+    experts_call = pl.pallas_call(
+        lambda *refs: expert_kernel(s, *refs),
+        grid=(s.half,),
+        out_shape=(
+            shape((2, s.slots, width), BF),
+            shape((2, s.slots, width), BF),
+            shape((two_y, two_x, s.half, 2 * shard, ff), BF),
+            shape((two_y, two_x, s.half, 2 * shard, ff), BF),
+            shape((2, n_t, s.half, s.lanes), F32),
+        ),
+        in_specs=[
+            whole(2, tokens, width),
+            whole(2, tokens, width),
+            whole(2, 8, tokens),
+            whole(2, n_t, experts, s.lanes),
+            pl.BlockSpec((1, width, ff), lambda e: (e, 0, 0)),
+            pl.BlockSpec((1, width, ff), lambda e: (e, 0, 0)),
+        ],
+        out_specs=[
+            pl.BlockSpec((2, CAP, width), lambda e: (0, e, 0)),
+            pl.BlockSpec((2, CAP, width), lambda e: (0, e, 0)),
+            pl.BlockSpec((two_y, two_x, 1, 2 * shard, ff), lambda e: (0, 0, e, 0, 0)),
+            pl.BlockSpec((two_y, two_x, 1, 2 * shard, ff), lambda e: (0, 0, e, 0, 0)),
+            whole(2, n_t, s.half, s.lanes),
+        ],
+        scratch_shapes=[
+            pltpu.VMEM((2, experts, tokens), F32),
+            pltpu.VMEM((2, s.half, tokens), F32),
+        ],
+        compiler_params=pltpu.CompilerParams(vmem_limit_bytes=VMEM_BYTES),
+        name="experts",
+    )
+    dx, ge, gi, go, dpr = experts_call(
+        n2_all.reshape(2, tokens, width),
+        dz_all.reshape(2, tokens, width),
+        tgt_all,
+        prob_all,
+        win_all.reshape(s.half, width, ff),
+        wout_all.reshape(s.half, width, ff),
+    )
+
+    per = s.half // 2
+    gsm_rows = up(experts + 2, 8)
+    back_links = 4 + 3 + (n_t - 1) * 7 + 4 + 4 + 2 * (n_dp - 1)
+    out, gx, gw, gqo, gsm = pl.pallas_call(
+        lambda *refs: back_kernel(s, *refs),
+        out_shape=(
+            shape((rows, width), BF),
+            shape((rows, width), F32),
+            shape((2, 2, s.half, shard, ff), F32),
+            shape((shard, 4 * heads), F32),
+            shape((gsm_rows, width), F32),
+        ),
+        in_specs=[VSPEC] * 14 + [ASPEC] * 5,
+        out_specs=[VSPEC] * 5,
+        scratch_shapes=[
+            pltpu.VMEM((2, s.slots, width), BF),
+            pltpu.VMEM((2, s.slots, width), BF),
+            pltpu.VMEM((n_t, 2, s.half, s.lanes), F32),
+            pltpu.VMEM((n_t - 1, 2, s.half, s.lanes), F32),
+            pltpu.VMEM((n_t, rows, width), F32),
+            pltpu.VMEM((n_t - 1, rows, width), BF),
+            pltpu.VMEM((n_t - 1, rows, width), BF),
+            pltpu.VMEM((n_t - 1, rows, width), BF),
+            pltpu.VMEM((n_t - 1, rows, width), BF),
+            pltpu.VMEM((n_t - 1, rows, width), BF),
+            pltpu.VMEM((n_t - 1, rows, width), BF),
+            pltpu.VMEM((rows, width), BF),
+            pltpu.VMEM((n_t, rows, heads), BF),
+            pltpu.VMEM((n_t, rows, heads), BF),
+            pltpu.VMEM((n_t, rows, heads), F32),
+            pltpu.VMEM((images, s.irows, heads), F32),
+            pltpu.VMEM((images, s.irows, 3 * heads), F32),
+            pltpu.VMEM((n_t, rows, 3 * heads), F32),
+            pltpu.VMEM((n_t, rows, 3 * heads), BF),
+            pltpu.VMEM((n_t, width, heads), BF),
+            pltpu.VMEM((n_t - 1, width, heads), BF),
+            pltpu.VMEM((n_dp, shard, 4 * heads), BF),
+            pltpu.VMEM((n_dp - 1, shard, 4 * heads), BF),
+            pltpu.VMEM((2, gsm_rows, width), F32),
+            pltpu.VMEM((n_t - 1, gsm_rows, width), F32),
+            pltpu.VMEM((n_dp - 1, gsm_rows, width), F32),
+            pltpu.VMEM((2, 2, s.half, 2 * shard, ff), BF),
+            pltpu.VMEM((2, 2, per, 2 * shard, ff), BF),
+            pltpu.VMEM((2, 2, per, 2 * shard, ff), BF),
+            pltpu.VMEM((2, per, 2 * shard, ff), BF),
+            pltpu.VMEM((2, per, 2 * shard, ff), BF),
+            pltpu.VMEM((2, per, 2 * shard, ff), BF),
+            pltpu.VMEM((2, per, 2 * shard, ff), BF),
+            pltpu.VMEM((2, 2, per, shard, ff), BF),
+            pltpu.VMEM((2, 2, per, shard, ff), BF),
+            pltpu.SemaphoreType.DMA((back_links,)),
+            pltpu.SemaphoreType.DMA((back_links,)),
+            pltpu.SemaphoreType.DMA((5,)),
+        ],
+        compiler_params=pltpu.CompilerParams(collective_id=2, **params),
+        name="back",
+    )(
+        x_own, dz_own, y, n2, prob, live, targets, qkv, p, n1, o,
+        wq_all, wo_all, small_sum, dpr, dx, ge, gi, go,
+    )
+
+    def by_image(values):
+        return values[:used].reshape(images, quarter, width)
+
+    gw = gw.reshape(2, experts, shard, ff)
+    own_small = lax.dynamic_slice(gsm, (0, dp * shard), (gsm_rows, shard))
+    return (
+        by_image(out),
+        by_image(gx),
+        own_small[experts : experts + 2].T,
+        gqo[:, : 3 * heads].reshape(shard, 3, heads),
+        gqo[:, 3 * heads :].T,
+        own_small[:experts].T,
+        gw[0].transpose(1, 0, 2),
+        gw[1].transpose(2, 0, 1),
+    )
+
+
 def solution(mesh):
     placed = (
         P("dp", "tensor", None),
@@ -302,8 +1109,9 @@
         P("dp", None, None),
         P("dp", "tensor", None),
     )
+    linked = mesh.shape["dp"] == 8 and mesh.shape["tensor"] > 1
     return jax.shard_map(
-        body,
+        linked_body if linked else body,
         mesh=mesh,
         in_specs=placed,
         out_specs=(

time: 1290 us -> 299 us (0.23)
  waiting for transfers between devices: 994 us -> 0 us
  Pallas kernels: 0 us -> 272 us
  matrix products: 132 us -> 0 us
  blocking collectives: 49.8 us -> 0 us
  local copies, waits for them, and re-layouts: 62.8 us -> 24 us
  other arithmetic: 27.5 us -> 0.78 us
  between operations: 16.9 us -> 1.48 us
    unnamed x21 -> x0, waiting for transfers between devices: 465 us -> none
    reduce_scatter x4 -> x0, waiting for transfers between devices: 304 us -> none  [the longest x1 120 us: body(): lax.psum_scatter(grad_expin, 'dp', scatter_dimension=0, tiled=True)]
    pallas_call x0 -> x3, Pallas kernels: none -> 272 us  [the longest x1 127 us: linked_body(): pl.pallas_call(lambda *refs: back_kernel(s, *refs), out_shape=(shape((row...]
    all_gather x7 -> x0, waiting for transfers between devices: 225 us -> none  [the longest x3 110 us: grads_in(): lax.all_gather(as_sent(values), 'tensor', axis=1, tiled=True)]
    dot_general x28 -> x0, matrix products: 131 us -> none  [the longest x1 21.4 us: body(): jnp.einsum('ecd,fed->ecf', grad_expert, expout_all, preferred_element_typ...]
    all_gather x4 -> x0, blocking collectives: 37.3 us -> none  [the longest x1 10.3 us: body(): lax.all_gather(gains, 'dp', axis=0, tiled=True)]
    unnamed x201 -> x17, local copies, waits for them, and re-layouts: 20.8 us -> 1.58 us
    transpose x1 -> x4, local copies, waits for them, and re-layouts: 20.3 us -> 5.61 us  [the longest x1 1.55 us: linked_body(): win_t = w_in.transpose(1, 0, 2).reshape(2, s.half, shard, ff)]
  transfers between devices with their start and end apart: 16 -> 0, of which waited for: 15 -> 0; matrix products, arithmetic and copies ran while one was open for 8% -> 0% of each run, Pallas kernels for 0% -> 0%
where the time goes in v1:
time: 299 us; the launch traced here: 298 us
  Pallas kernels  272 us (91%)
  local copies, waits for them, and re-layouts  24 us (8%)
    pallas_call x1, Pallas kernels, linked_body(): pl.pallas_call(lambda *refs: back_kernel(s, *refs), out_shape=(shape((row...  127 us
    pallas_call x1, Pallas kernels, linked_body(): front(x_own, dz_own, wq, wo, small, win_t, wout_t, live, tgt_rows)  113 us
    pallas_call x1, Pallas kernels, linked_body(): experts_call(n2_all.reshape(2, tokens, width), dz_all.reshape(2, tokens,...  31.8 us

profile of v1, /device:TPU:0, one launch (start us, length us, event | category | flops | bytes accessed | tf_op | source)
XLA Modules:
  0.0 298.2 jit_solution(17579371209270795521)
XLA Ops:
  0.7 1.1 reshape.103
  1.9 0.7 pad.21.refs_0_
  2.6 1.1 reshape.104
  3.7 0.7 pad.22.refs_1_
  4.4 0.6 copy_bitcast_fusion.2.refs_2_
  5.1 0.5 dynamic_update_slice.3.refs_4_
  5.6 1.5 copy.26
  7.9 0.1 convert_element_type.17
  8.1 0.7 pad_convert_fusion.refs_7_.refs_5_
  8.8 0.1 reshape.108
  9.0 0.2 copy.29
  9.3 0.2 copy.30
  9.5 0.6 pad.26.refs_8_
  10.1 113.1 %front.1 = (bf16[8,8,64,512]{3,2,1,0:T(8,128)(2,1)}, bf16[8,8,64,512]{3,2,1,0:T(8,128)(2,1)}, bf16[2,4,304,512]{3,2,1,0:T(8,128)(2,1)}, bf16[2,4,304,512]{3,2,1,...) custom-call(bf16[304,512]{1,0:T(8,128)(2,1)} %pad.21.refs_0_, ...), custom_call_target="tpu_custom_call" | custom-call | tf_op jit(solution)/shard_map/front/pallas_call | solution.py:974
  123.3 31.8 %experts.1 = (bf16[2,1536,512]{2,1,0:T(8,128)(2,1)}, bf16[2,1536,512]{2,1,0:T(8,128)(2,1)}, bf16[2,2,8,128,512]{4,3,2,1,0:T(8,128)(2,1)}, bf16[2,2,8,128,512]{4,3,2,1,0:T(8,128)(2,1)}, f32[2,4,8,384]{3,2,1,0:T(8,128)}) custom-call(bf16[2,1216,512]{2,1,0:T(8,128)(2,1)} %bitcast.53, bf16[2,1216,512]{2,1,0:T(8,128)(2,1)} %bitcast.54, ...), custom_call_target="tpu_custom_call" | custom-call | tf_op jit(solution)/shard_map/experts/pallas_call | solution.py:1011
  155.1 127.0 %back.1 = (bf16[304,512]{1,0:T(8,128)(2,1)}, f32[304,512]{1,0:T(8,128)}, f32[2,2,8,64,512]{4,3,2,1,0:T(8,128)}, f32[64,512]{1,0:T(8,128)}, f32[24,512]{1,0:T(8,128)}) custom-call(bf16[304,512]{1,0:T(8,128)(2,1)} %pad.21.refs_0_, bf16[304,512]{1,0:T(8,128)(2,1)} %pad.22.refs_1_, f32[304,512]{1,0:T(8,128)} %get-tuple-element.34.refs_2_, ...), custom_call_target="tpu_custom_call" | custom-call | tf_op jit(solution)/shard_map/back/pallas_call | solution.py:1023
  282.1 1.8 reshape.115
  283.9 2.0 reshape.116
  285.9 1.3 dynamic-slice_bitcast_fusion.1
  287.2 1.5 copy_bitcast_fusion.1
  288.8 1.4 slice_bitcast_fusion.1
  290.1 1.4 dynamic-slice_bitcast_fusion
  291.5 4.2 %fusion = (f32[1,2,8,64,512]{4,3,2,1,0:T(8,128)}, f32[1,2,8,64,512]{4,3,2,1,0:T(8,128)S(1)}) fusion(f32[2,2,8,64,512]{4,3,2,1,0:T(8,128)} %get-tuple-element.59), kind=kLoop, calls=%fused_computation.14 | loop fusion | bytes 8388608 | tf_op jit(solution)/shard_map/slice | solution.py:1094
  295.7 2.5 copy.39
  (25 shorter events, 0.3 us)
Async XLA Ops:
  0.6 3.8 %copy-start = (bf16[64,3,128]{2,0,1:T(8,128)(2,1)S(1)}, bf16[64,3,128]{2,0,1:T(8,128)(2,1)}, u32[]{:S(2)}) copy-start(bf16[64,3,128]{2,0,1:T(8,128)(2,1)} %param.13) | copy-start | bytes 147460
  0.7 4.4 %copy-start.7 = (bf16[64,2]{0,1:T(2,128)(2,1)S(1)}, bf16[64,2]{0,1:T(2,128)(2,1)}, u32[]{:S(2)}) copy-start(bf16[64,2]{0,1:T(2,128)(2,1)} %param.12) | copy-start | bytes 772
  0.7 4.4 %copy-start.6 = (bf16[64,16]{0,1:T(8,128)(2,1)S(1)}, bf16[64,16]{0,1:T(8,128)(2,1)}, u32[]{:S(2)}) copy-start(bf16[64,16]{0,1:T(8,128)(2,1)} %param.15) | copy-start | bytes 6148
  0.7 4.9 %copy-start.2 = (bf16[64,16,512]{2,1,0:T(8,128)(2,1)S(1)}, bf16[64,16,512]{2,1,0:T(8,128)(2,1)}, u32[]{:S(2)}) copy-start(bf16[64,16,512]{2,1,0:T(8,128)(2,1)} %param.16) | copy-start | bytes 3145732
  0.7 8.1 %copy-start.4 = (s32[6,200,2]{1,2,0:T(2,128)S(1)}, s32[6,200,2]{1,2,0:T(2,128)}, u32[]{:S(2)}) copy-start(s32[6,200,2]{1,2,0:T(2,128)} %param.20) | copy-start | bytes 28804
  0.7 8.1 %copy-start.5 = (s32[6,200,2]{1,2,0:T(2,128)S(1)}, s32[6,200,2]{1,2,0:T(2,128)}, u32[]{:S(2)}) copy-start(s32[6,200,2]{1,2,0:T(2,128)} %param.19) | copy-start | bytes 28804
  5.6 3.9 %copy-start.3 = (bf16[32,512]{1,0:T(8,128)(2,1)}, bf16[32,512]{1,0:T(8,128)(2,1)S(1)}, u32[]{:S(2)}) copy-start(bf16[32,512]{1,0:T(8,128)(2,1)S(1)} %dynamic_update_slice.3.refs_4_) | copy-start | bytes 98308
  9.3 145.8 %copy-start.1 = (s32[4,304,2]{2,1,0:T(8,128)}, s32[4,304,2]{2,1,0:T(8,128)S(1)}, u32[]{:S(2)}) copy-start(s32[4,304,2]{2,1,0:T(8,128)S(1)} %pad.25.refs_6_) | copy-start | bytes 29188

commit v2 on v1

--- a/solution.py
+++ b/solution.py
@@ -349,6 +349,11 @@
         self.chip_x = self.y * 2 + (1 - self.x)
         self.chip_y = (1 - self.y) * 2 + self.x
         self.sib = (self.chip * 2 + (1 - self.c), self.t)
+        self.nx_other = (self.chip_x * 2 + (1 - self.c), self.t)
+        self.ny_other = (self.chip_y * 2 + (1 - self.c), self.t)
+        self.pair = lax.rem(self.t, 2) * (-2) + self.t + 1
+        self.far = lax.rem(self.t + 2, 4)
+        self.cross = lax.rem(self.pair + 2, 4)
         self.nx = (self.chip_x * 2 + self.c, self.t)
         self.ny = (self.chip_y * 2 + self.c, self.t)
 
@@ -402,6 +407,64 @@
             copy.wait_send()
 
 
+def pieces_of(rows):
+    first = up(rows // 2, 16)
+    return [pl.ds(0, first), pl.ds(first, rows - first)]
+
+
+class Gather:
+    def __init__(self, go, here, own, full):
+        self.go, self.here, self.full = go, here, full
+        self.pieces = pieces_of(here.s.rows)
+        mine = full(here.t)
+        self.to_far = [go.to(own.at[p], mine.at[p], (here.dp, here.far)) for p in self.pieces]
+        self.to_pair = [go.to(own.at[p], mine.at[p], (here.dp, here.pair)) for p in self.pieces]
+
+    def relay(self):
+        block = self.full(self.here.far)
+        self.passed = []
+        for p, copy in zip(self.pieces, self.to_far):
+            copy.wait_recv()
+            self.passed.append(self.go.to(block.at[p], block.at[p], (self.here.dp, self.here.pair)))
+
+    def wait_pair(self):
+        for copy in self.to_pair:
+            copy.wait_recv()
+
+    def wait_cross(self):
+        for copy in self.passed:
+            copy.wait_recv()
+
+    def share(self, block):
+        return self.go.to(self.full(block), self.full(block), self.here.sib)
+
+
+class Reduce:
+    def __init__(self, go, here, send, recv):
+        self.go, self.here, self.send, self.recv = go, here, send, recv
+        self.pieces = pieces_of(here.s.rows)
+        self.copies = [[], [], []]
+
+    def put(self, k, p, device):
+        self.copies[k].append(self.go.to(self.send.at[k, p], self.recv.at[k, p], (self.here.dp, device)))
+
+    def pair(self, k, value):
+        self.send[k] = value.astype(BF)
+        for p in self.pieces:
+            self.put(k, p, self.here.pair)
+
+    def across(self, part):
+        for i, p in enumerate(self.pieces):
+            self.copies[0][i].wait_recv()
+            self.send[2, p] = (part[p] + self.recv[0, p].astype(F32)).astype(BF)
+            self.put(2, p, self.here.far)
+
+    def total(self, part):
+        for copy in self.copies[1] + self.copies[2]:
+            copy.wait_recv()
+        return part + self.recv[1].astype(F32) + self.recv[2].astype(F32)
+
+
 def head_masks(s):
     lane = lax.broadcasted_iota(jnp.int32, (s.irows, s.heads), 1)
     return [(lane // HEAD_DIM) == h for h in range(s.heads // HEAD_DIM)]
@@ -432,27 +495,26 @@
     go = Copies(send, recv, local)
     nt = s.n_t
 
-    keep_in = go.here(win_ref.at[c], win_all.at[:, dp])
-    keep_out = go.here(wout_ref.at[c], wout_all.at[:, dp])
-    give_in = go.to(win_ref.at[1 - c], win_all.at[:, dp], here.sib)
-    give_out = go.to(wout_ref.at[1 - c], wout_all.at[:, dp], here.sib)
+    wo_copies = [go.to(wo_ref, wo_z.at[t], (dp, here.ring_t(k))) for k in range(1, nt)]
+    x_all_blocks = Gather(go, here, x_ref, lambda block: x_all.at[block])
+    sm_copies = [go.to(sm_ref, sm_all.at[dp], (here.ring_dp(k), t)) for k in range(1, s.n_dp)]
+    wq_copies = [go.to(wq_ref, wq_all.at[dp], (here.ring_dp(k), t)) for k in range(1, s.n_dp)]
+
+    def spread(shard, full):
+        to = full.at[:, dp]
+        half, rest = shard.at[c], shard.at[1 - c]
+        from_x = [go.to(half, to, here.nx), go.to(rest, to, here.nx_other)]
+        from_y = [go.to(half, to, here.ny), go.to(rest, to, here.ny_other)]
+        return from_x, from_y, go.to(rest, to, here.sib), go.here(half, to)
+
+    in_x, in_y, in_sib, keep_in = spread(win_ref, win_all)
     keep_sm = go.here(sm_ref, sm_all.at[dp])
     keep_wq = go.here(wq_ref, wq_all.at[dp])
     keep_wo = go.here(wo_ref, wo_z.at[t])
-    wo_copies = [go.to(wo_ref, wo_z.at[t], (dp, here.ring_t(k))) for k in range(1, nt)]
-    sm_copies = [go.to(sm_ref, sm_all.at[dp], (here.ring_dp(k), t)) for k in range(1, s.n_dp)]
-    wq_copies = [go.to(wq_ref, wq_all.at[dp], (here.ring_dp(k), t)) for k in range(1, s.n_dp)]
-    x_copies = [go.to(x_ref, x_all.at[t], (dp, here.ring_t(k))) for k in range(1, nt)]
     tgt_copy = go.to(tgt_ref, tgt_all.at[c], here.sib)
     keep_tgt = go.here(tgt_ref, tgt_all.at[c])
     dz_sib = go.to(dz_ref, dz_all.at[c, t], here.sib)
     keep_dz = go.here(dz_ref, dz_all.at[c, t])
-
-    mine = pl.ds(2 * here.chip, 2)
-    keep_in.wait()
-    give_in.wait_recv()
-    in_x = go.to(win_all.at[:, mine], win_all.at[:, mine], here.nx)
-    in_y = go.to(win_all.at[:, mine], win_all.at[:, mine], here.ny)
 
     keep_sm.wait()
     for copy in sm_copies:
@@ -465,11 +527,6 @@
     for copy in wq_copies:
         copy.wait_recv()
 
-    keep_out.wait()
-    give_out.wait_recv()
-    out_x = go.to(wout_all.at[:, mine], wout_all.at[:, mine], here.nx)
-    out_y = go.to(wout_all.at[:, mine], wout_all.at[:, mine], here.ny)
-
     keep_wo.wait()
     for copy in wo_copies:
         copy.wait_recv()
@@ -484,20 +541,28 @@
         blk[slot] = dot(normed, weights)
 
     project(t, x_ref[...])
-    for k, copy in enumerate(x_copies, 1):
-        copy.wait_recv()
-        project(here.from_t(k), x_all[here.from_t(k)])
-
-    dz_copies = [go.to(dz_ref, dz_all.at[c, t], (dp, here.ring_t(k))) for k in range(1, nt)]
+    x_all_blocks.relay()
+    out_x, out_y, out_sib, keep_out = spread(wout_ref, wout_all)
+    project(here.far, x_all[here.far])
+    x_all_blocks.wait_pair()
+    project(here.pair, x_all[here.pair])
+    x_all_blocks.wait_cross()
+    project(here.cross, x_all[here.cross])
+    dz_blocks = Gather(go, here, dz_ref, lambda block: dz_all.at[c, block])
 
     from_x = pl.ds(2 * here.chip_x, 2)
     from_y = pl.ds(2 * here.chip_y, 2)
     low_half, high_half = pl.ds(0, s.half // 2), pl.ds(s.half // 2, s.half // 2)
-    in_x.wait_recv()
-    in_on_y = go.to(win_all.at[low_half, from_x], win_all.at[low_half, from_x], here.ny)
-    in_y.wait_recv()
-    in_on_x = go.to(win_all.at[high_half, from_y], win_all.at[high_half, from_y], here.nx)
-
+
+    def pass_on(full, by_x, by_y):
+        for copy in by_x:
+            copy.wait_recv()
+        on_y = go.to(full.at[low_half, from_x], full.at[low_half, from_x], here.ny)
+        for copy in by_y:
+            copy.wait_recv()
+        return on_y, go.to(full.at[high_half, from_y], full.at[high_half, from_y], here.nx)
+
+    in_on_y, in_on_x = pass_on(win_all, in_x, in_y)
     length = s.quarter * nt
     img[:, pl.ds(length, s.irows - length), :] = jnp.zeros((s.images, s.irows - length, 3 * s.heads), F32)
     for i in range(s.images):
@@ -529,6 +594,7 @@
     o_copies = [go.to(o_send.at[here.ring_t(k)], o_ref.at[t], (dp, here.ring_t(k))) for k in range(1, nt)]
     o_ref[t] = o_send[t]
 
+    dz_blocks.relay()
     keep_wo_all.wait()
     for copy in wo_out:
         copy.wait_recv()
@@ -543,7 +609,7 @@
     normed_two = (unit * gain_two).astype(BF)
     n2_ref[...] = normed_two
     n2_sib = go.to(n2_ref, n2_all.at[c, t], here.sib)
-    n2_copies = [go.to(n2_ref, n2_all.at[c, t], (dp, here.ring_t(k))) for k in range(1, nt)]
+    n2_blocks = Gather(go, here, n2_ref, lambda block: n2_all.at[c, block])
     keep_n2 = go.here(n2_ref, n2_all.at[c, t])
     logits = dot_nt(small[: s.experts].astype(BF), normed_two)
     expd = jnp.exp(logits - jnp.max(logits, 0, keepdims=True))
@@ -553,21 +619,23 @@
     pr_copies = [go.to(prob_ref, prob_all.at[c, t], (dp, here.ring_t(k))) for k in range(1, nt)]
     keep_pr = go.here(prob_ref, prob_all.at[c, t])
 
-    out_x.wait_recv()
-    out_on_y = go.to(wout_all.at[low_half, from_x], wout_all.at[low_half, from_x], here.ny)
-    out_y.wait_recv()
-    out_on_x = go.to(wout_all.at[high_half, from_y], wout_all.at[high_half, from_y], here.nx)
-
-    on = []
-    for k in range(1, nt):
-        slot = here.from_t(k)
-        for array, copies in ((dz_all, dz_copies), (n2_all, n2_copies), (prob_all, pr_copies)):
-            copies[k - 1].wait_recv()
-            on.append(go.to(array.at[c, slot], array.at[c, slot], here.sib))
-
-    for copy in (keep_tgt, keep_dz, keep_n2, keep_pr):
+    n2_blocks.relay()
+    on = [n2_blocks.share(here.far), dz_blocks.share(here.far)]
+    dz_blocks.wait_pair()
+    on.append(dz_blocks.share(here.pair))
+    dz_blocks.wait_cross()
+    on.append(dz_blocks.share(here.cross))
+    out_on_y, out_on_x = pass_on(wout_all, out_x, out_y)
+    n2_blocks.wait_pair()
+    on.append(n2_blocks.share(here.pair))
+    for k, copy in enumerate(pr_copies, 1):
+        copy.wait_recv()
+        on.append(go.to(prob_all.at[c, here.from_t(k)], prob_all.at[c, here.from_t(k)], here.sib))
+    n2_blocks.wait_cross()
+    on.append(n2_blocks.share(here.cross))
+    for copy in (keep_tgt, keep_dz, keep_n2, keep_pr, keep_in, keep_out):
         copy.wait()
-    for copy in [tgt_copy, dz_sib, n2_sib, pr_sib, in_on_y, in_on_x, out_on_y, out_on_x] + on:
+    for copy in [tgt_copy, dz_sib, n2_sib, pr_sib, in_sib, out_sib, in_on_y, in_on_x, out_on_y, out_on_x] + on:
         copy.wait_recv()
     go.finish()
 
@@ -635,9 +703,10 @@
     x_ref, dz_ref, y_ref, n2_ref, prob_ref, live_ref, tcol_ref, qkv_ref, p_ref, n1_ref, o_ref,
     wq_ref, wo_ref, small_ref, dpr_ref, dx_ref, ge_ref, gi_ref, go_ref,
     out_ref, gx_ref, gw_ref, gqo_ref, gsm_ref,
-    dxv, gev, dprf, dprz, comb, rs_send, rs_recv, m_send, m_recv, n_send, n_recv,
-    da_s, do_send, do_recv, doblk, doimg, dimg, dblk, dqkv, go_send, go_recv, gq_send, gq_recv,
-    sm_send, sm_z, sm_dp, own, ra, rb, sa, sb, fa, fb, fin, fin_recv, send, recv, local,
+    dxv, gev, dprf, dprz, comb, rs_send, rs_recv, m_send, m_recv, m_far, n_send, n_recv,
+    da_s, do_send, do_recv, doblk, doimg, dimg, dblk, dqkv, grads, gs_send, gs_recv, gx_send, gx_recv,
+    gy_send, gy_recv, gz_send, gz_recv, sm_send, sm_recv, own, ra, rb, sa, sb, fa, fb, fin, fin_recv,
+    send, recv, local,
 ):
     here = Place(s)
     dp, t, c = here.dp, here.t, here.c
@@ -674,27 +743,29 @@
 
     zero_rows = jnp.zeros((s.rows, s.width), F32)
     keep_dx.wait()
-    for k in range(nt):
-        comb[k] = combine(dxv, c, here.ring_t(k), zero_rows)
+    order = (here.cross, here.pair, here.far, t)
+    for k, q in enumerate(order):
+        comb[k] = combine(dxv, c, q, zero_rows)
     dx_sib.wait_recv()
-    rs_copies = []
-    for k in range(1, nt):
-        q = here.ring_t(k)
-        rs_send[k - 1] = combine(dxv, 1 - c, q, comb[k]).astype(BF)
-        rs_copies.append(go.to(rs_send.at[k - 1], rs_recv.at[k - 1], (dp, q)))
+    dn2_sum = Reduce(go, here, rs_send, rs_recv)
+    for k in range(2):
+        dn2_sum.pair(k, combine(dxv, 1 - c, order[k], comb[k]))
     keep_dpr.wait()
     dpr_sib.wait_recv()
     dpr_copies = [go.to(dprf.at[here.ring_t(k)], dprz.at[k - 1], (dp, here.ring_t(k))) for k in range(1, nt)]
-    comb[0] = combine(dxv, 1 - c, t, comb[0])
+    dn2_sum.across(combine(dxv, 1 - c, here.far, comb[2]))
+    comb[0] = combine(dxv, 1 - c, t, comb[3])
 
     keep_ge.wait()
     ge_sib.wait_recv()
-    for k in range(1, nt):
-        q = here.ring_t(k)
-        m_send[k - 1] = combine(gev, 1 - c, q, combine(gev, c, q, zero_rows)).astype(BF)
-    out_own = combine(gev, 1 - c, t, combine(gev, c, t, zero_rows))
-    gx_ref[...] = out_own
-
+
+    def forward_sum(q):
+        return combine(gev, 1 - c, q, combine(gev, c, q, zero_rows))
+
+    m_send[0] = forward_sum(here.cross).astype(BF)
+    m_send[1] = forward_sum(here.pair).astype(BF)
+    m_far[...] = forward_sum(here.far)
+    gx_ref[...] = forward_sum(t)
     dprobs = dprf[t]
     for k, copy in enumerate(dpr_copies):
         copy.wait_recv()
@@ -707,9 +778,7 @@
     gain_two = small[s.experts + 1 : s.experts + 2]
     grad_router = dot_tn(n2_ref[...], dlogits.T).T
     dn2 = comb[0] + dot_tn(dlogits, small[: s.experts].astype(BF))
-    for k, copy in enumerate(rs_copies):
-        copy.wait_recv()
-        dn2 = dn2 + rs_recv[k].astype(F32)
+    dn2 = dn2_sum.total(dn2)
     middle = y_ref[...]
     dy_ln, unit = norm_back(middle, gain_two, dn2)
     dgain_two = jnp.sum(dn2 * unit, 0, keepdims=True)
@@ -722,8 +791,8 @@
     do_copies = [go.to(do_send.at[here.ring_t(k)], do_recv.at[t], (dp, here.ring_t(k))) for k in range(1, nt)]
     do_recv[t] = do_send[t]
     for q in range(nt):
-        go_send[q] = dot_tn(da, o_ref[q]).astype(BF)
-
+        part = dot_tn(da, o_ref[q]).reshape(*grads.shape[:3], s.shard, s.heads)
+        grads[:, :, :, :, (3 + q) * s.heads : (4 + q) * s.heads] = part
     own_a.wait()
     own_b.wait()
 
@@ -745,12 +814,12 @@
         add_up(own.at[1, 1 - x, piece], rb.at[j, 1 - x], sb.at[j])
         fb_copies.append(go.to(sb.at[j], fb.at[j], here.nx))
 
-    pump(0)
-
     for copy in do_copies:
         copy.wait_recv()
-    go_copies = [go.to(go_send.at[here.ring_t(k)], go_recv.at[k - 1], (dp, here.ring_t(k))) for k in range(1, nt)]
-    m_copies = [go.to(m_send.at[k - 1], m_recv.at[k - 1], (dp, here.ring_t(k))) for k in range(1, nt)]
+    m_sum = Reduce(go, here, m_send, m_recv)
+    for k in range(2):
+        for p in m_sum.pieces:
+            m_sum.put(k, p, here.pair)
     length = s.quarter * nt
     doblk[...] = do_recv[...].astype(F32)
     doimg[:, pl.ds(length, s.irows - length), :] = jnp.zeros((s.images, s.irows - length, s.heads), F32)
@@ -778,6 +847,7 @@
         return carry
 
     lax.fori_loop(0, s.images, attend_back, 0)
+    pump(0)
     used = s.images * s.quarter
     for q in range(nt):
         dblk[q, pl.ds(used, s.rows - used), :] = jnp.zeros((s.rows - used, 3 * s.heads), F32)
@@ -785,59 +855,71 @@
             dblk[q, pl.ds(i * s.quarter, s.quarter), :] = dimg[i, pl.ds(q * s.quarter, s.quarter), :]
     dqkv[...] = dblk[...].astype(BF)
     w_qkv = wq_ref[...].reshape(s.width, 3 * s.heads)
-    n_copies = []
+    dn1_sum = Reduce(go, here, n_send, n_recv)
     dgain_one = jnp.zeros((1, s.width), F32)
-    for k in list(range(1, nt)) + [0]:
-        q = here.ring_t(k)
+    for k, q in enumerate(order):
         part = dot_nt(dqkv[q], w_qkv)
         dgain_one = dgain_one + jnp.sum(part * n1_ref[q].astype(F32), 0, keepdims=True)
-        if k:
-            n_send[k - 1] = part.astype(BF)
-            n_copies.append(go.to(n_send.at[k - 1], n_recv.at[k - 1], (dp, q)))
+        if k < 2:
+            dn1_sum.pair(k, part)
         else:
-            comb[1] = part
+            comb[2 * k - 3] = part
     dgain_one = dgain_one / gain_one
 
-    sm_send[0] = jnp.concatenate(
-        [grad_router, dgain_one, dgain_two, jnp.zeros((sm_send.shape[1] - s.experts - 2, s.width), F32)], 0
-    )
-    sm_copies = [go.to(sm_send.at[0], sm_z.at[k - 1], (dp, here.ring_t(k))) for k in range(1, nt)]
+    pump(1)
 
     grad_qkv = jnp.zeros((s.width, 3 * s.heads), F32)
     for q in range(nt):
         grad_qkv = grad_qkv + dot_tn(n1_ref[q], dqkv[q])
-    gq_send[:, :, : 3 * s.heads] = grad_qkv.astype(BF).reshape(s.n_dp, s.shard, 3 * s.heads)
-    total = go_send[t].astype(F32)
-    for k, copy in enumerate(go_copies):
-        copy.wait_recv()
-        total = total + go_recv[k].astype(F32)
-    gq_send[:, :, 3 * s.heads :] = total.astype(BF).reshape(s.n_dp, s.shard, s.heads)
-    gq_copies = [go.to(gq_send.at[here.ring_dp(k)], gq_recv.at[k - 1], (here.ring_dp(k), t)) for k in range(1, s.n_dp)]
-    pump(1)
-    total = sm_send[0]
+    grads[:, :, :, :, : 3 * s.heads] = grad_qkv.reshape(*grads.shape[:3], s.shard, 3 * s.heads)
+    gs_send[...] = grads[:, :, 1 - c].astype(BF)
+    sm_send[0] = jnp.concatenate(
+        [grad_router, dgain_one, dgain_two, jnp.zeros((sm_send.shape[1] - s.experts - 2, s.width), F32)], 0
+    )
+    step = [go.to(gs_send, gs_recv, here.sib), go.to(sm_send.at[0], sm_recv.at[0], here.sib)]
+    dn1_sum.across(comb[1])
+    m_sum.across(m_far[...])
+
+    def add_small(k):
+        sm_send[k + 1] = sm_send[k] + sm_recv[k]
+
+    for copy in step:
+        copy.wait_recv()
+    grads[:, :, c] = grads[:, :, c] + gs_recv[...].astype(F32)
+    add_small(0)
+    gx_send[...] = grads[:, 1 - x, c].astype(BF)
+    step = [go.to(gx_send, gx_recv, here.nx), go.to(sm_send.at[1], sm_recv.at[1], here.nx)]
+    for copy in step:
+        copy.wait_recv()
+    grads[:, x, c] = grads[:, x, c] + gx_recv[...].astype(F32)
+    add_small(1)
+    gy_send[...] = grads[1 - y, x, c].astype(BF)
+    step = [go.to(gy_send, gy_recv, here.ny), go.to(sm_send.at[2], sm_recv.at[2], here.ny)]
+    for copy in step:
+        copy.wait_recv()
+    add_small(2)
+    grads[y, x, c] = grads[y, x, c] + gy_recv[...].astype(F32)
+    gqo_ref[:, : 3 * s.heads] = grads[y, x, c, :, : 3 * s.heads]
+    for q in range(nt):
+        gz_send[q] = grads[y, x, c, :, (3 + q) * s.heads : (4 + q) * s.heads].astype(BF)
+    gz_copies = [go.to(gz_send.at[here.ring_t(k)], gz_recv.at[k - 1], (dp, here.ring_t(k))) for k in range(1, nt)]
+    sm_copies = [go.to(sm_send.at[3], sm_recv.at[2 + k], (dp, here.ring_t(k))) for k in range(1, nt)]
+
+    dn1 = dn1_sum.total(comb[3])
+    dx_ln, _ = norm_back(x_ref[...].astype(F32), gain_one, dn1)
+    result = gx_ref[...] + middle
+    gx_ref[...] = comb[0] + dx_ln
+    out_ref[...] = m_sum.total(result).astype(BF)
+    total = gz_send[t].astype(F32)
+    for k, copy in enumerate(gz_copies):
+        copy.wait_recv()
+        total = total + gz_recv[k].astype(F32)
+    gqo_ref[:, 3 * s.heads :] = total
+    total = sm_send[3]
     for k, copy in enumerate(sm_copies):
         copy.wait_recv()
-        total = total + sm_z[k]
-    sm_send[1] = total
-    smd_copies = [go.to(sm_send.at[1], sm_dp.at[k - 1], (here.ring_dp(k), t)) for k in range(1, s.n_dp)]
-
-    dn1 = comb[1]
-    for k, copy in enumerate(n_copies):
-        copy.wait_recv()
-        dn1 = dn1 + n_recv[k].astype(F32)
-    result = gx_ref[...] + middle
-    for k, copy in enumerate(m_copies):
-        copy.wait_recv()
-        result = result + m_recv[k].astype(F32)
-    out_ref[...] = result.astype(BF)
-    dx_ln, _ = norm_back(x_ref[...].astype(F32), gain_one, dn1)
-    gx_ref[...] = comb[0] + dx_ln
-
-    grad = gq_send[dp].astype(F32)
-    for k, copy in enumerate(gq_copies):
-        copy.wait_recv()
-        grad = grad + gq_recv[k].astype(F32)
-    gqo_ref[...] = grad
+        total = total + sm_recv[3 + k]
+    gsm_ref[...] = total
 
     mine = pl.ds(pl.multiple_of(c * s.shard, s.shard), s.shard)
     other = pl.ds(pl.multiple_of((1 - c) * s.shard, s.shard), s.shard)
@@ -860,11 +942,6 @@
 
             lax.fori_loop(0, per, last, 0)
             fin_copies.append(go.to(fin.at[w, j], fin_recv.at[w, j], here.sib))
-    total = sm_send[1]
-    for k, copy in enumerate(smd_copies):
-        copy.wait_recv()
-        total = total + sm_dp[k]
-    gsm_ref[...] = total
     for w in range(2):
         for j in range(2):
             fin_copies[2 * w + j].wait_recv()
@@ -929,7 +1006,7 @@
     tgt_rows = jnp.pad(targets.reshape(n_t * rows, 2).T, ((0, 6), (0, 0)), constant_values=-1)
 
     params = dict(has_side_effects=True, vmem_limit_bytes=VMEM_BYTES)
-    front_links = 2 + (n_t - 1) * 6 + (n_dp - 1) * 3 + 8 + 4 + (n_t - 1) * 3
+    front_links = 80
     front = pl.pallas_call(
         lambda *refs: front_kernel(s, *refs),
         out_shape=(
@@ -950,7 +1027,7 @@
             shape((n_dp, n_t, shard, heads), BF),
             shape((sm_rows, width), F32),
         ),
-        in_specs=[VSPEC] * 5 + [ASPEC] * 2 + [VSPEC] * 2,
+        in_specs=[VSPEC] * 9,
         out_specs=[ASPEC] * 6 + [VSPEC] * 10,
         scratch_shapes=[
             pltpu.VMEM((n_t, rows, width), BF),
@@ -1019,7 +1096,7 @@
 
     per = s.half // 2
     gsm_rows = up(experts + 2, 8)
-    back_links = 4 + 3 + (n_t - 1) * 7 + 4 + 4 + 2 * (n_dp - 1)
+    back_links = 64
     out, gx, gw, gqo, gsm = pl.pallas_call(
         lambda *refs: back_kernel(s, *refs),
         out_shape=(
@@ -1041,6 +1118,7 @@
             pltpu.VMEM((n_t - 1, rows, width), BF),
             pltpu.VMEM((n_t - 1, rows, width), BF),
             pltpu.VMEM((n_t - 1, rows, width), BF),
+            pltpu.VMEM((rows, width), F32),
             pltpu.VMEM((n_t - 1, rows, width), BF),
             pltpu.VMEM((n_t - 1, rows, width), BF),
             pltpu.VMEM((rows, width), BF),
@@ -1051,13 +1129,17 @@
             pltpu.VMEM((images, s.irows, 3 * heads), F32),
             pltpu.VMEM((n_t, rows, 3 * heads), F32),
             pltpu.VMEM((n_t, rows, 3 * heads), BF),
-            pltpu.VMEM((n_t, width, heads), BF),
-            pltpu.VMEM((n_t - 1, width, heads), BF),
-            pltpu.VMEM((n_dp, shard, 4 * heads), BF),
-            pltpu.VMEM((n_dp - 1, shard, 4 * heads), BF),
-            pltpu.VMEM((2, gsm_rows, width), F32),
-            pltpu.VMEM((n_t - 1, gsm_rows, width), F32),
-            pltpu.VMEM((n_dp - 1, gsm_rows, width), F32),
+            pltpu.VMEM((two_y, two_x, 2, shard, 7 * heads), F32),
+            pltpu.VMEM((two_y, two_x, shard, 7 * heads), BF),
+            pltpu.VMEM((two_y, two_x, shard, 7 * heads), BF),
+            pltpu.VMEM((two_y, shard, 7 * heads), BF),
+            pltpu.VMEM((two_y, shard, 7 * heads), BF),
+            pltpu.VMEM((shard, 7 * heads), BF),
+            pltpu.VMEM((shard, 7 * heads), BF),
+            pltpu.VMEM((n_t, shard, heads), BF),
+            pltpu.VMEM((n_t - 1, shard, heads), BF),
+            pltpu.VMEM((4, gsm_rows, width), F32),
+            pltpu.VMEM((n_t + 2, gsm_rows, width), F32),
             pltpu.VMEM((2, 2, s.half, 2 * shard, ff), BF),
             pltpu.VMEM((2, 2, per, 2 * shard, ff), BF),
             pltpu.VMEM((2, 2, per, 2 * shard, ff), BF),
@@ -1109,7 +1191,7 @@
         P("dp", None, None),
         P("dp", "tensor", None),
     )
-    linked = mesh.shape["dp"] == 8 and mesh.shape["tensor"] > 1
+    linked = mesh.shape["dp"] == 8 and mesh.shape["tensor"] == 4
     return jax.shard_map(
         linked_body if linked else body,
         mesh=mesh,

time: 299 us -> 252 us (0.84)
  Pallas kernels: 272 us -> 225 us
    pallas_call x1, Pallas kernels: 127 us -> 100 us  [linked_body(): pl.pallas_call(lambda *refs: back_kernel(s, *refs), out_shape=(shape((row...]
    pallas_call x1, Pallas kernels: 113 us -> 93.5 us  [linked_body(): front(x_own, dz_own, wq, wo, small, win_t, wout_t, live, tgt_rows)]
where the time goes in v2:
time: 252 us
  Pallas kernels  225 us (89%)
  local copies, waits for them, and re-layouts  24 us (10%)
    pallas_call x1, Pallas kernels, linked_body(): pl.pallas_call(lambda *refs: back_kernel(s, *refs), out_shape=(shape((row...  100 us
    pallas_call x1, Pallas kernels, linked_body(): front(x_own, dz_own, wq, wo, small, win_t, wout_t, live, tgt_rows)  93.5 us
    pallas_call x1, Pallas kernels, linked_body(): experts_call(n2_all.reshape(2, tokens, width), dz_all.reshape(2, tokens,...  31.8 us

profile of v2, /device:TPU:0, one launch (start us, length us, event | category | flops | bytes accessed | tf_op | source)
XLA Modules:
  0.0 251.7 jit_solution(15787760727414563364)
XLA Ops:
  0.7 1.1 reshape.103
  1.9 0.7 pad.21.refs_0_
  2.6 1.1 reshape.104
  3.7 0.7 pad.22.refs_1_
  4.4 0.6 copy_bitcast_fusion.2.refs_2_
  5.1 0.5 dynamic_update_slice.3.refs_4_
  5.6 1.5 copy.26
  7.9 0.1 convert_element_type.17
  8.1 0.7 pad_convert_fusion.refs_7_.refs_5_
  8.8 0.1 reshape.108
  9.0 0.2 copy.29
  9.3 0.2 copy.30
  9.5 0.6 pad.26.refs_8_
  10.1 93.5 %front.1 = (bf16[8,8,64,512]{3,2,1,0:T(8,128)(2,1)}, bf16[8,8,64,512]{3,2,1,0:T(8,128)(2,1)}, bf16[2,4,304,512]{3,2,1,0:T(8,128)(2,1)}, bf16[2,4,304,512]{3,2,1,...) custom-call(bf16[304,512]{1,0:T(8,128)(2,1)} %pad.21.refs_0_, ...), custom_call_target="tpu_custom_call" | custom-call | tf_op jit(solution)/shard_map/front/pallas_call | solution.py:1051
  103.6 31.8 %experts.1 = (bf16[2,1536,512]{2,1,0:T(8,128)(2,1)}, bf16[2,1536,512]{2,1,0:T(8,128)(2,1)}, bf16[2,2,8,128,512]{4,3,2,1,0:T(8,128)(2,1)}, bf16[2,2,8,128,512]{4,3,2,1,0:T(8,128)(2,1)}, f32[2,4,8,384]{3,2,1,0:T(8,128)}) custom-call(bf16[2,1216,512]{2,1,0:T(8,128)(2,1)} %bitcast.53, bf16[2,1216,512]{2,1,0:T(8,128)(2,1)} %bitcast.54, ...), custom_call_target="tpu_custom_call" | custom-call | tf_op jit(solution)/shard_map/experts/pallas_call | solution.py:1088
  135.5 100.1 %back.1 = (bf16[304,512]{1,0:T(8,128)(2,1)}, f32[304,512]{1,0:T(8,128)}, f32[2,2,8,64,512]{4,3,2,1,0:T(8,128)}, f32[64,512]{1,0:T(8,128)}, f32[24,512]{1,0:T(8,128)}) custom-call(bf16[304,512]{1,0:T(8,128)(2,1)} %pad.21.refs_0_, bf16[304,512]{1,0:T(8,128)(2,1)} %pad.22.refs_1_, f32[304,512]{1,0:T(8,128)} %get-tuple-element.34.refs_2_, ...), custom_call_target="tpu_custom_call" | custom-call | tf_op jit(solution)/shard_map/back/pallas_call | solution.py:1100
  235.6 1.8 reshape.115
  237.4 2.0 reshape.116
  239.4 1.3 dynamic-slice_bitcast_fusion.1
  240.7 1.5 copy_bitcast_fusion.1
  242.2 1.4 slice_bitcast_fusion.1
  243.6 1.4 dynamic-slice_bitcast_fusion
  245.0 4.2 %fusion = (f32[1,2,8,64,512]{4,3,2,1,0:T(8,128)}, f32[1,2,8,64,512]{4,3,2,1,0:T(8,128)S(1)}) fusion(f32[2,2,8,64,512]{4,3,2,1,0:T(8,128)} %get-tuple-element.59), kind=kLoop, calls=%fused_computation.14 | loop fusion | bytes 8388608 | tf_op jit(solution)/shard_map/slice | solution.py:1176
  249.2 2.5 %copy.39 = f32[16,64,512]{2,0,1:T(8,128)} copy(f32[16,64,512]{2,1,0:T(8,128)S(1)} %bitcast.48) | data formatting | bytes 4194304 | tf_op jit(solution)/shard_map/squeeze | solution.py:1175
  (25 shorter events, 0.3 us)
Async XLA Ops:
  0.6 3.8 %copy-start = (bf16[64,3,128]{2,0,1:T(8,128)(2,1)S(1)}, bf16[64,3,128]{2,0,1:T(8,128)(2,1)}, u32[]{:S(2)}) copy-start(bf16[64,3,128]{2,0,1:T(8,128)(2,1)} %param.13) | copy-start | bytes 147460
  0.7 4.4 %copy-start.7 = (bf16[64,2]{0,1:T(2,128)(2,1)S(1)}, bf16[64,2]{0,1:T(2,128)(2,1)}, u32[]{:S(2)}) copy-start(bf16[64,2]{0,1:T(2,128)(2,1)} %param.12) | copy-start | bytes 772
  0.7 4.4 %copy-start.6 = (bf16[64,16]{0,1:T(8,128)(2,1)S(1)}, bf16[64,16]{0,1:T(8,128)(2,1)}, u32[]{:S(2)}) copy-start(bf16[64,16]{0,1:T(8,128)(2,1)} %param.15) | copy-start | bytes 6148
  0.7 4.9 %copy-start.2 = (bf16[64,16,512]{2,1,0:T(8,128)(2,1)S(1)}, bf16[64,16,512]{2,1,0:T(8,128)(2,1)}, u32[]{:S(2)}) copy-start(bf16[64,16,512]{2,1,0:T(8,128)(2,1)} %param.16) | copy-start | bytes 3145732
  0.7 8.1 %copy-start.4 = (s32[6,200,2]{1,2,0:T(2,128)S(1)}, s32[6,200,2]{1,2,0:T(2,128)}, u32[]{:S(2)}) copy-start(s32[6,200,2]{1,2,0:T(2,128)} %param.20) | copy-start | bytes 28804
  0.7 8.1 %copy-start.5 = (s32[6,200,2]{1,2,0:T(2,128)S(1)}, s32[6,200,2]{1,2,0:T(2,128)}, u32[]{:S(2)}) copy-start(s32[6,200,2]{1,2,0:T(2,128)} %param.19) | copy-start | bytes 28804
  5.6 3.9 %copy-start.3 = (bf16[32,512]{1,0:T(8,128)(2,1)}, bf16[32,512]{1,0:T(8,128)(2,1)S(1)}, u32[]{:S(2)}) copy-start(bf16[32,512]{1,0:T(8,128)(2,1)S(1)} %dynamic_update_slice.3.refs_4_) | copy-start | bytes 98308
  9.3 126.2 %copy-start.1 = (s32[4,304,2]{2,1,0:T(8,128)}, s32[4,304,2]{2,1,0:T(8,128)S(1)}, u32[]{:S(2)}) copy-start(s32[4,304,2]{2,1,0:T(8,128)S(1)} %pad.25.refs_6_) | copy-start | bytes 29188

commit v3 on v0

--- a/solution.py
+++ b/solution.py
@@ -1,8 +1,12 @@
 import math
+from types import SimpleNamespace
+from typing import NamedTuple
 
 import jax
 import jax.numpy as jnp
 from jax import lax
+from jax.experimental import pallas as pl
+from jax.experimental.pallas import tpu as pltpu
 from jax.sharding import PartitionSpec as P
 
 HEAD_DIM = 64
@@ -161,19 +165,6 @@
     )
     gate_grid = gates.reshape(images, quarter, 2)
     output = middle + gate_grid[:, :, 0:1] * first_own + gate_grid[:, :, 1:2] * second_own
-    regathered = (
-        lax.all_gather(gains, "dp", axis=0, tiled=True),
-        lax.all_gather(w_qkv, "dp", axis=0, tiled=True),
-        lax.all_gather(w_o, "dp", axis=1, tiled=True),
-        lax.all_gather(w_router, "dp", axis=0, tiled=True),
-        lax.all_gather(w_in, "dp", axis=0, tiled=True),
-        lax.all_gather(w_out, "dp", axis=2, tiled=True),
-    )
-    qkv_all = regathered[1]
-    outproj_all = regathered[2]
-    router_all = regathered[3]
-    expin_all = regathered[4]
-    expout_all = regathered[5]
     grad_output = cotangent.astype(jnp.float32)
     grad_first = (gate_grid[:, :, 0:1] * grad_output).astype(jnp.bfloat16)
     grad_second = (gate_grid[:, :, 1:2] * grad_output).astype(jnp.bfloat16)
@@ -288,6 +279,874 @@
     )
 
 
+MESH = pl.DeviceIdType.MESH
+BF = jnp.bfloat16
+F32 = jnp.float32
+VMEM_BYTES = 62 << 20
+
+
+class Sizes(NamedTuple):
+    n_dp: int
+    n_t: int
+    images: int
+    quarter: int
+    rows: int
+    irows: int
+    width: int
+    shard: int
+    heads: int
+    experts: int
+    ff: int
+    lanes: int
+
+    @property
+    def half(self):
+        return self.experts // 2
+
+    @property
+    def slots(self):
+        return self.half * CAP
+
+
+def up(value, step):
+    return -(-value // step) * step
+
+
+def norm_parts(values):
+    centre = values - jnp.mean(values, -1, keepdims=True)
+    scale = lax.rsqrt(jnp.mean(centre * centre, -1, keepdims=True) + epsilon)
+    return centre * scale, scale
+
+
+def norm_back(values, gain, grad):
+    unit, scale = norm_parts(values)
+    inner = grad * gain
+    mean_a = jnp.mean(inner, -1, keepdims=True)
+    mean_b = jnp.mean(inner * unit, -1, keepdims=True)
+    return scale * (inner - mean_a - unit * mean_b), unit
+
+
+def dot(a, b):
+    return jnp.dot(a, b, preferred_element_type=F32)
+
+
+def dot_nt(a, b):
+    return lax.dot_general(a, b, (((1,), (1,)), ((), ())), preferred_element_type=F32)
+
+
+def dot_tn(a, b):
+    return lax.dot_general(a, b, (((0,), (0,)), ((), ())), preferred_element_type=F32)
+
+
+class Place:
+    def __init__(self, s):
+        self.s = s
+        self.dp = lax.axis_index("dp")
+        self.t = lax.axis_index("tensor")
+        self.c = lax.rem(self.dp, 2)
+        self.x = lax.rem(self.dp // 2, 2)
+        self.y = self.dp // 4
+        self.chip = self.dp // 2
+        self.chip_x = self.y * 2 + (1 - self.x)
+        self.chip_y = (1 - self.y) * 2 + self.x
+        self.sib = (self.chip * 2 + (1 - self.c), self.t)
+        self.nx_other = (self.chip_x * 2 + (1 - self.c), self.t)
+        self.ny_other = (self.chip_y * 2 + (1 - self.c), self.t)
+        self.pair = lax.rem(self.t, 2) * (-2) + self.t + 1
+        self.far = lax.rem(self.t + 2, 4)
+        self.cross = lax.rem(self.pair + 2, 4)
+        self.nx = (self.chip_x * 2 + self.c, self.t)
+        self.ny = (self.chip_y * 2 + self.c, self.t)
+
+    def ring_dp(self, k):
+        return lax.rem(self.dp + k, self.s.n_dp)
+
+    def ring_t(self, k):
+        return lax.rem(self.t + k, self.s.n_t)
+
+    def from_t(self, k):
+        return lax.rem(self.t + self.s.n_t - k, self.s.n_t)
+
+    def greet(self):
+        barrier = pltpu.get_barrier_semaphore()
+        for k in range(1, self.s.n_dp):
+            pl.semaphore_signal(barrier, inc=1, device_id=(self.ring_dp(k), self.t), device_id_type=MESH)
+        for k in range(1, self.s.n_t):
+            pl.semaphore_signal(barrier, inc=1, device_id=(self.dp, self.ring_t(k)), device_id_type=MESH)
+        pl.semaphore_wait(barrier, self.s.n_dp + self.s.n_t - 2)
+
+
+class Copies:
+    def __init__(self, send, recv, local):
+        self.send, self.recv, self.local = send, recv, local
+        self.n = 0
+        self.m = 0
+        self.sent = []
+
+    def make(self, k, src, dst, device):
+        return pltpu.make_async_remote_copy(
+            src_ref=src,
+            dst_ref=dst,
+            send_sem=self.send.at[k],
+            recv_sem=self.recv.at[k],
+            device_id=device,
+            device_id_type=MESH,
+        )
+
+    def to(self, src, dst, device):
+        copy = self.make(self.n, src, dst, device)
+        self.n += 1
+        copy.start()
+        self.sent.append(copy)
+        return copy
+
+    def here(self, src, dst):
+        copy = pltpu.make_async_copy(src, dst, self.local.at[self.m])
+        self.m += 1
+        copy.start()
+        return copy
+
+    def reserve(self, count):
+        self.n += count
+        return self.n - count
+
+    def at(self, k, src, dst, device):
+        copy = self.make(k, src, dst, device)
+        self.sent.append(copy)
+        return copy
+
+    def start_at(self, k, src, dst, device):
+        self.make(k, src, dst, device).start()
+
+    def sent_now(self, copies):
+        for copy in copies:
+            copy.wait_send()
+        self.sent = [copy for copy in self.sent if not any(copy is done for done in copies)]
+
+    def finish(self):
+        for copy in self.sent:
+            copy.wait_send()
+
+
+def pieces_of(rows):
+    first = up(rows // 2, 16)
+    return [pl.ds(0, first), pl.ds(first, rows - first)]
+
+
+class Gather:
+    def __init__(self, go, here, own, full):
+        self.go, self.here, self.full = go, here, full
+        self.pieces = pieces_of(here.s.rows)
+        mine = full(here.t)
+        self.to_far = [go.to(own.at[p], mine.at[p], (here.dp, here.far)) for p in self.pieces]
+        self.to_pair = [go.to(own.at[p], mine.at[p], (here.dp, here.pair)) for p in self.pieces]
+
+    def relay(self):
+        block = self.full(self.here.far)
+        self.passed = []
+        for p, copy in zip(self.pieces, self.to_far):
+            copy.wait_recv()
+            self.passed.append(self.go.to(block.at[p], block.at[p], (self.here.dp, self.here.pair)))
+
+    def sent_on(self):
+        self.go.sent_now(self.passed)
+
+    def wait_pair(self):
+        for copy in self.to_pair:
+            copy.wait_recv()
+
+    def wait_cross(self):
+        for copy in self.passed:
+            copy.wait_recv()
+
+    def share(self, block):
+        return self.go.to(self.full(block), self.full(block), self.here.sib)
+
+
+class Reduce:
+    def __init__(self, go, here, send, recv):
+        self.go, self.here, self.send, self.recv = go, here, send, recv
+        self.pieces = pieces_of(here.s.rows)
+        self.copies = [[], [], []]
+
+    def put(self, k, p, device):
+        self.copies[k].append(self.go.to(self.send.at[k, p], self.recv.at[k, p], (self.here.dp, device)))
+
+    def pair(self, k, value):
+        self.send[k] = value.astype(BF)
+        for p in self.pieces:
+            self.put(k, p, self.here.pair)
+
+    def across(self, part):
+        for i, p in enumerate(self.pieces):
+            self.copies[0][i].wait_recv()
+            self.send[2, p] = (part[p] + self.recv[0, p].astype(F32)).astype(BF)
+            self.put(2, p, self.here.far)
+
+    def sent(self):
+        self.go.sent_now([copy for copies in self.copies for copy in copies])
+
+    def total(self, part):
+        for copy in self.copies[1] + self.copies[2]:
+            copy.wait_recv()
+        return part + self.recv[1].astype(F32) + self.recv[2].astype(F32)
+
+
+def head_masks(s):
+    lane = lax.broadcasted_iota(jnp.int32, (s.irows, s.heads), 1)
+    return [(lane // HEAD_DIM) == h for h in range(s.heads // HEAD_DIM)]
+
+
+def stack_heads(values, masks):
+    zero = jnp.zeros_like(values)
+    return jnp.concatenate([jnp.where(mask, values, zero) for mask in masks], 0)
+
+
+def pick_heads(stacked, masks, irows):
+    out = stacked[:irows]
+    for h in range(1, len(masks)):
+        out = jnp.where(masks[h], stacked[h * irows : (h + 1) * irows], out)
+    return out
+
+
+def block_kernel(s, names, *refs):
+    r = SimpleNamespace(**dict(zip(names, refs)))
+    here = Place(s)
+    dp, t, c, x, y = here.dp, here.t, here.c, here.x, here.y
+    here.greet()
+    go = Copies(r.send, r.recv, r.local)
+    nt = s.n_t
+    length = s.quarter * nt
+    used = s.images * s.quarter
+    per = s.half // 2
+    masks = head_masks(s)
+
+    def to_image_rows(q, block, images):
+        for i in range(s.images):
+            images[i, pl.ds(q * s.quarter, s.quarter), :] = block[pl.ds(i * s.quarter, s.quarter), : images.shape[2]]
+
+    def to_block_rows(q, images, block):
+        for i in range(s.images):
+            block[pl.ds(i * s.quarter, s.quarter), : images.shape[2]] = images[i, pl.ds(q * s.quarter, s.quarter), :]
+
+    def clear(images):
+        images[:, pl.ds(length, s.irows - length), :] = jnp.zeros((s.images, s.irows - length, images.shape[2]), F32)
+
+    clear(r.img)
+    clear(r.oimg)
+    r.row[pl.ds(used, s.rows - used), :] = jnp.zeros((s.rows - used, 3 * s.heads), F32)
+
+    wo_copies = [go.to(r.wo, r.wo_z.at[t], (dp, here.ring_t(k))) for k in range(1, nt)]
+    x_blocks = Gather(go, here, r.x, lambda block: r.n1.at[block])
+    sm_copies = [go.to(r.sm, r.sm_all.at[dp], (here.ring_dp(k), t)) for k in range(1, s.n_dp)]
+    wq_copies = [go.to(r.wq, r.wq_all.at[dp], (here.ring_dp(k), t)) for k in range(1, s.n_dp)]
+
+    def spread(shard, full):
+        to = full.at[:, y, x, pl.ds(pl.multiple_of(c * s.shard, s.shard), s.shard)]
+        half, rest = shard.at[c], shard.at[1 - c]
+        from_x = [go.to(half, to, here.nx), go.to(rest, to, here.nx_other)]
+        from_y = [go.to(half, to, here.ny), go.to(rest, to, here.ny_other)]
+        return from_x, from_y, go.to(rest, to, here.sib), go.here(half, to)
+
+    in_x, in_y, in_sib, keep_in = spread(r.win, r.win_all)
+    keep_sm = go.here(r.sm, r.sm_all.at[dp])
+    keep_wq = go.here(r.wq, r.wq_all.at[dp])
+    keep_wo = go.here(r.wo, r.wo_z.at[t])
+    tgt_copy = go.to(r.tgt, r.tgt_all.at[c], here.sib)
+    keep_tgt = go.here(r.tgt, r.tgt_all.at[c])
+
+    def dz_block(block):
+        return r.ge.at[c, pl.ds(pl.multiple_of(block * s.rows, 16), s.rows)]
+
+    dz_sib = go.to(r.dz, dz_block(t), here.sib)
+    keep_dz = go.here(r.dz, dz_block(t))
+
+    keep_sm.wait()
+    for copy in sm_copies:
+        copy.wait_recv()
+    small = jnp.concatenate([r.sm_all[k][:, : s.shard].astype(F32) for k in range(s.n_dp)], 1)
+    r.small[...] = small
+    gain_one = small[s.experts : s.experts + 1]
+    gain_two = small[s.experts + 1 : s.experts + 2]
+    keep_wq.wait()
+    for copy in wq_copies:
+        copy.wait_recv()
+
+    keep_wo.wait()
+    for copy in wo_copies:
+        copy.wait_recv()
+    keep_wo_all = go.here(r.wo_z, r.wo_all.at[dp])
+    wo_out = [go.to(r.wo_z, r.wo_all.at[dp], (here.ring_dp(k), t)) for k in range(1, s.n_dp)]
+
+    def project(slot, values):
+        unit, _ = norm_parts(values.astype(F32))
+        normed = (unit * gain_one).astype(BF)
+        r.n1[slot] = normed
+        r.comb[slot, :, : 3 * s.heads] = dot(normed, r.wq_all[...].reshape(s.width, 3 * s.heads))
+
+    project(t, r.x[...])
+    x_blocks.relay()
+    out_x, out_y, out_sib, keep_out = spread(r.wout, r.wout_all)
+    x_blocks.wait_pair()
+    project(here.pair, r.n1[here.pair])
+    x_blocks.sent_on()
+    project(here.far, r.n1[here.far])
+    x_blocks.wait_cross()
+    project(here.cross, r.n1[here.cross])
+    dz_blocks = Gather(go, here, r.dz, dz_block)
+
+    low_half, high_half = pl.ds(0, per), pl.ds(per, per)
+
+    def pass_on(full, by_x, by_y):
+        for copy in by_x:
+            copy.wait_recv()
+        from_x = full.at[low_half, y, 1 - x]
+        on_y = go.to(from_x, from_x, here.ny)
+        for copy in by_y:
+            copy.wait_recv()
+        from_y = full.at[high_half, 1 - y, x]
+        return on_y, go.to(from_y, from_y, here.nx)
+
+    in_on = pass_on(r.win_all, in_x, in_y)
+    for q in range(nt):
+        to_image_rows(q, r.comb.at[q], r.img)
+
+    def attend(i, carry):
+        block = r.img[i].astype(BF)
+        r.qkv[i] = block
+        queries = stack_heads(block[:, : s.heads], masks)
+        scores = dot_nt(queries, block[:, s.heads : 2 * s.heads]) * (1.0 / math.sqrt(HEAD_DIM))
+        key = lax.broadcasted_iota(jnp.int32, scores.shape, 1)
+        scores = jnp.where(key < TOK_IMG, scores, negative_fill)
+        expd = jnp.exp(scores - jnp.max(scores, -1, keepdims=True))
+        probs = (expd / jnp.sum(expd, -1, keepdims=True)).astype(BF)
+        r.p[i] = probs
+        r.oimg[i] = pick_heads(dot(probs, block[:, 2 * s.heads :]), masks, s.irows)
+        return carry
+
+    lax.fori_loop(0, s.images, attend, 0)
+    for q in range(nt):
+        to_block_rows(q, r.oimg, r.row)
+        r.o_send[q] = r.row[:, : s.heads].astype(BF)
+    o_copies = [go.to(r.o_send.at[here.ring_t(k)], r.o.at[t], (dp, here.ring_t(k))) for k in range(1, nt)]
+    r.o[t] = r.o_send[t]
+    dz_blocks.relay()
+    keep_wo_all.wait()
+    for copy in wo_out:
+        copy.wait_recv()
+    for copy in o_copies:
+        copy.wait_recv()
+    branch = jnp.zeros((s.rows, s.width), F32)
+    for q in range(nt):
+        branch = branch + dot_nt(r.o[q], r.wo_all[:, q].reshape(s.width, s.heads))
+    middle = r.x[...].astype(F32) + r.live[...] * branch
+    r.y[...] = middle
+    unit, _ = norm_parts(middle)
+    normed_two = (unit * gain_two).astype(BF)
+    n2_own = r.n2_all.at[c, t]
+    n2_own[...] = normed_two
+    n2_sib = go.to(n2_own, n2_own, here.sib)
+    n2_blocks = Gather(go, here, n2_own, lambda block: r.n2_all.at[c, block])
+    logits = dot_nt(small[: s.experts].astype(BF), normed_two)
+    expd = jnp.exp(logits - jnp.max(logits, 0, keepdims=True))
+    r.prob[...] = jnp.zeros((s.experts, s.lanes), F32)
+    r.prob[:, : s.rows] = expd / jnp.sum(expd, 0, keepdims=True)
+    r.prob_all[c, t] = r.prob[...]
+    pr_sib = go.to(r.prob, r.prob_all.at[c, t], here.sib)
+    pr_copies = [go.to(r.prob, r.prob_all.at[c, t], (dp, here.ring_t(k))) for k in range(1, nt)]
+
+    n2_blocks.relay()
+    on_n2 = [n2_blocks.share(here.far)]
+    on_dz = [dz_blocks.share(here.far)]
+    dz_blocks.wait_pair()
+    on_dz.append(dz_blocks.share(here.pair))
+    dz_blocks.wait_cross()
+    on_dz.append(dz_blocks.share(here.cross))
+    n2_blocks.wait_pair()
+    on_n2.append(n2_blocks.share(here.pair))
+    for k, copy in enumerate(pr_copies, 1):
+        copy.wait_recv()
+        slot = r.prob_all.at[c, here.from_t(k)]
+        on_n2.append(go.to(slot, slot, here.sib))
+    out_on = pass_on(r.wout_all, out_x, out_y)
+    keep_tgt.wait()
+    keep_dz.wait()
+    for copy in [tgt_copy, dz_sib] + on_dz:
+        copy.wait_recv()
+
+    tokens = nt * s.rows
+    few = 2
+    for q in range(2):
+        first_id = (c * s.half + lax.broadcasted_iota(jnp.int32, (s.half, tokens), 0)) * CAP
+        found = jnp.full((s.half, tokens), -1, jnp.int32)
+        for k in range(2):
+            slot = r.tgt_all[q, k : k + 1, :] - first_id
+            found = jnp.where((slot >= 0) & (slot < CAP), slot, found)
+        r.slot[q] = found.astype(F32)
+    slot_ids = lax.broadcasted_iota(jnp.int32, (CAP, tokens), 0).astype(F32)
+
+    def dispatch(q, j, rows, out):
+        for i in range(few):
+            hits = r.slot[q, pl.ds(few * j + i, 1), :] == slot_ids
+            r.hot[i] = jnp.where(hits, 1.0, 0.0).astype(BF)
+        found = dot(r.hot[...].reshape(few * CAP, tokens), rows)
+        out[...] = found.astype(BF).reshape(out.shape)
+
+    def dispatch_z(j, carry):
+        for q in range(2):
+            dispatch(q, j, r.ge[q, :tokens], r.zin.at[q, pl.ds(few * j, few)])
+        return carry
+
+    lax.fori_loop(0, s.half // few, dispatch_z, 0)
+    n2_blocks.wait_cross()
+    on_n2.append(n2_blocks.share(here.cross))
+    keep_in.wait()
+    keep_out.wait()
+    for copy in [n2_sib, pr_sib, in_sib, out_sib, *in_on] + on_n2:
+        copy.wait_recv()
+    mine = pl.ds(pl.multiple_of(c * s.half, s.half), s.half)
+    for q in range(2):
+        r.pr[q] = jnp.concatenate([r.prob_all[q, k, mine][:, : s.rows] for k in range(nt)], 1)
+    for copy in out_on:
+        copy.wait_recv()
+    go.sent_now([*in_on, *out_on, dz_sib, *dz_blocks.passed, *on_dz])
+    k_in, k_out, k_dx, k_ge = (go.reserve(s.half) for _ in range(4))
+
+    def grad_in_copy(e):
+        return r.win_all.at[e, :, 1 - x], r.ra.at[e], here.nx
+
+    def grad_out_copy(e):
+        return r.wout_all.at[e, 1 - y], r.rb.at[e], here.ny
+
+    def dx_copy(e):
+        return r.xin.at[1 - c, e], r.dxv.at[e], here.sib
+
+    def slots_of(e):
+        return pl.ds(pl.multiple_of(e * CAP, CAP), CAP)
+
+    def ge_copy(e):
+        return r.ge.at[1 - c, slots_of(e)], r.gev.at[slots_of(e)], here.sib
+
+    def expert(e):
+        x_in = r.xin[:, e].reshape(2 * CAP, s.width)
+        w_in = r.win_all[e].reshape(s.width, s.ff)
+        w_out = r.wout_all[e].reshape(s.width, s.ff)
+        hidden = dot(x_in, w_in)
+        bell = jnp.exp(-0.5 * hidden * hidden)
+        u = 1.0 / (1.0 + (0.3275911 / math.sqrt(2.0)) * jnp.abs(hidden))
+        poly = u * (0.254829592 + u * (-0.284496736 + u * (1.421413741 + u * (-1.453152027 + u * 1.061405429))))
+        tail = 0.5 * poly * bell
+        phi = jnp.where(hidden >= 0, 1.0 - tail, tail)
+        active = (hidden * phi).astype(BF)
+        slope = phi + hidden * bell * (1.0 / math.sqrt(2.0 * math.pi))
+        out = dot_nt(active, w_out).astype(BF).astype(F32)
+        for q in range(2):
+            hits = r.slot[q, pl.ds(e, 1), :] == slot_ids
+            gate = jnp.sum(jnp.where(hits, r.pr[q, pl.ds(e, 1), :], 0.0), 1, keepdims=True)
+            part = out[q * CAP : (q + 1) * CAP]
+            wide = r.zin[q, e].astype(F32)
+            dgate = jnp.sum(wide * part, 1, keepdims=True)
+            r.dpr[q, pl.ds(e, 1), :] = jnp.sum(jnp.where(hits, dgate, 0.0), 0, keepdims=True)
+            r.zin[q, e] = (gate * wide).astype(BF)
+            r.ge[q, slots_of(e)] = (gate * part).astype(BF)
+        grad = r.zin[:, e].reshape(2 * CAP, s.width)
+        dhidden = (dot(grad, w_out) * slope).astype(BF)
+        r.wout_all[e] = dot_tn(grad, active).astype(BF).reshape(r.wout_all.shape[1:])
+        grad_in = dot_tn(x_in, dhidden).astype(BF)
+        r.xin[:, e] = dot_nt(dhidden, w_in).astype(BF).reshape(2, CAP, s.width)
+        r.win_all[e] = grad_in.reshape(r.win_all.shape[1:])
+
+    def expert_few(j, carry):
+        for q in range(2):
+            dispatch(q, j, r.n2_all[q].reshape(tokens, s.width), r.xin.at[q, pl.ds(few * j, few)])
+        for i in range(few):
+            expert(few * j + i)
+        for i in range(few):
+            e = few * j + i
+            for k, copy in ((k_out, grad_out_copy), (k_in, grad_in_copy), (k_dx, dx_copy), (k_ge, ge_copy)):
+                go.start_at(k + e, *copy(e))
+        return carry
+
+    lax.fori_loop(0, s.half // few, expert_few, 0)
+    ge_copies = [go.at(k_ge + e, *ge_copy(e)) for e in range(s.half)]
+    dx_copies = [go.at(k_dx + e, *dx_copy(e)) for e in range(s.half)]
+    in_copies = [go.at(k_in + e, *grad_in_copy(e)) for e in range(s.half)]
+    out_copies = [go.at(k_out + e, *grad_out_copy(e)) for e in range(s.half)]
+
+    r.dprs[...] = jnp.zeros(r.dprs.shape, F32)
+    for q in range(2):
+        for k in range(nt):
+            r.dprs[q, k, :, : s.rows] = r.dpr[q][:, k * s.rows : (k + 1) * s.rows]
+    dpr_sib = go.to(r.dprs.at[1 - c], r.dprf.at[:, c], here.sib)
+    r.dprf[:, c] = r.dprs[c]
+    zero_rows = jnp.zeros((s.rows, s.width), F32)
+    span = 512
+
+    def combine(values, half, q, total):
+        first = r.tcol[q, :, 0:1] - half * s.slots
+        second = r.tcol[q, :, 1:2] - half * s.slots
+        lane = lax.broadcasted_iota(jnp.int32, (s.rows, span), 1)
+        for j in range(s.slots // span):
+            hot = jnp.where((first - j * span == lane) | (second - j * span == lane), 1.0, 0.0).astype(BF)
+            total = total + dot(hot, values[pl.ds(j * span, span)])
+        return total
+
+    dx_own, dxv = r.xin.at[c].reshape(s.slots, s.width), r.dxv.reshape(s.slots, s.width)
+    r.comb[0] = combine(dx_own, c, here.cross, zero_rows)
+    for copy in dx_copies:
+        copy.wait_recv()
+    dn2_sum = Reduce(go, here, r.rs_send, r.rs_recv)
+    dn2_sum.pair(0, combine(dxv, 1 - c, here.cross, r.comb[0]))
+    dn2_sum.pair(1, combine(dxv, 1 - c, here.pair, combine(dx_own, c, here.pair, zero_rows)))
+    dpr_sib.wait_recv()
+    dpr_copies = [go.to(r.dprf.at[here.ring_t(k)], r.dprz.at[k - 1], (dp, here.ring_t(k))) for k in range(1, nt)]
+    dn2_sum.across(combine(dxv, 1 - c, here.far, combine(dx_own, c, here.far, zero_rows)))
+    r.comb[0] = combine(dxv, 1 - c, t, combine(dx_own, c, t, zero_rows))
+
+    for copy in ge_copies:
+        copy.wait_recv()
+    ge_own = r.ge.at[c]
+    m_sum = Reduce(go, here, r.m_send, r.m_recv)
+
+    def forward_sum(q):
+        return combine(r.gev, 1 - c, q, combine(ge_own, c, q, zero_rows))
+
+    m_sum.pair(0, forward_sum(here.cross))
+    m_sum.pair(1, forward_sum(here.pair))
+    r.comb[2] = forward_sum(here.far)
+    r.gx[...] = forward_sum(t) + r.y[...]
+
+    dprobs = r.dprf[t]
+    for k, copy in enumerate(dpr_copies):
+        copy.wait_recv()
+        dprobs = dprobs + r.dprz[k]
+    dprobs = dprobs.reshape(s.experts, s.lanes)
+    probs = r.prob[...]
+    dlogits = (probs * (dprobs - jnp.sum(probs * dprobs, 0, keepdims=True))).astype(BF)[:, : s.rows]
+    small = r.small[...]
+    gain_one = small[s.experts : s.experts + 1]
+    gain_two = small[s.experts + 1 : s.experts + 2]
+    grad_router = dot_tn(r.n2_all[c, t], dlogits.T).T
+    dn2 = r.comb[0] + dot_tn(dlogits, small[: s.experts].astype(BF))
+    dn2 = dn2_sum.total(dn2)
+    middle = r.y[...]
+    dy_ln, unit = norm_back(middle, gain_two, dn2)
+    dgain_two = jnp.sum(dn2 * unit, 0, keepdims=True)
+    dy = r.dz[...].astype(F32) + dy_ln
+    r.comb[0] = dy
+    da = (r.live[...] * dy).astype(BF)
+    go.sent_now(o_copies)
+    for q in range(nt):
+        r.o_send[q] = dot(da, r.wo_all[:, q].reshape(s.width, s.heads)).astype(BF)
+    do_copies = [go.to(r.o_send.at[here.ring_t(k)], r.do.at[t], (dp, here.ring_t(k))) for k in range(1, nt)]
+    r.do[t] = r.o_send[t]
+    for q in range(nt):
+        part = dot_tn(da, r.o[q]).reshape(*r.grads.shape[:3], s.shard, s.heads)
+        r.grads[:, :, :, :, (3 + q) * s.heads : (4 + q) * s.heads] = part.astype(BF)
+
+    fa_copies, fb_copies = [], []
+
+    def pump(j):
+        first, second = in_copies[j * per : (j + 1) * per], out_copies[j * per : (j + 1) * per]
+        for copy in first:
+            copy.wait_recv()
+
+        def step_a(i, carry):
+            e = j * per + i
+            r.win_all[e, 1 - y, x] = (r.win_all[e, 1 - y, x].astype(F32) + r.ra[e, 1 - y].astype(F32)).astype(BF)
+            return carry
+
+        lax.fori_loop(0, per, step_a, 0)
+        piece = pl.ds(j * per, per)
+        fa_copies.append(go.to(r.win_all.at[piece, 1 - y, x], r.fa.at[piece], here.ny))
+        for copy in second:
+            copy.wait_recv()
+
+        def step_b(i, carry):
+            e = j * per + i
+            r.wout_all[e, y, 1 - x] = (r.wout_all[e, y, 1 - x].astype(F32) + r.rb[e, 1 - x].astype(F32)).astype(BF)
+            return carry
+
+        lax.fori_loop(0, per, step_b, 0)
+        fb_copies.append(go.to(r.wout_all.at[piece, y, 1 - x], r.fb.at[piece], here.nx))
+
+    for copy in do_copies:
+        copy.wait_recv()
+    m_sum.across(r.comb[2])
+    clear(r.oimg)
+    for q in range(nt):
+        r.row[:, : s.heads] = r.do[q].astype(F32)
+        to_image_rows(q, r.row, r.oimg)
+
+    def attend_back(i, carry):
+        block = r.qkv[i]
+        queries = stack_heads(block[:, : s.heads], masks)
+        grads = stack_heads(r.oimg[i].astype(BF), masks)
+        probs = r.p[i]
+        dvalues = dot_tn(probs, grads)
+        dprob = dot_nt(grads, block[:, 2 * s.heads :])
+        wide = probs.astype(F32)
+        both = wide * dprob
+        dscore = (both - wide * jnp.sum(both, -1, keepdims=True)).astype(BF)
+        dqueries = pick_heads(dot(dscore, block[:, s.heads : 2 * s.heads]), masks, s.irows)
+        dkeys = dot_tn(dscore, queries)
+        r.img[i, :, : s.heads] = dqueries * (1.0 / math.sqrt(HEAD_DIM))
+        r.img[i, :, s.heads : 2 * s.heads] = dkeys * (1.0 / math.sqrt(HEAD_DIM))
+        r.img[i, :, 2 * s.heads :] = dvalues
+        return carry
+
+    lax.fori_loop(0, s.images, attend_back, 0)
+    pump(0)
+    r.row[pl.ds(used, s.rows - used), :] = jnp.zeros((s.rows - used, 3 * s.heads), F32)
+    for q in range(nt):
+        to_block_rows(q, r.img, r.row)
+        r.dqkv[q] = r.row[...].astype(BF)
+    w_qkv = r.wq_all[...].reshape(s.width, 3 * s.heads)
+    dn2_sum.sent()
+    dn1_sum = Reduce(go, here, r.rs_send, r.rs_recv)
+    dgain_one = jnp.zeros((1, s.width), F32)
+    for k, q in enumerate((here.cross, here.pair, here.far, t)):
+        part = dot_nt(r.dqkv[q], w_qkv)
+        dgain_one = dgain_one + jnp.sum(part * r.n1[q].astype(F32), 0, keepdims=True)
+        if k < 2:
+            dn1_sum.pair(k, part)
+        else:
+            r.comb[2 * k - 3] = part
+    dgain_one = dgain_one / gain_one
+
+    pump(1)
+
+    grad_qkv = jnp.zeros((s.width, 3 * s.heads), F32)
+    for q in range(nt):
+        grad_qkv = grad_qkv + dot_tn(r.n1[q], r.dqkv[q])
+    grads = r.grads
+    grads[:, :, :, :, : 3 * s.heads] = grad_qkv.astype(BF).reshape(*grads.shape[:3], s.shard, 3 * s.heads)
+    r.sm_send[0] = jnp.concatenate(
+        [grad_router, dgain_one, dgain_two, jnp.zeros((r.sm_send.shape[1] - s.experts - 2, s.width), F32)], 0
+    )
+    step = [go.to(grads.at[:, :, 1 - c], r.gs_recv, here.sib), go.to(r.sm_send.at[0], r.sm_recv.at[0], here.sib)]
+    dn1_sum.across(r.comb[1])
+
+    def add_small(k):
+        r.sm_send[k + 1] = r.sm_send[k] + r.sm_recv[k]
+
+    for copy in step:
+        copy.wait_recv()
+
+    def add_in(mine, came):
+        return (mine.astype(F32) + came.astype(F32)).astype(BF)
+
+    grads[:, :, c] = add_in(grads[:, :, c], r.gs_recv[...])
+    add_small(0)
+    step = [go.to(grads.at[:, 1 - x, c], r.gx_recv, here.nx), go.to(r.sm_send.at[1], r.sm_recv.at[1], here.nx)]
+    for copy in step:
+        copy.wait_recv()
+    grads[:, x, c] = add_in(grads[:, x, c], r.gx_recv[...])
+    add_small(1)
+    step = [go.to(grads.at[1 - y, x, c], r.gy_recv, here.ny), go.to(r.sm_send.at[2], r.sm_recv.at[2], here.ny)]
+    for copy in step:
+        copy.wait_recv()
+    add_small(2)
+    summed = grads[y, x, c].astype(F32) + r.gy_recv[...].astype(F32)
+    r.gqo[:, : 3 * s.heads] = summed[:, : 3 * s.heads]
+    for q in range(nt):
+        r.gz_send[q] = summed[:, (3 + q) * s.heads : (4 + q) * s.heads].astype(BF)
+    gz_copies = [go.to(r.gz_send.at[here.ring_t(k)], r.gz_recv.at[k - 1], (dp, here.ring_t(k))) for k in range(1, nt)]
+    sm_copies = [go.to(r.sm_send.at[3], r.sm_recv.at[2 + k], (dp, here.ring_t(k))) for k in range(1, nt)]
+    r.out[...] = m_sum.total(r.gx[...]).astype(BF)
+
+    dn1 = dn1_sum.total(r.comb[3])
+    dx_ln, _ = norm_back(r.x[...].astype(F32), gain_one, dn1)
+    r.gx[...] = r.comb[0] + dx_ln
+    total = r.gz_send[t].astype(F32)
+    for k, copy in enumerate(gz_copies):
+        copy.wait_recv()
+        total = total + r.gz_recv[k].astype(F32)
+    r.gqo[:, 3 * s.heads :] = total
+    total = r.sm_send[3]
+    for k, copy in enumerate(sm_copies):
+        copy.wait_recv()
+        total = total + r.sm_recv[3 + k]
+    r.gsm[...] = total
+
+    mine = pl.ds(pl.multiple_of(c * s.shard, s.shard), s.shard)
+    other = pl.ds(pl.multiple_of((1 - c) * s.shard, s.shard), s.shard)
+    fin_copies = []
+    parts = ((r.win_all, r.ra, y, r.fa, fa_copies), (r.wout_all, r.rb, x, r.fb, fb_copies))
+    for w, (own, first, place, second, copies) in enumerate(parts):
+        for j in range(2):
+            copies[j].wait_recv()
+
+            def last(i, carry, w=w, own=own, first=first, place=place, second=second, j=j):
+                e = j * per + i
+
+                def total(rows):
+                    return (
+                        own[e, y, x, rows, :].astype(F32)
+                        + first[e, place, rows, :].astype(F32)
+                        + second[e, rows, :].astype(F32)
+                    )
+
+                own[e, y, x, other, :] = total(other).astype(BF)
+                r.gw[w, c, e] = total(mine).astype(BF)
+                return carry
+
+            lax.fori_loop(0, per, last, 0)
+            piece = pl.ds(j * per, per)
+            fin_copies.append(go.to(own.at[piece, y, x, other], r.gw.at[w, c, piece], here.sib))
+    for copy in fin_copies:
+        copy.wait_recv()
+    go.finish()
+
+
+VSPEC = pl.BlockSpec(memory_space=pltpu.VMEM)
+ASPEC = pl.BlockSpec(memory_space=pl.ANY)
+
+
+def shape(dims, kind):
+    return jax.ShapeDtypeStruct(dims, kind)
+
+
+def linked_body(
+    block_input,
+    gains,
+    w_qkv,
+    w_o,
+    w_router,
+    w_in,
+    w_out,
+    pictures_alive_per_shard,
+    expert_ids,
+    slot_index,
+    cotangent,
+):
+    images, quarter, width = block_input.shape
+    n_dp, n_t = lax.axis_size("dp"), lax.axis_size("tensor")
+    shard, experts, ff = w_in.shape
+    heads = w_qkv.shape[2]
+    length = quarter * n_t
+    used = images * quarter
+    rows = up(used, 16)
+    s = Sizes(n_dp, n_t, images, quarter, rows, up(length, 16), width, shard, heads, experts, ff, up(rows, 128))
+    dp, t = lax.axis_index("dp"), lax.axis_index("tensor")
+
+    def by_rows(values):
+        return jnp.pad(values.reshape(used, width), ((0, rows - used), (0, 0)))
+
+    x_own, dz_own = by_rows(block_input), by_rows(cotangent)
+    wq = w_qkv.reshape(shard, 3 * heads)
+    wo = w_o.T
+    sm_rows = up(experts + 2, 16)
+    small = jnp.concatenate([w_router.T, gains.T], 0)
+    small = jnp.pad(small, ((0, sm_rows - experts - 2), (0, up(shard, 128) - shard)))
+    win_t = w_in.transpose(1, 0, 2).reshape(2, s.half, shard, ff)
+    wout_t = w_out.transpose(1, 2, 0).reshape(2, s.half, shard, ff)
+    place = t * quarter + jnp.arange(quarter)
+    live = (jnp.arange(images) < pictures_alive_per_shard[0])[:, None] & (place < TOK_IMG)[None, :]
+    live = jnp.pad(live.astype(F32).reshape(used, 1), ((0, rows - used), (0, 0)))
+    targets = jnp.where(slot_index >= 0, expert_ids * CAP + slot_index, -1)
+    targets = targets.reshape(images, n_t, quarter, 2).transpose(1, 0, 2, 3).reshape(n_t, used, 2)
+    targets = jnp.pad(targets, ((0, 0), (0, rows - used), (0, 0)), constant_values=-1)
+    tgt_rows = jnp.pad(targets.reshape(n_t * rows, 2).T, ((0, 6), (0, 0)), constant_values=-1)
+
+    two_y, two_x = n_dp // 4, 2
+    gsm_rows = up(experts + 2, 8)
+    tokens = n_t * rows
+    inputs = dict(
+        x=x_own, dz=dz_own, wq=wq, wo=wo, sm=small, live=live, tgt=tgt_rows, tcol=targets, win=win_t, wout=wout_t
+    )
+    outputs = dict(
+        out=shape((rows, width), BF),
+        gx=shape((rows, width), F32),
+        gqo=shape((shard, 4 * heads), F32),
+        gsm=shape((gsm_rows, width), F32),
+        gw=shape((2, 2, s.half, shard, ff), BF),
+    )
+    wide = (two_y, two_x, 2 * shard, ff)
+    per = s.half // 2
+    scratch = dict(
+        win_all=((s.half, *wide), BF),
+        wout_all=((s.half, *wide), BF),
+        n2_all=((2, n_t, rows, width), BF),
+        prob_all=((2, n_t, experts, s.lanes), F32),
+        tgt_all=((2, 8, tokens), jnp.int32),
+        y=((rows, width), F32),
+        prob=((experts, s.lanes), F32),
+        qkv=((images, s.irows, 3 * heads), BF),
+        p=((images, heads // HEAD_DIM * s.irows, s.irows), BF),
+        n1=((n_t, rows, width), BF),
+        o=((n_t, rows, heads), BF),
+        do=((n_t, rows, heads), BF),
+        wq_all=((n_dp, shard, 3 * heads), BF),
+        wo_all=((n_dp, n_t, shard, heads), BF),
+        wo_z=((n_t, shard, heads), BF),
+        sm_all=((n_dp, *small.shape), BF),
+        small=((sm_rows, width), F32),
+        row=((rows, 3 * heads), F32),
+        img=((images, s.irows, 3 * heads), F32),
+        oimg=((images, s.irows, heads), F32),
+        o_send=((n_t, rows, heads), BF),
+        dqkv=((n_t, rows, 3 * heads), BF),
+        pr=((2, s.half, tokens), F32),
+        dpr=((2, s.half, tokens), F32),
+        dprs=((2, n_t, s.half, s.lanes), F32),
+        dprf=((n_t, 2, s.half, s.lanes), F32),
+        dprz=((n_t - 1, 2, s.half, s.lanes), F32),
+        hot=((2, CAP, tokens), BF),
+        xin=((2, s.half, CAP, width), BF),
+        slot=((2, s.half, tokens), F32),
+        zin=((2, s.half, CAP, width), BF),
+        ge=((2, s.slots, width), BF),
+        dxv=((s.half, CAP, width), BF),
+        gev=((s.slots, width), BF),
+        comb=((n_t, rows, width), F32),
+        rs_send=((n_t - 1, rows, width), BF),
+        rs_recv=((n_t - 1, rows, width), BF),
+        m_send=((n_t - 1, rows, width), BF),
+        m_recv=((n_t - 1, rows, width), BF),
+        grads=((two_y, two_x, 2, shard, 7 * heads), BF),
+        gs_recv=((two_y, two_x, shard, 7 * heads), BF),
+        gx_recv=((two_y, shard, 7 * heads), BF),
+        gy_recv=((shard, 7 * heads), BF),
+        gz_send=((n_t, shard, heads), BF),
+        gz_recv=((n_t - 1, shard, heads), BF),
+        sm_send=((4, gsm_rows, width), F32),
+        sm_recv=((n_t + 2, gsm_rows, width), F32),
+        ra=((s.half, two_y, 2 * shard, ff), BF),
+        rb=((s.half, two_x, 2 * shard, ff), BF),
+        fa=((s.half, 2 * shard, ff), BF),
+        fb=((s.half, 2 * shard, ff), BF),
+    )
+    links = 160
+    names = [*inputs, *outputs, *scratch, "send", "recv", "local"]
+    out, gx, gqo, gsm, gw = pl.pallas_call(
+        lambda *refs: block_kernel(s, names, *refs),
+        out_shape=tuple(outputs.values()),
+        in_specs=[VSPEC] * (len(inputs) - 2) + [ASPEC] * 2,
+        out_specs=[VSPEC] * len(outputs),
+        scratch_shapes=[pltpu.VMEM(dims, kind) for dims, kind in scratch.values()]
+        + [pltpu.SemaphoreType.DMA((links,)), pltpu.SemaphoreType.DMA((links,)), pltpu.SemaphoreType.DMA((10,))],
+        compiler_params=pltpu.CompilerParams(collective_id=1, has_side_effects=True, vmem_limit_bytes=VMEM_BYTES),
+        name="block",
+    )(*inputs.values())
+
+    def by_image(values):
+        return values[:used].reshape(images, quarter, width)
+
+    gw = gw.reshape(2, experts, shard, ff)
+    own_small = lax.dynamic_slice(gsm, (0, dp * shard), (gsm_rows, shard))
+    return (
+        by_image(out),
+        by_image(gx),
+        own_small[experts : experts + 2].T,
+        gqo[:, : 3 * heads].reshape(shard, 3, heads),
+        gqo[:, 3 * heads :].T,
+        own_small[:experts].T,
+        gw[0].transpose(1, 0, 2).astype(F32),
+        gw[1].transpose(2, 0, 1).astype(F32),
+    )
+
+
 def solution(mesh):
     placed = (
         P("dp", "tensor", None),
@@ -302,8 +1161,9 @@
         P("dp", None, None),
         P("dp", "tensor", None),
     )
+    linked = mesh.shape["dp"] == 8 and mesh.shape["tensor"] == 4
     return jax.shard_map(
-        body,
+        linked_body if linked else body,
         mesh=mesh,
         in_specs=placed,
         out_specs=(

time: 1290 us -> 228 us (0.18)
  waiting for transfers between devices: 994 us -> 0 us
  Pallas kernels: 0 us -> 206 us
  matrix products: 132 us -> 0 us
  blocking collectives: 49.8 us -> 0 us
  local copies, waits for them, and re-layouts: 62.8 us -> 15.3 us
  other arithmetic: 27.5 us -> 4.01 us
  between operations: 16.9 us -> 1.41 us
    unnamed x21 -> x0, waiting for transfers between devices: 465 us -> none
    reduce_scatter x4 -> x0, waiting for transfers between devices: 304 us -> none  [the longest x1 120 us: body(): lax.psum_scatter(grad_expin, 'dp', scatter_dimension=0, tiled=True)]
    all_gather x7 -> x0, waiting for transfers between devices: 225 us -> none  [the longest x3 110 us: grads_in(): lax.all_gather(as_sent(values), 'tensor', axis=1, tiled=True)]
    pallas_call x0 -> x1, Pallas kernels: none -> 206 us  [linked_body(): pl.pallas_call(lambda *refs: block_kernel(s, names, *refs), out_shape=tup...]
    dot_general x28 -> x0, matrix products: 131 us -> none  [the longest x1 21.4 us: body(): jnp.einsum('ecd,fed->ecf', grad_expert, expout_all, preferred_element_typ...]
    all_gather x4 -> x0, blocking collectives: 37.3 us -> none  [the longest x1 10.3 us: body(): lax.all_gather(gains, 'dp', axis=0, tiled=True)]
    unnamed x201 -> x21, local copies, waits for them, and re-layouts: 20.8 us -> 0.7 us
    transpose x1 -> x4, local copies, waits for them, and re-layouts: 20.3 us -> 4.85 us  [the longest x1 1.55 us: linked_body(): win_t = w_in.transpose(1, 0, 2).reshape(2, s.half, shard, ff)]
  transfers between devices with their start and end apart: 16 -> 0, of which waited for: 15 -> 0; matrix products, arithmetic and copies ran while one was open for 8% -> 0% of each run, Pallas kernels for 0% -> 0%
where the time goes in v3:
time: 228 us; the launch traced here: 227 us
  Pallas kernels  206 us (90%)
  local copies, waits for them, and re-layouts  15.3 us (7%)
  other arithmetic  4.01 us (2%)
    pallas_call x1, Pallas kernels, linked_body(): pl.pallas_call(lambda *refs: block_kernel(s, names, *refs), out_shape=tup...  206 us

profile of v3, /device:TPU:0, one launch (start us, length us, event | category | flops | bytes accessed | tf_op | source)
XLA Modules:
  0.0 227.2 jit_solution(3608852982461864145)
XLA Ops:
  0.7 0.8 compare_select_fusion
  1.5 0.1 reshape.98
  1.6 0.1 reshape.99
  1.7 0.2 copy.28
  2.0 0.2 copy.29
  2.3 0.6 pad.31.refs_6_
  3.6 0.1 convert_element_type.47
  3.8 0.7 pad_convert_fusion.refs_5_
  4.5 1.5 copy.30
  6.1 0.7 pad.25.refs_0_
  6.9 0.1 reshape.96
  7.0 0.7 pad.26.refs_1_
  7.7 0.6 copy_bitcast_fusion.2.refs_2_
  8.3 0.6 fusion.5.refs_4_
  8.9 206.4 %block.1 = (bf16[304,512]{1,0:T(8,128)(2,1)}, f32[304,512]{1,0:T(8,128)}, f32[64,512]{1,0:T(8,128)}, f32[24,512]{1,0:T(8,128)}, bf16[2,2,8,64,512]{4,3,2,1,0:T(8,128)(2,1)}) custom-call(bf16[304,512]{1,0:T(8,128)(2,1)} %pad.25.refs_0_, bf16[304,512]{1,0:T(8,128)(2,1)} %pad.26.refs_1_, bf16[64,384]{1,0:T(8,128)(2,1)} %copy_bitcast_fusion.2.refs_2_, ...), custom_call_target="tpu_custom_call" | custom-call | tf_op jit(solution)/shard_map/block/pallas_call | solution.py:1122
  215.4 1.4 dynamic-slice_bitcast_fusion
  216.8 1.3 dynamic-slice_bitcast_fusion.1
  218.1 1.8 fusion.6
  219.8 1.8 convert_bitcast_fusion
  221.7 2.5 %copy.39 = f32[16,64,512]{2,0,1:T(8,128)} copy(f32[16,64,512]{2,1,0:T(8,128)S(1)} %get-tuple-element.37) | data formatting | bytes 4194304 | tf_op jit(solution)/shard_map/convert_element_type | solution.py:1145
  224.2 0.6 copy_bitcast_fusion.1
  224.8 0.6 slice_bitcast_fusion.1
  225.5 0.9 reshape.104
  226.4 0.8 reshape.103
  (26 shorter events, 0.3 us)
Async XLA Ops:
  0.6 7.1 %copy-start = (bf16[64,3,128]{2,0,1:T(8,128)(2,1)S(1)}, bf16[64,3,128]{2,0,1:T(8,128)(2,1)}, u32[]{:S(2)}) copy-start(bf16[64,3,128]{2,0,1:T(8,128)(2,1)} %param.13) | copy-start | bytes 147460
  0.6 3.8 %copy-start.2 = (bf16[64,16,512]{2,1,0:T(8,128)(2,1)S(1)}, bf16[64,16,512]{2,1,0:T(8,128)(2,1)}, u32[]{:S(2)}) copy-start(bf16[64,16,512]{2,1,0:T(8,128)(2,1)} %param.16) | copy-start | bytes 3145732
  2.0 4.1 %copy-start.4 = (bf16[6,50,512]{2,1,0:T(8,128)(2,1)S(1)}, bf16[6,50,512]{2,1,0:T(8,128)(2,1)}, u32[]{:S(2)}) copy-start(bf16[6,50,512]{2,1,0:T(8,128)(2,1)} %param.11) | copy-start | bytes 921604
  2.0 4.9 %copy-start.1 = (s32[4,304,2]{2,1,0:T(8,128)}, s32[4,304,2]{2,1,0:T(8,128)S(1)}, u32[]{:S(2)}) copy-start(s32[4,304,2]{2,1,0:T(8,128)S(1)} %pad.30.refs_7_) | copy-start | bytes 29188
  2.0 4.8 %copy-start.5 = (bf16[6,50,512]{2,1,0:T(8,128)(2,1)S(1)}, bf16[6,50,512]{2,1,0:T(8,128)(2,1)}, u32[]{:S(2)}) copy-start(bf16[6,50,512]{2,1,0:T(8,128)(2,1)} %param.21) | copy-start | bytes 921604
  4.5 3.8 %copy-start.8 = (bf16[64,16]{0,1:T(8,128)(2,1)S(1)}, bf16[64,16]{0,1:T(8,128)(2,1)}, u32[]{:S(2)}) copy-start(bf16[64,16]{0,1:T(8,128)(2,1)} %param.15) | copy-start | bytes 6148
  4.5 3.8 %copy-start.9 = (bf16[64,2]{0,1:T(2,128)(2,1)S(1)}, bf16[64,2]{0,1:T(2,128)(2,1)}, u32[]{:S(2)}) copy-start(bf16[64,2]{0,1:T(2,128)(2,1)} %param.12) | copy-start | bytes 772
  221.7 2.5 %copy-start.7 = (f32[64,512]{1,0:T(8,128)S(1)}, f32[64,512]{1,0:T(8,128)}, u32[]{:S(2)}) copy-start(f32[64,512]{1,0:T(8,128)} %get-tuple-element.16) | copy-start | bytes 393220
  221.7 3.8 %copy-start.3 = (f32[304,512]{1,0:T(8,128)S(1)}, f32[304,512]{1,0:T(8,128)}, u32[]{:S(2)}) copy-start(f32[304,512]{1,0:T(8,128)} %get-tuple-element.14) | copy-start | bytes 1867780
  221.7 4.7 %copy-start.6 = (bf16[304,512]{1,0:T(8,128)(2,1)S(1)}, bf16[304,512]{1,0:T(8,128)(2,1)}, u32[]{:S(2)}) copy-start(bf16[304,512]{1,0:T(8,128)(2,1)} %get-tuple-element.13) | copy-start | bytes 933892

commit v4 on v3

--- a/solution.py
+++ b/solution.py
@@ -350,6 +350,7 @@
         self.chip_x = self.y * 2 + (1 - self.x)
         self.chip_y = (1 - self.y) * 2 + self.x
         self.sib = (self.chip * 2 + (1 - self.c), self.t)
+        self.nxy = (((1 - self.y) * 2 + 1 - self.x) * 2 + self.c, self.t)
         self.nx_other = (self.chip_x * 2 + (1 - self.c), self.t)
         self.ny_other = (self.chip_y * 2 + (1 - self.c), self.t)
         self.pair = lax.rem(self.t, 2) * (-2) + self.t + 1
@@ -461,6 +462,22 @@
 
     def share(self, block):
         return self.go.to(self.full(block), self.full(block), self.here.sib)
+
+
+class PlaneGather:
+    def __init__(self, go, here, full):
+        self.go, self.here, self.full = go, here, full
+        mine = full.at[here.y, here.x, here.c]
+        self.copies = [go.to(mine, mine, device) for device in (here.nx, here.ny, here.nxy)]
+
+    def share(self):
+        for copy in self.copies:
+            copy.wait_recv()
+        mine = self.full.at[:, :, self.here.c]
+        self.shared = self.go.to(mine, mine, self.here.sib)
+
+    def wait(self):
+        self.shared.wait_recv()
 
 
 class Reduce:
@@ -534,12 +551,29 @@
 
     clear(r.img)
     clear(r.oimg)
-    r.row[pl.ds(used, s.rows - used), :] = jnp.zeros((s.rows - used, 3 * s.heads), F32)
+    line = r.comb.at[3]
+
+    rows_at = [pl.ds(i * s.quarter, s.quarter) for i in range(s.images)]
+
+    def rows_of(images, out):
+        r.tmp[pl.ds(used, s.rows - used), :] = jnp.zeros((s.rows - used, s.width), F32)
+        for i, at in enumerate(rows_at):
+            r.tmp[at, :] = images[i].astype(F32)
+        out[...] = r.tmp[...].astype(BF)
 
     wo_copies = [go.to(r.wo, r.wo_z.at[t], (dp, here.ring_t(k))) for k in range(1, nt)]
+    keep_wo = go.here(r.wo, r.wo_z.at[t])
+    pack_own = r.pack.at[y, x, c]
+    cols = 3 * s.shard
+    for k in range(3):
+        pack_own[pl.ds(k * s.shard, s.shard), :] = r.wq[k]
+    pack_own[pl.ds(cols, s.experts), : s.shard] = r.wr[...]
+    gains = jnp.concatenate([r.gains[...].astype(F32), jnp.zeros((14, s.shard), F32)], 0)
+    pack_own[pl.ds(cols + s.experts, 16), : s.shard] = gains.astype(BF)
+    packs = PlaneGather(go, here, r.pack)
+    rows_of(r.x_in, r.x)
     x_blocks = Gather(go, here, r.x, lambda block: r.n1.at[block])
-    sm_copies = [go.to(r.sm, r.sm_all.at[dp], (here.ring_dp(k), t)) for k in range(1, s.n_dp)]
-    wq_copies = [go.to(r.wq, r.wq_all.at[dp], (here.ring_dp(k), t)) for k in range(1, s.n_dp)]
+    rows_of(r.dz_in, r.dz)
 
     def spread(shard, full):
         to = full.at[:, y, x, pl.ds(pl.multiple_of(c * s.shard, s.shard), s.shard)]
@@ -549,9 +583,6 @@
         return from_x, from_y, go.to(rest, to, here.sib), go.here(half, to)
 
     in_x, in_y, in_sib, keep_in = spread(r.win, r.win_all)
-    keep_sm = go.here(r.sm, r.sm_all.at[dp])
-    keep_wq = go.here(r.wq, r.wq_all.at[dp])
-    keep_wo = go.here(r.wo, r.wo_z.at[t])
     tgt_copy = go.to(r.tgt, r.tgt_all.at[c], here.sib)
     keep_tgt = go.here(r.tgt, r.tgt_all.at[c])
 
@@ -561,28 +592,29 @@
     dz_sib = go.to(r.dz, dz_block(t), here.sib)
     keep_dz = go.here(r.dz, dz_block(t))
 
-    keep_sm.wait()
-    for copy in sm_copies:
-        copy.wait_recv()
-    small = jnp.concatenate([r.sm_all[k][:, : s.shard].astype(F32) for k in range(s.n_dp)], 1)
+    keep_wo.wait()
+    for copy in wo_copies:
+        copy.wait_recv()
+    r.wo_all[y, x, c] = r.wo_z[...]
+    wos = PlaneGather(go, here, r.wo_all)
+    packs.share()
+    packs.wait()
+    small = jnp.concatenate(
+        [r.pack[k // 4, k // 2 % 2, k % 2, cols:, : s.shard].astype(F32) for k in range(s.n_dp)], 1
+    )
     r.small[...] = small
     gain_one = small[s.experts : s.experts + 1]
     gain_two = small[s.experts + 1 : s.experts + 2]
-    keep_wq.wait()
-    for copy in wq_copies:
-        copy.wait_recv()
-
-    keep_wo.wait()
-    for copy in wo_copies:
-        copy.wait_recv()
-    keep_wo_all = go.here(r.wo_z, r.wo_all.at[dp])
-    wo_out = [go.to(r.wo_z, r.wo_all.at[dp], (here.ring_dp(k), t)) for k in range(1, s.n_dp)]
+
+    def qkv_weights(k):
+        return r.pack[:, :, :, k * s.shard : (k + 1) * s.shard].reshape(s.width, s.heads)
 
     def project(slot, values):
         unit, _ = norm_parts(values.astype(F32))
         normed = (unit * gain_one).astype(BF)
         r.n1[slot] = normed
-        r.comb[slot, :, : 3 * s.heads] = dot(normed, r.wq_all[...].reshape(s.width, 3 * s.heads))
+        weights = jnp.concatenate([qkv_weights(k) for k in range(3)], 1)
+        r.comb[slot, :, : 3 * s.heads] = dot(normed, weights)
 
     project(t, r.x[...])
     x_blocks.relay()
@@ -593,6 +625,7 @@
     project(here.far, r.n1[here.far])
     x_blocks.wait_cross()
     project(here.cross, r.n1[here.cross])
+    wos.share()
     dz_blocks = Gather(go, here, r.dz, dz_block)
 
     low_half, high_half = pl.ds(0, per), pl.ds(per, per)
@@ -625,21 +658,26 @@
         return carry
 
     lax.fori_loop(0, s.images, attend, 0)
+    line[pl.ds(used, s.rows - used), :] = jnp.zeros((s.rows - used, s.width), F32)
     for q in range(nt):
-        to_block_rows(q, r.oimg, r.row)
-        r.o_send[q] = r.row[:, : s.heads].astype(BF)
+        to_block_rows(q, r.oimg, line)
+        r.o_send[q] = line[:, : s.heads].astype(BF)
     o_copies = [go.to(r.o_send.at[here.ring_t(k)], r.o.at[t], (dp, here.ring_t(k))) for k in range(1, nt)]
     r.o[t] = r.o_send[t]
     dz_blocks.relay()
-    keep_wo_all.wait()
-    for copy in wo_out:
-        copy.wait_recv()
+    wos.wait()
     for copy in o_copies:
         copy.wait_recv()
     branch = jnp.zeros((s.rows, s.width), F32)
     for q in range(nt):
-        branch = branch + dot_nt(r.o[q], r.wo_all[:, q].reshape(s.width, s.heads))
-    middle = r.x[...].astype(F32) + r.live[...] * branch
+        branch = branch + dot_nt(r.o[q], r.wo_all[:, :, :, q].reshape(s.width, s.heads))
+    row = lax.broadcasted_iota(jnp.int32, (s.rows, 1), 0)
+    place = t * s.quarter + row
+    for _ in range(1, s.images):
+        place = jnp.where(place >= t * s.quarter + s.quarter, place - s.quarter, place)
+    live = jnp.where((row < r.alive[0] * s.quarter) & (place < TOK_IMG) & (row < used), 1.0, 0.0)
+    r.live[...] = live
+    middle = r.x[...].astype(F32) + live * branch
     r.y[...] = middle
     unit, _ = norm_parts(middle)
     normed_two = (unit * gain_two).astype(BF)
@@ -655,6 +693,7 @@
     pr_sib = go.to(r.prob, r.prob_all.at[c, t], here.sib)
     pr_copies = [go.to(r.prob, r.prob_all.at[c, t], (dp, here.ring_t(k))) for k in range(1, nt)]
 
+    out_on = pass_on(r.wout_all, out_x, out_y)
     n2_blocks.relay()
     on_n2 = [n2_blocks.share(here.far)]
     on_dz = [dz_blocks.share(here.far)]
@@ -668,7 +707,6 @@
         copy.wait_recv()
         slot = r.prob_all.at[c, here.from_t(k)]
         on_n2.append(go.to(slot, slot, here.sib))
-    out_on = pass_on(r.wout_all, out_x, out_y)
     keep_tgt.wait()
     keep_dz.wait()
     for copy in [tgt_copy, dz_sib] + on_dz:
@@ -811,10 +849,10 @@
     def forward_sum(q):
         return combine(r.gev, 1 - c, q, combine(ge_own, c, q, zero_rows))
 
-    m_sum.pair(0, forward_sum(here.cross))
-    m_sum.pair(1, forward_sum(here.pair))
+    r.m_send[0] = forward_sum(here.cross).astype(BF)
+    r.m_send[1] = forward_sum(here.pair).astype(BF)
     r.comb[2] = forward_sum(here.far)
-    r.gx[...] = forward_sum(t) + r.y[...]
+    r.tmp[...] = forward_sum(t) + r.y[...]
 
     dprobs = r.dprf[t]
     for k, copy in enumerate(dpr_copies):
@@ -829,6 +867,9 @@
     grad_router = dot_tn(r.n2_all[c, t], dlogits.T).T
     dn2 = r.comb[0] + dot_tn(dlogits, small[: s.experts].astype(BF))
     dn2 = dn2_sum.total(dn2)
+    for k in range(2):
+        for p in m_sum.pieces:
+            m_sum.put(k, p, here.pair)
     middle = r.y[...]
     dy_ln, unit = norm_back(middle, gain_two, dn2)
     dgain_two = jnp.sum(dn2 * unit, 0, keepdims=True)
@@ -837,7 +878,7 @@
     da = (r.live[...] * dy).astype(BF)
     go.sent_now(o_copies)
     for q in range(nt):
-        r.o_send[q] = dot(da, r.wo_all[:, q].reshape(s.width, s.heads)).astype(BF)
+        r.o_send[q] = dot(da, r.wo_all[:, :, :, q].reshape(s.width, s.heads)).astype(BF)
     do_copies = [go.to(r.o_send.at[here.ring_t(k)], r.do.at[t], (dp, here.ring_t(k))) for k in range(1, nt)]
     r.do[t] = r.o_send[t]
     for q in range(nt):
@@ -870,13 +911,13 @@
         lax.fori_loop(0, per, step_b, 0)
         fb_copies.append(go.to(r.wout_all.at[piece, y, 1 - x], r.fb.at[piece], here.nx))
 
+    pump(0)
     for copy in do_copies:
         copy.wait_recv()
-    m_sum.across(r.comb[2])
     clear(r.oimg)
     for q in range(nt):
-        r.row[:, : s.heads] = r.do[q].astype(F32)
-        to_image_rows(q, r.row, r.oimg)
+        line[:, : s.heads] = r.do[q].astype(F32)
+        to_image_rows(q, line, r.oimg)
 
     def attend_back(i, carry):
         block = r.qkv[i]
@@ -896,12 +937,12 @@
         return carry
 
     lax.fori_loop(0, s.images, attend_back, 0)
-    pump(0)
-    r.row[pl.ds(used, s.rows - used), :] = jnp.zeros((s.rows - used, 3 * s.heads), F32)
+    m_sum.across(r.comb[2])
+    line[pl.ds(used, s.rows - used), :] = jnp.zeros((s.rows - used, s.width), F32)
     for q in range(nt):
-        to_block_rows(q, r.img, r.row)
-        r.dqkv[q] = r.row[...].astype(BF)
-    w_qkv = r.wq_all[...].reshape(s.width, 3 * s.heads)
+        to_block_rows(q, r.img, line)
+        r.dqkv[q] = line[:, : 3 * s.heads].astype(BF)
+    w_qkv = jnp.concatenate([qkv_weights(k) for k in range(3)], 1)
     dn2_sum.sent()
     dn1_sum = Reduce(go, here, r.rs_send, r.rs_recv)
     dgain_one = jnp.zeros((1, s.width), F32)
@@ -925,7 +966,6 @@
         [grad_router, dgain_one, dgain_two, jnp.zeros((r.sm_send.shape[1] - s.experts - 2, s.width), F32)], 0
     )
     step = [go.to(grads.at[:, :, 1 - c], r.gs_recv, here.sib), go.to(r.sm_send.at[0], r.sm_recv.at[0], here.sib)]
-    dn1_sum.across(r.comb[1])
 
     def add_small(k):
         r.sm_send[k + 1] = r.sm_send[k] + r.sm_recv[k]
@@ -939,6 +979,7 @@
     grads[:, :, c] = add_in(grads[:, :, c], r.gs_recv[...])
     add_small(0)
     step = [go.to(grads.at[:, 1 - x, c], r.gx_recv, here.nx), go.to(r.sm_send.at[1], r.sm_recv.at[1], here.nx)]
+    dn1_sum.across(r.comb[1])
     for copy in step:
         copy.wait_recv()
     grads[:, x, c] = add_in(grads[:, x, c], r.gx_recv[...])
@@ -948,36 +989,29 @@
         copy.wait_recv()
     add_small(2)
     summed = grads[y, x, c].astype(F32) + r.gy_recv[...].astype(F32)
-    r.gqo[:, : 3 * s.heads] = summed[:, : 3 * s.heads]
+    for k in range(3):
+        r.gq[k] = summed[:, k * s.heads : (k + 1) * s.heads]
     for q in range(nt):
         r.gz_send[q] = summed[:, (3 + q) * s.heads : (4 + q) * s.heads].astype(BF)
     gz_copies = [go.to(r.gz_send.at[here.ring_t(k)], r.gz_recv.at[k - 1], (dp, here.ring_t(k))) for k in range(1, nt)]
-    sm_copies = [go.to(r.sm_send.at[3], r.sm_recv.at[2 + k], (dp, here.ring_t(k))) for k in range(1, nt)]
-    r.out[...] = m_sum.total(r.gx[...]).astype(BF)
-
-    dn1 = dn1_sum.total(r.comb[3])
-    dx_ln, _ = norm_back(r.x[...].astype(F32), gain_one, dn1)
-    r.gx[...] = r.comb[0] + dx_ln
-    total = r.gz_send[t].astype(F32)
-    for k, copy in enumerate(gz_copies):
-        copy.wait_recv()
-        total = total + r.gz_recv[k].astype(F32)
-    r.gqo[:, 3 * s.heads :] = total
-    total = r.sm_send[3]
-    for k, copy in enumerate(sm_copies):
-        copy.wait_recv()
-        total = total + r.sm_recv[3 + k]
-    r.gsm[...] = total
+    sums = r.sm_send[3]
+    pieces = [jnp.where(dp == k, sums[:, k * s.shard : (k + 1) * s.shard], 0.0) for k in range(s.n_dp)]
+    r.sz_send[...] = jnp.zeros(r.sz_send.shape, F32)
+    r.sz_send[:, : s.shard] = sum(pieces[1:], pieces[0])
+    sm_copies = [go.to(r.sz_send, r.sz_recv.at[k - 1], (dp, here.ring_t(k))) for k in range(1, nt)]
+    r.tmp[...] = m_sum.total(r.tmp[...])
+    for i, at in enumerate(rows_at):
+        r.out[i] = r.tmp[at, :].astype(BF)
 
     mine = pl.ds(pl.multiple_of(c * s.shard, s.shard), s.shard)
     other = pl.ds(pl.multiple_of((1 - c) * s.shard, s.shard), s.shard)
     fin_copies = []
-    parts = ((r.win_all, r.ra, y, r.fa, fa_copies), (r.wout_all, r.rb, x, r.fb, fb_copies))
-    for w, (own, first, place, second, copies) in enumerate(parts):
+    parts = ((r.win_all, r.ra, y, r.fa, fa_copies, r.gwi), (r.wout_all, r.rb, x, r.fb, fb_copies, r.gwo))
+    for own, first, place, second, copies, gw in parts:
         for j in range(2):
             copies[j].wait_recv()
 
-            def last(i, carry, w=w, own=own, first=first, place=place, second=second, j=j):
+            def last(i, carry, own=own, first=first, place=place, second=second, gw=gw, j=j):
                 e = j * per + i
 
                 def total(rows):
@@ -988,12 +1022,29 @@
                     )
 
                 own[e, y, x, other, :] = total(other).astype(BF)
-                r.gw[w, c, e] = total(mine).astype(BF)
+                gw[c, e] = total(mine).astype(BF)
                 return carry
 
             lax.fori_loop(0, per, last, 0)
             piece = pl.ds(j * per, per)
-            fin_copies.append(go.to(own.at[piece, y, x, other], r.gw.at[w, c, piece], here.sib))
+            fin_copies.append(go.to(own.at[piece, y, x, other], gw.at[c, piece], here.sib))
+    dn1 = dn1_sum.total(r.comb[3])
+    dx_ln, _ = norm_back(r.x[...].astype(F32), gain_one, dn1)
+    r.tmp[...] = r.comb[0] + dx_ln
+    for i, at in enumerate(rows_at):
+        r.gx[i] = r.tmp[at, :]
+    total = r.gz_send[t].astype(F32)
+    for k, copy in enumerate(gz_copies):
+        copy.wait_recv()
+        total = total + r.gz_recv[k].astype(F32)
+    r.go[...] = total
+    total = r.sz_send[...]
+    for k, copy in enumerate(sm_copies):
+        copy.wait_recv()
+        total = total + r.sz_recv[k]
+    r.gr[...] = total[: s.experts, : s.shard]
+    r.gg[...] = total[s.experts : s.experts + 2, : s.shard]
+
     for copy in fin_copies:
         copy.wait_recv()
     go.finish()
@@ -1028,22 +1079,8 @@
     used = images * quarter
     rows = up(used, 16)
     s = Sizes(n_dp, n_t, images, quarter, rows, up(length, 16), width, shard, heads, experts, ff, up(rows, 128))
-    dp, t = lax.axis_index("dp"), lax.axis_index("tensor")
-
-    def by_rows(values):
-        return jnp.pad(values.reshape(used, width), ((0, rows - used), (0, 0)))
-
-    x_own, dz_own = by_rows(block_input), by_rows(cotangent)
-    wq = w_qkv.reshape(shard, 3 * heads)
-    wo = w_o.T
-    sm_rows = up(experts + 2, 16)
-    small = jnp.concatenate([w_router.T, gains.T], 0)
-    small = jnp.pad(small, ((0, sm_rows - experts - 2), (0, up(shard, 128) - shard)))
     win_t = w_in.transpose(1, 0, 2).reshape(2, s.half, shard, ff)
     wout_t = w_out.transpose(1, 2, 0).reshape(2, s.half, shard, ff)
-    place = t * quarter + jnp.arange(quarter)
-    live = (jnp.arange(images) < pictures_alive_per_shard[0])[:, None] & (place < TOK_IMG)[None, :]
-    live = jnp.pad(live.astype(F32).reshape(used, 1), ((0, rows - used), (0, 0)))
     targets = jnp.where(slot_index >= 0, expert_ids * CAP + slot_index, -1)
     targets = targets.reshape(images, n_t, quarter, 2).transpose(1, 0, 2, 3).reshape(n_t, used, 2)
     targets = jnp.pad(targets, ((0, 0), (0, rows - used), (0, 0)), constant_values=-1)
@@ -1053,14 +1090,28 @@
     gsm_rows = up(experts + 2, 8)
     tokens = n_t * rows
     inputs = dict(
-        x=x_own, dz=dz_own, wq=wq, wo=wo, sm=small, live=live, tgt=tgt_rows, tcol=targets, win=win_t, wout=wout_t
-    )
+        x_in=block_input,
+        dz_in=cotangent,
+        wq=w_qkv.transpose(1, 0, 2),
+        wo=w_o.T,
+        wr=w_router.T,
+        gains=gains.T,
+        tgt=tgt_rows,
+        tcol=targets,
+        alive=pictures_alive_per_shard,
+        win=win_t,
+        wout=wout_t,
+    )
+    in_specs = {"win": ASPEC, "wout": ASPEC, "alive": pl.BlockSpec(memory_space=pltpu.SMEM)}
     outputs = dict(
-        out=shape((rows, width), BF),
-        gx=shape((rows, width), F32),
-        gqo=shape((shard, 4 * heads), F32),
-        gsm=shape((gsm_rows, width), F32),
-        gw=shape((2, 2, s.half, shard, ff), BF),
+        out=shape((images, quarter, width), BF),
+        gx=shape((images, quarter, width), F32),
+        gq=shape((3, shard, heads), F32),
+        go=shape((shard, heads), F32),
+        gr=shape((experts, shard), F32),
+        gg=shape((2, shard), F32),
+        gwi=shape((2, s.half, shard, ff), BF),
+        gwo=shape((2, s.half, shard, ff), BF),
     )
     wide = (two_y, two_x, 2 * shard, ff)
     per = s.half // 2
@@ -1077,12 +1128,14 @@
         n1=((n_t, rows, width), BF),
         o=((n_t, rows, heads), BF),
         do=((n_t, rows, heads), BF),
-        wq_all=((n_dp, shard, 3 * heads), BF),
-        wo_all=((n_dp, n_t, shard, heads), BF),
+        x=((rows, width), BF),
+        dz=((rows, width), BF),
+        tmp=((rows, width), F32),
+        live=((rows, 1), F32),
+        pack=((two_y, two_x, 2, 3 * shard + up(experts + 2, 16), heads), BF),
+        wo_all=((two_y, two_x, 2, n_t, shard, heads), BF),
         wo_z=((n_t, shard, heads), BF),
-        sm_all=((n_dp, *small.shape), BF),
-        small=((sm_rows, width), F32),
-        row=((rows, 3 * heads), F32),
+        small=((up(experts + 2, 16), width), F32),
         img=((images, s.irows, 3 * heads), F32),
         oimg=((images, s.irows, heads), F32),
         o_send=((n_t, rows, heads), BF),
@@ -1111,7 +1164,9 @@
         gz_send=((n_t, shard, heads), BF),
         gz_recv=((n_t - 1, shard, heads), BF),
         sm_send=((4, gsm_rows, width), F32),
-        sm_recv=((n_t + 2, gsm_rows, width), F32),
+        sm_recv=((3, gsm_rows, width), F32),
+        sz_send=((gsm_rows, up(shard, 128)), F32),
+        sz_recv=((n_t - 1, gsm_rows, up(shard, 128)), F32),
         ra=((s.half, two_y, 2 * shard, ff), BF),
         rb=((s.half, two_x, 2 * shard, ff), BF),
         fa=((s.half, 2 * shard, ff), BF),
@@ -1119,10 +1174,10 @@
     )
     links = 160
     names = [*inputs, *outputs, *scratch, "send", "recv", "local"]
-    out, gx, gqo, gsm, gw = pl.pallas_call(
+    out, gx, gq, grad_o, gr, gg, gwi, gwo = pl.pallas_call(
         lambda *refs: block_kernel(s, names, *refs),
         out_shape=tuple(outputs.values()),
-        in_specs=[VSPEC] * (len(inputs) - 2) + [ASPEC] * 2,
+        in_specs=[in_specs.get(name, VSPEC) for name in inputs],
         out_specs=[VSPEC] * len(outputs),
         scratch_shapes=[pltpu.VMEM(dims, kind) for dims, kind in scratch.values()]
         + [pltpu.SemaphoreType.DMA((links,)), pltpu.SemaphoreType.DMA((links,)), pltpu.SemaphoreType.DMA((10,))],
@@ -1130,20 +1185,15 @@
         name="block",
     )(*inputs.values())
 
-    def by_image(values):
-        return values[:used].reshape(images, quarter, width)
-
-    gw = gw.reshape(2, experts, shard, ff)
-    own_small = lax.dynamic_slice(gsm, (0, dp * shard), (gsm_rows, shard))
     return (
-        by_image(out),
-        by_image(gx),
-        own_small[experts : experts + 2].T,
-        gqo[:, : 3 * heads].reshape(shard, 3, heads),
-        gqo[:, 3 * heads :].T,
-        own_small[:experts].T,
-        gw[0].transpose(1, 0, 2).astype(F32),
-        gw[1].transpose(2, 0, 1).astype(F32),
+        out,
+        gx,
+        gg.T,
+        gq.transpose(1, 0, 2),
+        grad_o.T,
+        gr.T,
+        gwi.reshape(experts, shard, ff).transpose(1, 0, 2).astype(F32),
+        gwo.reshape(experts, shard, ff).transpose(2, 0, 1).astype(F32),
     )
 
 

time: 228 us -> 208 us (0.912)
  Pallas kernels: 206 us -> 193 us
  local copies, waits for them, and re-layouts: 15.3 us -> 9.45 us
    pallas_call x1, Pallas kernels: 206 us -> 193 us  [linked_body(): pl.pallas_call(lambda *refs: block_kernel(s, names, *refs), out_shape=tup...]
    unnamed x21 -> x22, local copies, waits for them, and re-layouts: 0.7 us -> 4.03 us
    transpose x3 -> x0, local copies, waits for them, and re-layouts: 3.3 us -> none  [the longest x1 1.38 us: linked_body(): own_small[:experts]]
    reshape x5 -> x0, local copies, waits for them, and re-layouts: 2.51 us -> none  [the longest x2 1.72 us: by_image(): return values[:used].reshape(images, quarter, width)]
where the time goes in v4:
time: 208 us
  Pallas kernels  193 us (93%)
  local copies, waits for them, and re-layouts  9.45 us (5%)
  other arithmetic  3.94 us (2%)
    pallas_call x1, Pallas kernels, linked_body(): pl.pallas_call(lambda *refs: block_kernel(s, names, *refs), out_shape=tup...  193 us

profile of v4, /device:TPU:0, one launch (start us, length us, event | category | flops | bytes accessed | tf_op | source)
XLA Modules:
  0.0 207.7 jit_solution(14680367073936358936)
XLA Ops:
  0.6 0.0 copy-start.1
  1.4 0.7 compare_select_fusion
  2.1 0.1 reshape.37
  2.2 0.1 reshape.38
  2.3 0.2 copy.24
  2.6 0.0 copy-start
  2.6 0.2 copy.25
  2.9 0.6 pad.9.refs_6_
  3.5 0.0 copy-done.1
  3.5 1.5 copy.26
  5.1 0.0 copy-done
  5.1 192.8 %block.1 = (bf16[6,50,512]{2,1,0:T(8,128)(2,1)}, f32[6,50,512]{2,1,0:T(8,128)}, f32[3,64,128]{2,1,0:T(8,128)}, f32[64,128]{1,0:T(8,128)}, f32[16,64]{1,0:T(8,128...) custom-call(bf16[6,50,512]{2,1,0:T(8,128)(2,1)} %refs_0_.1, ...), custom_call_target="tpu_custom_call" | custom-call | tf_op jit(solution)/shard_map/block/pallas_call | solution.py:1177
  197.9 3.2 %convert_bitcast_fusion = (f32[512,16,64]{0,2,1:T(8,128)}, f32[16,64,512]{2,1,0:T(8,128)S(1)}) fusion(bf16[2,8,64,512]{3,2,1,0:T(8,128)(2,1)} %get-tuple-element.23, bf16[2,8,64,512]{3,2,1,0:T(8,128)(2,1)} %get-tuple-element.22), kind=kLoop, calls=%fused_computation | loop fusion | flops 1048576 | bytes 6291456 | tf_op jit(solution)/shard_map/convert_element_type | solution.py:1196
  201.1 2.5 %copy.30 = f32[16,64,512]{2,0,1:T(8,128)} copy(f32[16,64,512]{2,1,0:T(8,128)S(1)} %get-tuple-element.25) | data formatting | bytes 4194304 | tf_op jit(solution)/shard_map/convert_element_type | solution.py:1195
  203.7 0.0 copy-done.3
  203.7 0.7 copy.39
  204.4 0.0 copy-done.2
  204.4 0.8 copy.40
  205.2 0.0 copy-done.7
  205.2 0.6 copy.41
  205.8 0.0 copy-done.4
  205.8 0.6 copy.42
  206.4 0.6 copy.43
  207.1 0.6 copy.44
  (10 shorter events, 0.1 us)
Async XLA Ops:
  0.6 2.9 %copy-start.1 = (bf16[64,16,512]{2,1,0:T(8,128)(2,1)S(1)}, bf16[64,16,512]{2,1,0:T(8,128)(2,1)}, u32[]{:S(2)}) copy-start(bf16[64,16,512]{2,1,0:T(8,128)(2,1)} %param.16) | copy-start | bytes 3145732
  2.6 2.4 %copy-start = (s32[4,304,2]{2,1,0:T(8,128)}, s32[4,304,2]{2,1,0:T(8,128)S(1)}, u32[]{:S(2)}) copy-start(s32[4,304,2]{2,1,0:T(8,128)S(1)} %pad.8.refs_7_) | copy-start | bytes 29188
  201.1 2.6 %copy-start.3 = (bf16[6,50,512]{2,1,0:T(8,128)(2,1)S(1)}, bf16[6,50,512]{2,1,0:T(8,128)(2,1)}, u32[]{:S(2)}) copy-start(bf16[6,50,512]{2,1,0:T(8,128)(2,1)} %get-tuple-element.34) | copy-start | bytes 921604
  201.1 3.3 %copy-start.2 = (f32[6,50,512]{2,1,0:T(8,128)S(1)}, f32[6,50,512]{2,1,0:T(8,128)}, u32[]{:S(2)}) copy-start(f32[6,50,512]{2,1,0:T(8,128)} %get-tuple-element.35) | copy-start | bytes 1843204
  201.1 4.1 %copy-start.7 = (f32[2,64]{1,0:T(2,128)S(1)}, f32[2,64]{1,0:T(2,128)}, u32[]{:S(2)}) copy-start(f32[2,64]{1,0:T(2,128)} %get-tuple-element.18) | copy-start | bytes 1540
  201.1 4.7 %copy-start.4 = (f32[3,64,128]{2,1,0:T(8,128)S(1)}, f32[3,64,128]{2,1,0:T(8,128)}, u32[]{:S(2)}) copy-start(f32[3,64,128]{2,1,0:T(8,128)} %get-tuple-element.19) | copy-start | bytes 294916
  203.6 2.8 %copy-start.5 = (f32[64,128]{1,0:T(8,128)S(1)}, f32[64,128]{1,0:T(8,128)}, u32[]{:S(2)}) copy-start(f32[64,128]{1,0:T(8,128)} %get-tuple-element.20) | copy-start | bytes 98308
  203.6 3.4 %copy-start.6 = (f32[16,64]{1,0:T(8,128)S(1)}, f32[16,64]{1,0:T(8,128)}, u32[]{:S(2)}) copy-start(f32[16,64]{1,0:T(8,128)} %get-tuple-element.21) | copy-start | bytes 12292

commit v5 on v4

--- a/solution.py
+++ b/solution.py
@@ -374,7 +374,7 @@
             pl.semaphore_signal(barrier, inc=1, device_id=(self.ring_dp(k), self.t), device_id_type=MESH)
         for k in range(1, self.s.n_t):
             pl.semaphore_signal(barrier, inc=1, device_id=(self.dp, self.ring_t(k)), device_id_type=MESH)
-        pl.semaphore_wait(barrier, self.s.n_dp + self.s.n_t - 2)
+        return lambda: pl.semaphore_wait(barrier, self.s.n_dp + self.s.n_t - 2)
 
 
 class Copies:
@@ -530,7 +530,7 @@
     r = SimpleNamespace(**dict(zip(names, refs)))
     here = Place(s)
     dp, t, c, x, y = here.dp, here.t, here.c, here.x, here.y
-    here.greet()
+    all_there = here.greet()
     go = Copies(r.send, r.recv, r.local)
     nt = s.n_t
     length = s.quarter * nt
@@ -561,7 +561,6 @@
             r.tmp[at, :] = images[i].astype(F32)
         out[...] = r.tmp[...].astype(BF)
 
-    wo_copies = [go.to(r.wo, r.wo_z.at[t], (dp, here.ring_t(k))) for k in range(1, nt)]
     keep_wo = go.here(r.wo, r.wo_z.at[t])
     pack_own = r.pack.at[y, x, c]
     cols = 3 * s.shard
@@ -570,8 +569,10 @@
     pack_own[pl.ds(cols, s.experts), : s.shard] = r.wr[...]
     gains = jnp.concatenate([r.gains[...].astype(F32), jnp.zeros((14, s.shard), F32)], 0)
     pack_own[pl.ds(cols + s.experts, 16), : s.shard] = gains.astype(BF)
+    rows_of(r.x_in, r.x)
+    all_there()
+    wo_copies = [go.to(r.wo, r.wo_z.at[t], (dp, here.ring_t(k))) for k in range(1, nt)]
     packs = PlaneGather(go, here, r.pack)
-    rows_of(r.x_in, r.x)
     x_blocks = Gather(go, here, r.x, lambda block: r.n1.at[block])
     rows_of(r.dz_in, r.dz)
 
@@ -583,8 +584,18 @@
         return from_x, from_y, go.to(rest, to, here.sib), go.here(half, to)
 
     in_x, in_y, in_sib, keep_in = spread(r.win, r.win_all)
-    tgt_copy = go.to(r.tgt, r.tgt_all.at[c], here.sib)
-    keep_tgt = go.here(r.tgt, r.tgt_all.at[c])
+
+    chosen = jnp.where(r.slots[...] >= 0, r.ids[...] * CAP + r.slots[...], -1)
+    by_block = []
+    for q in range(nt):
+        parts = [chosen[i, :, q * s.quarter : (q + 1) * s.quarter] for i in range(s.images)]
+        by_block.append(jnp.concatenate(parts + [jnp.full((2, s.rows - used), -1, jnp.int32)], 1))
+        wide = jnp.concatenate([by_block[q], jnp.zeros((2, s.lanes - s.rows), jnp.int32)], 1)
+        wide = jnp.concatenate([wide, jnp.zeros((6, s.lanes), jnp.int32)], 0)
+        r.tcol[q] = wide.T[: s.rows, :2]
+    tgt_own = r.tgt_all.at[c]
+    tgt_own[:2, :] = jnp.concatenate(by_block, 1)
+    tgt_copy = go.to(tgt_own, tgt_own, here.sib)
 
     def dz_block(block):
         return r.ge.at[c, pl.ds(pl.multiple_of(block * s.rows, 16), s.rows)]
@@ -625,22 +636,8 @@
     project(here.far, r.n1[here.far])
     x_blocks.wait_cross()
     project(here.cross, r.n1[here.cross])
-    wos.share()
     dz_blocks = Gather(go, here, r.dz, dz_block)
 
-    low_half, high_half = pl.ds(0, per), pl.ds(per, per)
-
-    def pass_on(full, by_x, by_y):
-        for copy in by_x:
-            copy.wait_recv()
-        from_x = full.at[low_half, y, 1 - x]
-        on_y = go.to(from_x, from_x, here.ny)
-        for copy in by_y:
-            copy.wait_recv()
-        from_y = full.at[high_half, 1 - y, x]
-        return on_y, go.to(from_y, from_y, here.nx)
-
-    in_on = pass_on(r.win_all, in_x, in_y)
     for q in range(nt):
         to_image_rows(q, r.comb.at[q], r.img)
 
@@ -657,14 +654,41 @@
         r.oimg[i] = pick_heads(dot(probs, block[:, 2 * s.heads :]), masks, s.irows)
         return carry
 
-    lax.fori_loop(0, s.images, attend, 0)
+    lax.fori_loop(0, s.images, attend, 0, unroll=2)
     line[pl.ds(used, s.rows - used), :] = jnp.zeros((s.rows - used, s.width), F32)
     for q in range(nt):
         to_block_rows(q, r.oimg, line)
         r.o_send[q] = line[:, : s.heads].astype(BF)
     o_copies = [go.to(r.o_send.at[here.ring_t(k)], r.o.at[t], (dp, here.ring_t(k))) for k in range(1, nt)]
     r.o[t] = r.o_send[t]
+    few = 2
+
+    def pass_on(full, by_x, by_y):
+        for copy in by_x + by_y:
+            copy.wait_recv()
+        copies = []
+        for e in range(0, per, few):
+            from_x = full.at[pl.ds(e, few), y, 1 - x]
+            from_y = full.at[pl.ds(per + e, few), 1 - y, x]
+            copies.append([go.to(from_x, from_x, here.ny), go.to(from_y, from_y, here.nx)])
+        return copies
+
+    in_on = pass_on(r.win_all, in_x, in_y)
+    wos.share()
     dz_blocks.relay()
+    on_dz = [dz_blocks.share(here.far)]
+    tgt_copy.wait_recv()
+    tokens = nt * s.rows
+    half_rows = tokens // 2
+    for q in range(2):
+        first_id = (c * s.half + lax.broadcasted_iota(jnp.int32, (s.half, tokens), 0)) * CAP
+        found = jnp.full((s.half, tokens), -1, jnp.int32)
+        for k in range(2):
+            slot = r.tgt_all[q, k : k + 1, :] - first_id
+            found = jnp.where((slot >= 0) & (slot < CAP), slot, found)
+        r.slot[q] = found.astype(F32)
+        for h in range(2):
+            r.sloth[h, q] = r.slot[q][:, h * half_rows : (h + 1) * half_rows]
     wos.wait()
     for copy in o_copies:
         copy.wait_recv()
@@ -693,34 +717,13 @@
     pr_sib = go.to(r.prob, r.prob_all.at[c, t], here.sib)
     pr_copies = [go.to(r.prob, r.prob_all.at[c, t], (dp, here.ring_t(k))) for k in range(1, nt)]
 
-    out_on = pass_on(r.wout_all, out_x, out_y)
-    n2_blocks.relay()
-    on_n2 = [n2_blocks.share(here.far)]
-    on_dz = [dz_blocks.share(here.far)]
     dz_blocks.wait_pair()
-    on_dz.append(dz_blocks.share(here.pair))
     dz_blocks.wait_cross()
-    on_dz.append(dz_blocks.share(here.cross))
-    n2_blocks.wait_pair()
-    on_n2.append(n2_blocks.share(here.pair))
-    for k, copy in enumerate(pr_copies, 1):
-        copy.wait_recv()
-        slot = r.prob_all.at[c, here.from_t(k)]
-        on_n2.append(go.to(slot, slot, here.sib))
-    keep_tgt.wait()
+    on_dz += [dz_blocks.share(here.pair), dz_blocks.share(here.cross)]
     keep_dz.wait()
-    for copy in [tgt_copy, dz_sib] + on_dz:
-        copy.wait_recv()
-
-    tokens = nt * s.rows
-    few = 2
-    for q in range(2):
-        first_id = (c * s.half + lax.broadcasted_iota(jnp.int32, (s.half, tokens), 0)) * CAP
-        found = jnp.full((s.half, tokens), -1, jnp.int32)
-        for k in range(2):
-            slot = r.tgt_all[q, k : k + 1, :] - first_id
-            found = jnp.where((slot >= 0) & (slot < CAP), slot, found)
-        r.slot[q] = found.astype(F32)
+    for copy in [dz_sib] + on_dz:
+        copy.wait_recv()
+
     slot_ids = lax.broadcasted_iota(jnp.int32, (CAP, tokens), 0).astype(F32)
 
     def dispatch(q, j, rows, out):
@@ -736,18 +739,47 @@
         return carry
 
     lax.fori_loop(0, s.half // few, dispatch_z, 0)
+    n2_blocks.relay()
+    out_on = pass_on(r.wout_all, out_x, out_y)
+    on_n2 = [n2_blocks.share(here.far)]
+    n2_blocks.wait_pair()
+    on_n2.append(n2_blocks.share(here.pair))
+    for k, copy in enumerate(pr_copies, 1):
+        copy.wait_recv()
+        slot = r.prob_all.at[c, here.from_t(k)]
+        on_n2.append(go.to(slot, slot, here.sib))
+
+    def dispatch_x(h, first):
+        def step(j, carry):
+            for q in range(2):
+                for i in range(few):
+                    hits = r.sloth[h, q, pl.ds(few * j + i, 1), :] == slot_ids[:, :half_rows]
+                    r.hot[i, :, :half_rows] = jnp.where(hits, 1.0, 0.0).astype(BF)
+                rows = r.n2_all[q, pl.ds(2 * h, 2)].reshape(half_rows, s.width)
+                found = dot(r.hot[:, :, :half_rows].reshape(few * CAP, half_rows), rows)
+                found = found.reshape(few, CAP, s.width)
+                out = r.xin.at[q, pl.ds(few * j, few)]
+                out[...] = (found if first else found + out[...].astype(F32)).astype(BF)
+            return carry
+
+        lax.fori_loop(0, s.half // few, step, 0)
+
+    n2_sib.wait_recv()
+    on_n2[1].wait_recv()
+    dispatch_x(t // 2, True)
     n2_blocks.wait_cross()
     on_n2.append(n2_blocks.share(here.cross))
     keep_in.wait()
     keep_out.wait()
-    for copy in [n2_sib, pr_sib, in_sib, out_sib, *in_on] + on_n2:
+    for copy in [pr_sib, in_sib, out_sib, *in_on[0], *in_on[1], on_n2[0]] + on_n2[2:]:
         copy.wait_recv()
     mine = pl.ds(pl.multiple_of(c * s.half, s.half), s.half)
     for q in range(2):
         r.pr[q] = jnp.concatenate([r.prob_all[q, k, mine][:, : s.rows] for k in range(nt)], 1)
-    for copy in out_on:
-        copy.wait_recv()
-    go.sent_now([*in_on, *out_on, dz_sib, *dz_blocks.passed, *on_dz])
+    dispatch_x(1 - t // 2, False)
+    for copy in out_on[0]:
+        copy.wait_recv()
+    go.sent_now([*in_on[0], *in_on[1], *out_on[0], dz_sib, *dz_blocks.passed, *on_dz])
     k_in, k_out, k_dx, k_ge = (go.reserve(s.half) for _ in range(4))
 
     def grad_in_copy(e):
@@ -794,9 +826,8 @@
         r.xin[:, e] = dot_nt(dhidden, w_in).astype(BF).reshape(2, CAP, s.width)
         r.win_all[e] = grad_in.reshape(r.win_all.shape[1:])
 
-    def expert_few(j, carry):
-        for q in range(2):
-            dispatch(q, j, r.n2_all[q].reshape(tokens, s.width), r.xin.at[q, pl.ds(few * j, few)])
+    def expert_few(k, carry):
+        j = lax.rem(k, 2) * (per // few) + k // 2
         for i in range(few):
             expert(few * j + i)
         for i in range(few):
@@ -805,18 +836,17 @@
                 go.start_at(k + e, *copy(e))
         return carry
 
-    lax.fori_loop(0, s.half // few, expert_few, 0)
+    lax.fori_loop(0, 2, expert_few, 0)
+    for copies in out_on[1:]:
+        for copy in copies:
+            copy.wait_recv()
+        go.sent_now(copies)
+    lax.fori_loop(2, s.half // few, expert_few, 0)
     ge_copies = [go.at(k_ge + e, *ge_copy(e)) for e in range(s.half)]
     dx_copies = [go.at(k_dx + e, *dx_copy(e)) for e in range(s.half)]
     in_copies = [go.at(k_in + e, *grad_in_copy(e)) for e in range(s.half)]
     out_copies = [go.at(k_out + e, *grad_out_copy(e)) for e in range(s.half)]
 
-    r.dprs[...] = jnp.zeros(r.dprs.shape, F32)
-    for q in range(2):
-        for k in range(nt):
-            r.dprs[q, k, :, : s.rows] = r.dpr[q][:, k * s.rows : (k + 1) * s.rows]
-    dpr_sib = go.to(r.dprs.at[1 - c], r.dprf.at[:, c], here.sib)
-    r.dprf[:, c] = r.dprs[c]
     zero_rows = jnp.zeros((s.rows, s.width), F32)
     span = 512
 
@@ -836,8 +866,15 @@
     dn2_sum = Reduce(go, here, r.rs_send, r.rs_recv)
     dn2_sum.pair(0, combine(dxv, 1 - c, here.cross, r.comb[0]))
     dn2_sum.pair(1, combine(dxv, 1 - c, here.pair, combine(dx_own, c, here.pair, zero_rows)))
+    r.dprs[...] = jnp.zeros(r.dprs.shape, F32)
+    for q in range(2):
+        for k in range(nt):
+            r.dprs[q, k, :, : s.rows] = r.dpr[q][:, k * s.rows : (k + 1) * s.rows]
+    dpr_sib = go.to(r.dprs.at[1 - c], r.dprf.at[:, c], here.sib)
+    r.dprf[:, c] = r.dprs[c]
     dpr_sib.wait_recv()
-    dpr_copies = [go.to(r.dprf.at[here.ring_t(k)], r.dprz.at[k - 1], (dp, here.ring_t(k))) for k in range(1, nt)]
+    r.dprb[...] = r.dprf[...].reshape(r.dprb.shape).astype(BF)
+    dpr_copies = [go.to(r.dprb.at[here.ring_t(k)], r.dprz.at[k - 1], (dp, here.ring_t(k))) for k in range(1, nt)]
     dn2_sum.across(combine(dxv, 1 - c, here.far, combine(dx_own, c, here.far, zero_rows)))
     r.comb[0] = combine(dxv, 1 - c, t, combine(dx_own, c, t, zero_rows))
 
@@ -854,11 +891,10 @@
     r.comb[2] = forward_sum(here.far)
     r.tmp[...] = forward_sum(t) + r.y[...]
 
-    dprobs = r.dprf[t]
+    dprobs = r.dprf[t].reshape(s.experts, s.lanes)
     for k, copy in enumerate(dpr_copies):
         copy.wait_recv()
-        dprobs = dprobs + r.dprz[k]
-    dprobs = dprobs.reshape(s.experts, s.lanes)
+        dprobs = dprobs + r.dprz[k].astype(F32)
     probs = r.prob[...]
     dlogits = (probs * (dprobs - jnp.sum(probs * dprobs, 0, keepdims=True))).astype(BF)[:, : s.rows]
     small = r.small[...]
@@ -867,9 +903,6 @@
     grad_router = dot_tn(r.n2_all[c, t], dlogits.T).T
     dn2 = r.comb[0] + dot_tn(dlogits, small[: s.experts].astype(BF))
     dn2 = dn2_sum.total(dn2)
-    for k in range(2):
-        for p in m_sum.pieces:
-            m_sum.put(k, p, here.pair)
     middle = r.y[...]
     dy_ln, unit = norm_back(middle, gain_two, dn2)
     dgain_two = jnp.sum(dn2 * unit, 0, keepdims=True)
@@ -880,6 +913,9 @@
     for q in range(nt):
         r.o_send[q] = dot(da, r.wo_all[:, :, :, q].reshape(s.width, s.heads)).astype(BF)
     do_copies = [go.to(r.o_send.at[here.ring_t(k)], r.do.at[t], (dp, here.ring_t(k))) for k in range(1, nt)]
+    for k in range(2):
+        for p in m_sum.pieces:
+            m_sum.put(k, p, here.pair)
     r.do[t] = r.o_send[t]
     for q in range(nt):
         part = dot_tn(da, r.o[q]).reshape(*r.grads.shape[:3], s.shard, s.heads)
@@ -936,8 +972,7 @@
         r.img[i, :, 2 * s.heads :] = dvalues
         return carry
 
-    lax.fori_loop(0, s.images, attend_back, 0)
-    m_sum.across(r.comb[2])
+    lax.fori_loop(0, s.images, attend_back, 0, unroll=2)
     line[pl.ds(used, s.rows - used), :] = jnp.zeros((s.rows - used, s.width), F32)
     for q in range(nt):
         to_block_rows(q, r.img, line)
@@ -955,6 +990,7 @@
             r.comb[2 * k - 3] = part
     dgain_one = dgain_one / gain_one
 
+    m_sum.across(r.comb[2])
     pump(1)
 
     grad_qkv = jnp.zeros((s.width, 3 * s.heads), F32)
@@ -1005,7 +1041,7 @@
 
     mine = pl.ds(pl.multiple_of(c * s.shard, s.shard), s.shard)
     other = pl.ds(pl.multiple_of((1 - c) * s.shard, s.shard), s.shard)
-    fin_copies = []
+    fin_copies, kept = [], []
     parts = ((r.win_all, r.ra, y, r.fa, fa_copies, r.gwi), (r.wout_all, r.rb, x, r.fb, fb_copies, r.gwo))
     for own, first, place, second, copies, gw in parts:
         for j in range(2):
@@ -1022,12 +1058,13 @@
                     )
 
                 own[e, y, x, other, :] = total(other).astype(BF)
-                gw[c, e] = total(mine).astype(BF)
+                own[e, y, x, mine, :] = total(mine).astype(BF)
                 return carry
 
             lax.fori_loop(0, per, last, 0)
             piece = pl.ds(j * per, per)
             fin_copies.append(go.to(own.at[piece, y, x, other], gw.at[c, piece], here.sib))
+            kept.append(go.here(own.at[piece, y, x, mine], gw.at[c, piece]))
     dn1 = dn1_sum.total(r.comb[3])
     dx_ln, _ = norm_back(r.x[...].astype(F32), gain_one, dn1)
     r.tmp[...] = r.comb[0] + dx_ln
@@ -1047,6 +1084,8 @@
 
     for copy in fin_copies:
         copy.wait_recv()
+    for copy in kept:
+        copy.wait()
     go.finish()
 
 
@@ -1081,11 +1120,6 @@
     s = Sizes(n_dp, n_t, images, quarter, rows, up(length, 16), width, shard, heads, experts, ff, up(rows, 128))
     win_t = w_in.transpose(1, 0, 2).reshape(2, s.half, shard, ff)
     wout_t = w_out.transpose(1, 2, 0).reshape(2, s.half, shard, ff)
-    targets = jnp.where(slot_index >= 0, expert_ids * CAP + slot_index, -1)
-    targets = targets.reshape(images, n_t, quarter, 2).transpose(1, 0, 2, 3).reshape(n_t, used, 2)
-    targets = jnp.pad(targets, ((0, 0), (0, rows - used), (0, 0)), constant_values=-1)
-    tgt_rows = jnp.pad(targets.reshape(n_t * rows, 2).T, ((0, 6), (0, 0)), constant_values=-1)
-
     two_y, two_x = n_dp // 4, 2
     gsm_rows = up(experts + 2, 8)
     tokens = n_t * rows
@@ -1096,8 +1130,8 @@
         wo=w_o.T,
         wr=w_router.T,
         gains=gains.T,
-        tgt=tgt_rows,
-        tcol=targets,
+        ids=expert_ids.transpose(0, 2, 1),
+        slots=slot_index.transpose(0, 2, 1),
         alive=pictures_alive_per_shard,
         win=win_t,
         wout=wout_t,
@@ -1121,6 +1155,7 @@
         n2_all=((2, n_t, rows, width), BF),
         prob_all=((2, n_t, experts, s.lanes), F32),
         tgt_all=((2, 8, tokens), jnp.int32),
+        tcol=((n_t, rows, 2), jnp.int32),
         y=((rows, width), F32),
         prob=((experts, s.lanes), F32),
         qkv=((images, s.irows, 3 * heads), BF),
@@ -1144,10 +1179,12 @@
         dpr=((2, s.half, tokens), F32),
         dprs=((2, n_t, s.half, s.lanes), F32),
         dprf=((n_t, 2, s.half, s.lanes), F32),
-        dprz=((n_t - 1, 2, s.half, s.lanes), F32),
+        dprb=((n_t, experts, s.lanes), BF),
+        dprz=((n_t - 1, experts, s.lanes), BF),
         hot=((2, CAP, tokens), BF),
         xin=((2, s.half, CAP, width), BF),
         slot=((2, s.half, tokens), F32),
+        sloth=((2, 2, s.half, tokens // 2), F32),
         zin=((2, s.half, CAP, width), BF),
         ge=((2, s.slots, width), BF),
         dxv=((s.half, CAP, width), BF),
@@ -1178,7 +1215,7 @@
         lambda *refs: block_kernel(s, names, *refs),
         out_shape=tuple(outputs.values()),
         in_specs=[in_specs.get(name, VSPEC) for name in inputs],
-        out_specs=[VSPEC] * len(outputs),
+        out_specs=[ASPEC if name in ("gwi", "gwo") else VSPEC for name in outputs],
         scratch_shapes=[pltpu.VMEM(dims, kind) for dims, kind in scratch.values()]
         + [pltpu.SemaphoreType.DMA((links,)), pltpu.SemaphoreType.DMA((links,)), pltpu.SemaphoreType.DMA((10,))],
         compiler_params=pltpu.CompilerParams(collective_id=1, has_side_effects=True, vmem_limit_bytes=VMEM_BYTES),
@@ -1192,7 +1229,7 @@
         gq.transpose(1, 0, 2),
         grad_o.T,
         gr.T,
-        gwi.reshape(experts, shard, ff).transpose(1, 0, 2).astype(F32),
+        lax.optimization_barrier(gwi.reshape(experts, shard, ff).transpose(1, 0, 2)).astype(F32),
         gwo.reshape(experts, shard, ff).transpose(2, 0, 1).astype(F32),
     )
 

time: 208 us -> 196 us (0.942)
  Pallas kernels: 193 us -> 182 us
    pallas_call x1, Pallas kernels: 193 us -> 182 us  [linked_body(): pl.pallas_call(lambda *refs: block_kernel(s, names, *refs), out_shape=tup...]
    convert_element_type x1 -> x0, local copies, waits for them, and re-layouts: 2.54 us -> none  [linked_body(): gwi.reshape(experts, shard, ff).transpose(1, 0, 2).astype(F32)]
where the time goes in v5:
time: 196 us; the launch traced here: 195 us
  Pallas kernels  182 us (93%)
  local copies, waits for them, and re-layouts  8.6 us (4%)
  other arithmetic  3.29 us (2%)
    pallas_call x1, Pallas kernels, linked_body(): pl.pallas_call(lambda *refs: block_kernel(s, names, *refs), out_shape=tup...  182 us
    unnamed x20, local copies, waits for them, and re-layouts  4.02 us

profile of v5, /device:TPU:0, one launch (start us, length us, event | category | flops | bytes accessed | tf_op | source)
XLA Modules:
  0.0 195.4 jit_solution(8984129475201161960)
XLA Ops:
  1.3 2.8 %copy.19 = bf16[16,64,512]{2,1,0:T(8,128)(2,1)} copy(bf16[16,64,512]{2,0,1:T(8,128)(2,1)} %bitcast.26) | data formatting | bytes 2097152 | tf_op jit(solution)/shard_map/transpose | solution.py:1121
  4.1 182.2 %block.1 = (bf16[6,50,512]{2,1,0:T(8,128)(2,1)}, f32[6,50,512]{2,1,0:T(8,128)}, f32[3,64,128]{2,1,0:T(8,128)}, f32[64,128]{1,0:T(8,128)}, f32[16,64]{1,0:T(8,128...) custom-call(bf16[6,50,512]{2,1,0:T(8,128)(2,1)} %refs_0_.1, ...), custom_call_target="tpu_custom_call" | custom-call | tf_op jit(solution)/shard_map/block/pallas_call | solution.py:1214
  186.3 1.8 copy.22
  188.1 0.0 copy-start
  188.1 1.6 convert_element_type.12
  189.7 0.0 copy-done
  189.7 0.0 copy-start.2
  189.7 0.0 copy-start.1
  189.7 0.0 copy-start.3
  189.7 0.0 copy-start.4
  189.7 0.0 copy-start.5
  189.7 1.7 convert_bitcast_fusion
  191.4 0.0 copy-done.2
  191.4 0.7 copy.30
  192.1 0.0 copy-done.1
  192.1 0.8 copy.31
  193.0 0.0 copy-done.6
  193.0 0.6 copy.32
  193.6 0.0 copy-done.3
  193.6 0.6 copy.33
  194.2 0.0 copy-done.4
  194.2 0.6 copy.34
  194.8 0.0 copy-done.5
  194.8 0.6 copy.35
  (1 shorter events, 0.0 us)
Async XLA Ops:
  188.1 1.6 copy-start
  189.7 1.7 copy-start.2
  189.7 2.4 %copy-start.1 = (f32[6,50,512]{2,1,0:T(8,128)S(1)}, f32[6,50,512]{2,1,0:T(8,128)}, u32[]{:S(2)}) copy-start(f32[6,50,512]{2,1,0:T(8,128)} %get-tuple-element.33) | copy-start | bytes 1843204
  189.7 3.3 %copy-start.6 = (f32[2,64]{1,0:T(2,128)S(1)}, f32[2,64]{1,0:T(2,128)}, u32[]{:S(2)}) copy-start(f32[2,64]{1,0:T(2,128)} %get-tuple-element.18) | copy-start | bytes 1540
  189.7 3.9 %copy-start.3 = (f32[3,64,128]{2,1,0:T(8,128)S(1)}, f32[3,64,128]{2,1,0:T(8,128)}, u32[]{:S(2)}) copy-start(f32[3,64,128]{2,1,0:T(8,128)} %get-tuple-element.19) | copy-start | bytes 294916
  189.7 4.5 %copy-start.4 = (f32[64,128]{1,0:T(8,128)S(1)}, f32[64,128]{1,0:T(8,128)}, u32[]{:S(2)}) copy-start(f32[64,128]{1,0:T(8,128)} %get-tuple-element.20) | copy-start | bytes 98308
  189.7 5.1 %copy-start.5 = (f32[16,64]{1,0:T(8,128)S(1)}, f32[16,64]{1,0:T(8,128)}, u32[]{:S(2)}) copy-start(f32[16,64]{1,0:T(8,128)} %get-tuple-element.21) | copy-start | bytes 12292

commit v6 on v5

--- a/solution.py
+++ b/solution.py
@@ -282,7 +282,7 @@
 MESH = pl.DeviceIdType.MESH
 BF = jnp.bfloat16
 F32 = jnp.float32
-VMEM_BYTES = 62 << 20
+VMEM_BYTES = 63 << 20
 
 
 class Sizes(NamedTuple):
@@ -561,6 +561,7 @@
             r.tmp[at, :] = images[i].astype(F32)
         out[...] = r.tmp[...].astype(BF)
 
+    fetch = go.here(r.win, r.gwi)
     keep_wo = go.here(r.wo, r.wo_z.at[t])
     pack_own = r.pack.at[y, x, c]
     cols = 3 * s.shard
@@ -583,7 +584,10 @@
         from_y = [go.to(half, to, here.ny), go.to(rest, to, here.ny_other)]
         return from_x, from_y, go.to(rest, to, here.sib), go.here(half, to)
 
-    in_x, in_y, in_sib, keep_in = spread(r.win, r.win_all)
+    fetch.wait()
+    shards = r.xin.at[:, :, pl.ds(0, s.shard)]
+    shards[...] = jnp.swapaxes(r.gwi[...], 0, 1).reshape(2, s.half, s.shard, s.ff)
+    in_x, in_y, in_sib, keep_in = spread(shards, r.win_all)
 
     chosen = jnp.where(r.slots[...] >= 0, r.ids[...] * CAP + r.slots[...], -1)
     by_block = []
@@ -713,9 +717,10 @@
     expd = jnp.exp(logits - jnp.max(logits, 0, keepdims=True))
     r.prob[...] = jnp.zeros((s.experts, s.lanes), F32)
     r.prob[:, : s.rows] = expd / jnp.sum(expd, 0, keepdims=True)
-    r.prob_all[c, t] = r.prob[...]
-    pr_sib = go.to(r.prob, r.prob_all.at[c, t], here.sib)
-    pr_copies = [go.to(r.prob, r.prob_all.at[c, t], (dp, here.ring_t(k))) for k in range(1, nt)]
+    pr_own = r.prob_all.at[c, t]
+    pr_own[...] = r.prob[...].astype(BF)
+    pr_sib = go.to(pr_own, pr_own, here.sib)
+    pr_copies = [go.to(pr_own, pr_own, (dp, here.ring_t(k))) for k in range(1, nt)]
 
     dz_blocks.wait_pair()
     dz_blocks.wait_cross()
@@ -726,16 +731,18 @@
 
     slot_ids = lax.broadcasted_iota(jnp.int32, (CAP, tokens), 0).astype(F32)
 
-    def dispatch(q, j, rows, out):
+    def hot_rows(h, q, j):
         for i in range(few):
-            hits = r.slot[q, pl.ds(few * j + i, 1), :] == slot_ids
+            hits = r.sloth[h, q, pl.ds(few * j + i, 1), :] == slot_ids[:, :half_rows]
             r.hot[i] = jnp.where(hits, 1.0, 0.0).astype(BF)
-        found = dot(r.hot[...].reshape(few * CAP, tokens), rows)
-        out[...] = found.astype(BF).reshape(out.shape)
+        return r.hot[...].reshape(few * CAP, half_rows)
 
     def dispatch_z(j, carry):
         for q in range(2):
-            dispatch(q, j, r.ge[q, :tokens], r.zin.at[q, pl.ds(few * j, few)])
+            found = jnp.zeros((few * CAP, s.width), F32)
+            for h in range(2):
+                found = found + dot(hot_rows(h, q, j), r.ge[q, pl.ds(h * half_rows, half_rows)])
+            r.zin[q, pl.ds(few * j, few)] = found.astype(BF).reshape(few, CAP, s.width)
         return carry
 
     lax.fori_loop(0, s.half // few, dispatch_z, 0)
@@ -749,34 +756,34 @@
         slot = r.prob_all.at[c, here.from_t(k)]
         on_n2.append(go.to(slot, slot, here.sib))
 
-    def dispatch_x(h, first):
+    def dispatch_x(h, first, only=None):
         def step(j, carry):
             for q in range(2):
-                for i in range(few):
-                    hits = r.sloth[h, q, pl.ds(few * j + i, 1), :] == slot_ids[:, :half_rows]
-                    r.hot[i, :, :half_rows] = jnp.where(hits, 1.0, 0.0).astype(BF)
                 rows = r.n2_all[q, pl.ds(2 * h, 2)].reshape(half_rows, s.width)
-                found = dot(r.hot[:, :, :half_rows].reshape(few * CAP, half_rows), rows)
+                found = dot(hot_rows(h, q, j), rows)
                 found = found.reshape(few, CAP, s.width)
                 out = r.xin.at[q, pl.ds(few * j, few)]
                 out[...] = (found if first else found + out[...].astype(F32)).astype(BF)
             return carry
 
-        lax.fori_loop(0, s.half // few, step, 0)
-
+        if only is None:
+            lax.fori_loop(0, s.half // few, step, 0)
+        else:
+            step(only, 0)
+
+    keep_in.wait()
+    go.sent_now([*in_x, *in_y, in_sib])
     n2_sib.wait_recv()
     on_n2[1].wait_recv()
     dispatch_x(t // 2, True)
     n2_blocks.wait_cross()
     on_n2.append(n2_blocks.share(here.cross))
-    keep_in.wait()
     keep_out.wait()
     for copy in [pr_sib, in_sib, out_sib, *in_on[0], *in_on[1], on_n2[0]] + on_n2[2:]:
         copy.wait_recv()
-    mine = pl.ds(pl.multiple_of(c * s.half, s.half), s.half)
     for q in range(2):
-        r.pr[q] = jnp.concatenate([r.prob_all[q, k, mine][:, : s.rows] for k in range(nt)], 1)
-    dispatch_x(1 - t // 2, False)
+        probs = jnp.concatenate([r.prob_all[q, k].astype(F32)[:, : s.rows] for k in range(nt)], 1)
+        r.pr[q] = jnp.where(c == 0, probs[: s.half], probs[s.half :])
     for copy in out_on[0]:
         copy.wait_recv()
     go.sent_now([*in_on[0], *in_on[1], *out_on[0], dz_sib, *dz_blocks.passed, *on_dz])
@@ -797,39 +804,52 @@
     def ge_copy(e):
         return r.ge.at[1 - c, slots_of(e)], r.gev.at[slots_of(e)], here.sib
 
-    def expert(e):
-        x_in = r.xin[:, e].reshape(2 * CAP, s.width)
-        w_in = r.win_all[e].reshape(s.width, s.ff)
-        w_out = r.wout_all[e].reshape(s.width, s.ff)
-        hidden = dot(x_in, w_in)
-        bell = jnp.exp(-0.5 * hidden * hidden)
-        u = 1.0 / (1.0 + (0.3275911 / math.sqrt(2.0)) * jnp.abs(hidden))
-        poly = u * (0.254829592 + u * (-0.284496736 + u * (1.421413741 + u * (-1.453152027 + u * 1.061405429))))
-        tail = 0.5 * poly * bell
-        phi = jnp.where(hidden >= 0, 1.0 - tail, tail)
-        active = (hidden * phi).astype(BF)
-        slope = phi + hidden * bell * (1.0 / math.sqrt(2.0 * math.pi))
-        out = dot_nt(active, w_out).astype(BF).astype(F32)
-        for q in range(2):
-            hits = r.slot[q, pl.ds(e, 1), :] == slot_ids
-            gate = jnp.sum(jnp.where(hits, r.pr[q, pl.ds(e, 1), :], 0.0), 1, keepdims=True)
-            part = out[q * CAP : (q + 1) * CAP]
-            wide = r.zin[q, e].astype(F32)
-            dgate = jnp.sum(wide * part, 1, keepdims=True)
-            r.dpr[q, pl.ds(e, 1), :] = jnp.sum(jnp.where(hits, dgate, 0.0), 0, keepdims=True)
-            r.zin[q, e] = (gate * wide).astype(BF)
-            r.ge[q, slots_of(e)] = (gate * part).astype(BF)
-        grad = r.zin[:, e].reshape(2 * CAP, s.width)
-        dhidden = (dot(grad, w_out) * slope).astype(BF)
-        r.wout_all[e] = dot_tn(grad, active).astype(BF).reshape(r.wout_all.shape[1:])
-        grad_in = dot_tn(x_in, dhidden).astype(BF)
-        r.xin[:, e] = dot_nt(dhidden, w_in).astype(BF).reshape(2, CAP, s.width)
-        r.win_all[e] = grad_in.reshape(r.win_all.shape[1:])
+    def experts_at(first):
+        es = [first + i for i in range(few)]
+        x_in = [r.xin[:, e].reshape(2 * CAP, s.width) for e in es]
+        w_in = [r.win_all[e].reshape(s.width, s.ff) for e in es]
+        w_out = [r.wout_all[e].reshape(s.width, s.ff) for e in es]
+        hidden = [dot(a, b) for a, b in zip(x_in, w_in)]
+        active, slope = [], []
+        for value in hidden:
+            bell = jnp.exp(-0.5 * value * value)
+            u = 1.0 / (1.0 + (0.3275911 / math.sqrt(2.0)) * jnp.abs(value))
+            poly = u * (0.254829592 + u * (-0.284496736 + u * (1.421413741 + u * (-1.453152027 + u * 1.061405429))))
+            tail = 0.5 * poly * bell
+            phi = jnp.where(value >= 0, 1.0 - tail, tail)
+            active.append((value * phi).astype(BF))
+            slope.append(phi + value * bell * (1.0 / math.sqrt(2.0 * math.pi)))
+        gates, wides = [], []
+        for e in es:
+            for q in range(2):
+                hits = r.slot[q, pl.ds(e, 1), :] == slot_ids
+                gate = jnp.sum(jnp.where(hits, r.pr[q, pl.ds(e, 1), :], 0.0), 1, keepdims=True)
+                gates.append(gate)
+                wides.append(r.zin[q, e].astype(F32))
+                r.zin[q, e] = (gate * wides[-1]).astype(BF)
+        grad = [r.zin[:, e].reshape(2 * CAP, s.width) for e in es]
+        dactive = [dot(a, b) for a, b in zip(grad, w_out)]
+        out = [dot_nt(a, b).astype(BF).astype(F32) for a, b in zip(active, w_out)]
+        dhidden = [(a * b).astype(BF) for a, b in zip(dactive, slope)]
+        grad_out = [dot_tn(a, b).astype(BF) for a, b in zip(grad, active)]
+        for i, e in enumerate(es):
+            for q in range(2):
+                part = out[i][q * CAP : (q + 1) * CAP]
+                dgate = jnp.sum(wides[2 * i + q] * part, 1, keepdims=True)
+                hits = r.slot[q, pl.ds(e, 1), :] == slot_ids
+                r.dpr[q, pl.ds(e, 1), :] = jnp.sum(jnp.where(hits, dgate, 0.0), 0, keepdims=True)
+                r.ge[q, slots_of(e)] = (gates[2 * i + q] * part).astype(BF)
+        dx = [dot_nt(a, b).astype(BF) for a, b in zip(dhidden, w_in)]
+        grad_in = [dot_tn(a, b).astype(BF) for a, b in zip(x_in, dhidden)]
+        for i, e in enumerate(es):
+            r.wout_all[e] = grad_out[i].reshape(r.wout_all.shape[1:])
+            r.xin[:, e] = dx[i].reshape(2, CAP, s.width)
+            r.win_all[e] = grad_in[i].reshape(r.win_all.shape[1:])
 
     def expert_few(k, carry):
         j = lax.rem(k, 2) * (per // few) + k // 2
-        for i in range(few):
-            expert(few * j + i)
+        dispatch_x(1 - t // 2, False, j)
+        experts_at(few * j)
         for i in range(few):
             e = few * j + i
             for k, copy in ((k_out, grad_out_copy), (k_in, grad_in_copy), (k_dx, dx_copy), (k_ge, ge_copy)):
@@ -877,6 +897,7 @@
     dpr_copies = [go.to(r.dprb.at[here.ring_t(k)], r.dprz.at[k - 1], (dp, here.ring_t(k))) for k in range(1, nt)]
     dn2_sum.across(combine(dxv, 1 - c, here.far, combine(dx_own, c, here.far, zero_rows)))
     r.comb[0] = combine(dxv, 1 - c, t, combine(dx_own, c, t, zero_rows))
+    go.sent_now(dx_copies)
 
     for copy in ge_copies:
         copy.wait_recv()
@@ -1042,7 +1063,7 @@
     mine = pl.ds(pl.multiple_of(c * s.shard, s.shard), s.shard)
     other = pl.ds(pl.multiple_of((1 - c) * s.shard, s.shard), s.shard)
     fin_copies, kept = [], []
-    parts = ((r.win_all, r.ra, y, r.fa, fa_copies, r.gwi), (r.wout_all, r.rb, x, r.fb, fb_copies, r.gwo))
+    parts = ((r.win_all, r.ra, y, r.fa, fa_copies, shards), (r.wout_all, r.rb, x, r.fb, fb_copies, r.gwo))
     for own, first, place, second, copies, gw in parts:
         for j in range(2):
             copies[j].wait_recv()
@@ -1065,6 +1086,11 @@
             piece = pl.ds(j * per, per)
             fin_copies.append(go.to(own.at[piece, y, x, other], gw.at[c, piece], here.sib))
             kept.append(go.here(own.at[piece, y, x, mine], gw.at[c, piece]))
+    for copy in fin_copies[:2]:
+        copy.wait_recv()
+    for copy in kept[:2]:
+        copy.wait()
+    r.gwi[...] = jnp.swapaxes(shards[...].reshape(s.experts, s.shard, s.ff), 0, 1)
     dn1 = dn1_sum.total(r.comb[3])
     dx_ln, _ = norm_back(r.x[...].astype(F32), gain_one, dn1)
     r.tmp[...] = r.comb[0] + dx_ln
@@ -1082,9 +1108,9 @@
     r.gr[...] = total[: s.experts, : s.shard]
     r.gg[...] = total[s.experts : s.experts + 2, : s.shard]
 
-    for copy in fin_copies:
-        copy.wait_recv()
-    for copy in kept:
+    for copy in fin_copies[2:]:
+        copy.wait_recv()
+    for copy in kept[2:]:
         copy.wait()
     go.finish()
 
@@ -1118,7 +1144,6 @@
     used = images * quarter
     rows = up(used, 16)
     s = Sizes(n_dp, n_t, images, quarter, rows, up(length, 16), width, shard, heads, experts, ff, up(rows, 128))
-    win_t = w_in.transpose(1, 0, 2).reshape(2, s.half, shard, ff)
     wout_t = w_out.transpose(1, 2, 0).reshape(2, s.half, shard, ff)
     two_y, two_x = n_dp // 4, 2
     gsm_rows = up(experts + 2, 8)
@@ -1133,7 +1158,7 @@
         ids=expert_ids.transpose(0, 2, 1),
         slots=slot_index.transpose(0, 2, 1),
         alive=pictures_alive_per_shard,
-        win=win_t,
+        win=w_in,
         wout=wout_t,
     )
     in_specs = {"win": ASPEC, "wout": ASPEC, "alive": pl.BlockSpec(memory_space=pltpu.SMEM)}
@@ -1144,7 +1169,7 @@
         go=shape((shard, heads), F32),
         gr=shape((experts, shard), F32),
         gg=shape((2, shard), F32),
-        gwi=shape((2, s.half, shard, ff), BF),
+        gwi=shape((shard, experts, ff), BF),
         gwo=shape((2, s.half, shard, ff), BF),
     )
     wide = (two_y, two_x, 2 * shard, ff)
@@ -1153,7 +1178,7 @@
         win_all=((s.half, *wide), BF),
         wout_all=((s.half, *wide), BF),
         n2_all=((2, n_t, rows, width), BF),
-        prob_all=((2, n_t, experts, s.lanes), F32),
+        prob_all=((2, n_t, experts, s.lanes), BF),
         tgt_all=((2, 8, tokens), jnp.int32),
         tcol=((n_t, rows, 2), jnp.int32),
         y=((rows, width), F32),
@@ -1181,7 +1206,7 @@
         dprf=((n_t, 2, s.half, s.lanes), F32),
         dprb=((n_t, experts, s.lanes), BF),
         dprz=((n_t - 1, experts, s.lanes), BF),
-        hot=((2, CAP, tokens), BF),
+        hot=((2, CAP, tokens // 2), BF),
         xin=((2, s.half, CAP, width), BF),
         slot=((2, s.half, tokens), F32),
         sloth=((2, 2, s.half, tokens // 2), F32),
@@ -1215,7 +1240,7 @@
         lambda *refs: block_kernel(s, names, *refs),
         out_shape=tuple(outputs.values()),
         in_specs=[in_specs.get(name, VSPEC) for name in inputs],
-        out_specs=[ASPEC if name in ("gwi", "gwo") else VSPEC for name in outputs],
+        out_specs=[ASPEC if name == "gwo" else VSPEC for name in outputs],
         scratch_shapes=[pltpu.VMEM(dims, kind) for dims, kind in scratch.values()]
         + [pltpu.SemaphoreType.DMA((links,)), pltpu.SemaphoreType.DMA((links,)), pltpu.SemaphoreType.DMA((10,))],
         compiler_params=pltpu.CompilerParams(collective_id=1, has_side_effects=True, vmem_limit_bytes=VMEM_BYTES),
@@ -1229,7 +1254,7 @@
         gq.transpose(1, 0, 2),
         grad_o.T,
         gr.T,
-        lax.optimization_barrier(gwi.reshape(experts, shard, ff).transpose(1, 0, 2)).astype(F32),
+        gwi.astype(F32),
         gwo.reshape(experts, shard, ff).transpose(2, 0, 1).astype(F32),
     )
 

time: 196 us -> 191 us (0.974)
  local copies, waits for them, and re-layouts: 8.6 us -> 4.02 us
  Pallas kernels: 182 us -> 180 us
    transpose x1 -> x0, local copies, waits for them, and re-layouts: 2.77 us -> none  [linked_body(): win_t = w_in.transpose(1, 0, 2).reshape(2, s.half, shard, ff)]
where the time goes in v6:
time: 191 us; the launch traced here: 190 us
  Pallas kernels  180 us (94%)
  other arithmetic  4.6 us (2%)
  local copies, waits for them, and re-layouts  4.02 us (2%)
    pallas_call x1, Pallas kernels, linked_body(): pl.pallas_call(lambda *refs: block_kernel(s, names, *refs), out_shape=tup...  180 us
    unnamed x20, local copies, waits for them, and re-layouts  4.02 us

profile of v6, /device:TPU:0, one launch (start us, length us, event | category | flops | bytes accessed | tf_op | source)
XLA Modules:
  0.0 190.4 jit_solution(14911443659960488868)
XLA Ops:
  1.3 180.4 %block.1 = (bf16[6,50,512]{2,1,0:T(8,128)(2,1)}, f32[6,50,512]{2,1,0:T(8,128)}, f32[3,64,128]{2,1,0:T(8,128)}, f32[64,128]{1,0:T(8,128)}, f32[16,64]{1,0:T(8,128...) custom-call(bf16[6,50,512]{2,1,0:T(8,128)(2,1)} %refs_0_.1, ...), custom_call_target="tpu_custom_call" | custom-call | tf_op jit(solution)/shard_map/block/pallas_call | solution.py:1239
  181.7 0.0 copy-start
  181.7 2.9 %convert_element_type.12 = f32[64,16,512]{2,1,0:T(8,128)} convert(bf16[64,16,512]{2,1,0:T(8,128)(2,1)} %get-tuple-element.22) | non-fusion elementwise | flops 524288 | bytes 3145728 | tf_op jit(solution)/shard_map/convert_element_type | solution.py:1257
  184.6 0.0 copy-done
  184.6 0.0 copy-start.2
  184.6 0.0 copy-start.1
  184.7 0.0 copy-start.6
  184.7 0.0 copy-start.3
  184.7 0.0 copy-start.4
  184.7 0.0 copy-start.5
  184.7 1.7 convert_bitcast_fusion
  186.4 0.0 copy-done.2
  186.4 0.7 copy.26
  187.1 0.0 copy-done.1
  187.1 0.8 copy.27
  187.9 0.0 copy-done.6
  187.9 0.6 copy.28
  188.5 0.0 copy-done.3
  188.5 0.6 copy.29
  189.1 0.0 copy-done.4
  189.2 0.6 copy.30
  189.8 0.0 copy-done.5
  189.8 0.6 copy.31
Async XLA Ops:
  181.7 2.9 %copy-start = (bf16[2,8,64,512]{3,2,1,0:T(8,128)(2,1)S(1)}, bf16[2,8,64,512]{3,2,1,0:T(8,128)(2,1)}, u32[]{:S(2)}) copy-start(bf16[2,8,64,512]{3,2,1,0:T(8,128)(2,1)} %get-tuple-element.23) | copy-start | bytes 3145732
  184.6 1.7 copy-start.2
  184.6 2.4 %copy-start.1 = (f32[6,50,512]{2,1,0:T(8,128)S(1)}, f32[6,50,512]{2,1,0:T(8,128)}, u32[]{:S(2)}) copy-start(f32[6,50,512]{2,1,0:T(8,128)} %get-tuple-element.33) | copy-start | bytes 1843204
  184.7 3.3 %copy-start.6 = (f32[2,64]{1,0:T(2,128)S(1)}, f32[2,64]{1,0:T(2,128)}, u32[]{:S(2)}) copy-start(f32[2,64]{1,0:T(2,128)} %get-tuple-element.18) | copy-start | bytes 1540
  184.7 3.9 %copy-start.3 = (f32[3,64,128]{2,1,0:T(8,128)S(1)}, f32[3,64,128]{2,1,0:T(8,128)}, u32[]{:S(2)}) copy-start(f32[3,64,128]{2,1,0:T(8,128)} %get-tuple-element.19) | copy-start | bytes 294916
  184.7 4.5 %copy-start.4 = (f32[64,128]{1,0:T(8,128)S(1)}, f32[64,128]{1,0:T(8,128)}, u32[]{:S(2)}) copy-start(f32[64,128]{1,0:T(8,128)} %get-tuple-element.20) | copy-start | bytes 98308
  184.7 5.1 %copy-start.5 = (f32[16,64]{1,0:T(8,128)S(1)}, f32[16,64]{1,0:T(8,128)}, u32[]{:S(2)}) copy-start(f32[16,64]{1,0:T(8,128)} %get-tuple-element.21) | copy-start | bytes 12292
